TPU v7x, 32 devices: a whole 2x2x4 slice. The times are simulated.
32 devices in a mesh: dp: 8 (over z, x), tensor: 4 (over y, core).
Axes of the slice: x: 2, y: 2, z: 4, core: 2. Of those that a mesh axis runs over, the one named last changes fastest.
Arguments:
- tokens: bfloat16 [16384, 768], P('dp'), may hold values from -6 to 6
- attn_gain: float32 [768], replicated, may hold values from 0.5 to 1.5
- qkv_weight: bfloat16 [3, 768, 768], P(None, None, 'tensor'), may hold values from -0.21875 to 0.21875
- proj_weight: bfloat16 [768, 768], P(None, 'tensor'), may hold values from -3.5 to 3.5
- bias_table: float32 [12, 32], P('tensor'), may hold values from -4 to 4
- buckets: int32 [2047], replicated, may hold values from 0 to 31
- ffn_gain: float32 [768], replicated, may hold values from 0.5 to 1.5
- router_weight: bfloat16 [768, 4], replicated, may hold values from -0.15625 to 0.15625
- routes: int32 [16384, 1], P('dp'), may hold values from 0 to 3; in each aligned block of 2048 rows (0 to 2047, 2048 to 4095, ...) at most 1024 rows name the same one
- up_weight: bfloat16 [4, 768, 3072], P(None, None, 'tensor'), may hold values from -0.21875 to 0.21875
- down_weight: bfloat16 [4, 768, 3072], P(None, None, 'tensor'), may hold values from -0.4375 to 0.4375
- cotangent: bfloat16 [16384, 768], P(('dp', 'tensor')), may hold values from -6 to 6
Outputs:
- layer_out: bfloat16 [16384, 768], P(('dp', 'tensor'))
- tokens_grad: float32 [16384, 768], P(('dp', 'tensor'))
- attn_gain_grad: float32 [768], replicated
- qkv_grad: float32 [3, 768, 768], P(None, 'dp', 'tensor')
- proj_grad: float32 [768, 768], P('dp', 'tensor')
- table_grad: float32 [12, 32], replicated
- ffn_gain_grad: float32 [768], replicated
- router_grad: float32 [768, 4], replicated
- up_grad: float32 [4, 768, 3072], P(None, 'dp', 'tensor')
- down_grad: float32 [4, 768, 3072], P(None, 'dp', 'tensor')
Inputs may be any that keep to these rules, and one draw needn't show every extreme that they name: `routes`: in each aligned block of 2048 rows (the rows of one index of dp) no expert is named by more than 1024 rows; in every draw some block has an expert named by exactly 1024 rows.
All inputs are finite; a program needn't handle non-finite values.
Results may differ from a plain program's by a relative error of at most 0.015.
The roundings to bfloat16 on the way count: a program that leaves them out, or rounds other values in their place, can miss the bound.
Values may be sent and summed in bfloat16 or wider, within the bound.
No kernel may reach another device: no remote copies, remote signals or barrier semaphores. Data moves between devices by JAX's collectives and lax.ppermute only.
A program may use at most 192 MiB of HBM per device.

v0:
```python
import functools
import jax, jax.numpy as jnp
from jax import lax
from jax.experimental import pallas as pl
from jax.experimental.pallas import tpu as pltpu
from jax.sharding import PartitionSpec as P

QB = 256
KB = 128


def mm(a, b, dims):
    return lax.dot_general(a, b, (dims, ((), ())), preferred_element_type=jnp.float32)


def score_block(keys, queries, skew, first_query, seq_len):
    scores = mm(keys, queries, ((1,), (0,)))
    bias = [
        skew[:, pl.ds(pl.multiple_of(first_query - first_key + seq_len - KB, KB), QB)]
        for first_key in range(0, seq_len, KB)
    ]
    return scores + jnp.concatenate(bias, axis=0)


def forward_kernel(seq_ref, qkv_ref, offset_ref, mixed_ref, lse_ref, skew):
    seq_len = qkv_ref.shape[2]
    scale = qkv_ref.shape[1] ** -0.5
    skew[...] = pltpu.roll(
        jnp.broadcast_to(offset_ref[0], (KB, 2 * seq_len)), 0, 1, stride=1, stride_axis=0
    )
    keys = qkv_ref[1].T
    values = qkv_ref[2]

    def block(index, carry):
        first = pl.multiple_of(index * QB, QB)
        queries = qkv_ref[0, :, pl.ds(first, QB)] * jnp.bfloat16(scale)
        scores = score_block(keys, queries, skew, first, seq_len)
        largest = jnp.max(scores, axis=0, keepdims=True)
        expos = jnp.exp(scores - largest)
        total = jnp.sum(expos, axis=0, keepdims=True)
        weights = (expos * (1.0 / total)).astype(jnp.bfloat16)
        mixed_ref[:, pl.ds(first, QB)] = mm(values, weights, ((1,), (0,))).astype(jnp.bfloat16)
        lse_ref[0, :, pl.ds(first, QB)] = largest + jnp.log(total)
        return carry

    lax.fori_loop(0, seq_len // QB, block, 0, unroll=True)


def forward_attention(seq, qkv, offsets, seq_len):
    _, width, rows = qkv.shape
    heads = offsets.shape[0]
    size = width // heads
    return pl.pallas_call(
        forward_kernel,
        grid_spec=pltpu.PrefetchScalarGridSpec(
            num_scalar_prefetch=1,
            grid=(heads,),
            in_specs=[
                pl.BlockSpec((3, size, seq_len), lambda h, s: (0, h, s[0])),
                pl.BlockSpec((1, 1, 2 * seq_len), lambda h, s: (h, 0, 0)),
            ],
            out_specs=[
                pl.BlockSpec((size, seq_len), lambda h, s: (h, 0)),
                pl.BlockSpec((1, 1, seq_len), lambda h, s: (h, 0, 0)),
            ],
            scratch_shapes=[pltpu.VMEM((KB, 2 * seq_len), jnp.float32)],
        ),
        out_shape=[
            jax.ShapeDtypeStruct((width, seq_len), jnp.bfloat16),
            jax.ShapeDtypeStruct((heads, 1, seq_len), jnp.float32),
        ],
        compiler_params=pltpu.CompilerParams(vmem_limit_bytes=48 * 2**20),
        name="attention_forward",
    )(seq, qkv, offsets)


def backward_kernel(
    seq_ref, qkv_ref, grad_ref, lse_ref, offset_ref, out_ref, diag_ref, skew, sums, probs_all, score_all
):
    seq_len = qkv_ref.shape[2]
    scale = qkv_ref.shape[1] ** -0.5
    skew[...] = pltpu.roll(
        jnp.broadcast_to(offset_ref[0], (KB, 2 * seq_len)), 0, 1, stride=1, stride_axis=0
    )
    sums[...] = jnp.zeros_like(sums)
    keys_t = qkv_ref[1]
    keys = keys_t.T
    values = qkv_ref[2].T

    def block(index, carry):
        first = pl.multiple_of(index * QB, QB)
        here = pl.ds(first, QB)
        queries = qkv_ref[0, :, here] * jnp.bfloat16(scale)
        scores = score_block(keys, queries, skew, first, seq_len)
        probs = jnp.exp(scores - lse_ref[0, :, here])
        probs_all[:, here] = probs.astype(jnp.bfloat16)
        prob_grad = mm(values, grad_ref[:, here], ((1,), (0,)))
        centre = jnp.sum(probs * prob_grad, axis=0, keepdims=True)
        score_grad = probs * (prob_grad - centre)
        rounded = score_grad.astype(jnp.bfloat16)
        score_all[:, here] = rounded
        for first_key in range(0, seq_len, KB):
            spot = pl.ds(pl.multiple_of(first - first_key + seq_len - KB, KB), QB)
            sums[:, spot] += score_grad[first_key : first_key + KB]
        out_ref[0, :, here] = (mm(keys_t, rounded, ((1,), (0,))) * scale).astype(jnp.bfloat16)
        return carry

    lax.fori_loop(0, seq_len // QB, block, 0, unroll=True)
    queries = qkv_ref[0] * jnp.bfloat16(scale)
    out_ref[1] = mm(queries, score_all[...], ((1,), (1,))).astype(jnp.bfloat16)
    out_ref[2] = mm(grad_ref[...], probs_all[...], ((1,), (1,))).astype(jnp.bfloat16)
    part = sums[...]
    half = KB // 2
    while half >= 1:
        part = part[:half] + pltpu.roll(part[half:], 2 * seq_len - half, 1)
        half //= 2
    diag_ref[0] = part


def backward_attention(seq, qkv, grads, lse, offsets, seq_len):
    _, width, rows = qkv.shape
    heads = offsets.shape[0]
    size = width // heads
    return pl.pallas_call(
        backward_kernel,
        grid_spec=pltpu.PrefetchScalarGridSpec(
            num_scalar_prefetch=1,
            grid=(heads,),
            in_specs=[
                pl.BlockSpec((3, size, seq_len), lambda h, s: (0, h, s[0])),
                pl.BlockSpec((size, seq_len), lambda h, s: (h, 0)),
                pl.BlockSpec((1, 1, seq_len), lambda h, s: (h, 0, 0)),
                pl.BlockSpec((1, 1, 2 * seq_len), lambda h, s: (h, 0, 0)),
            ],
            out_specs=[
                pl.BlockSpec((3, size, seq_len), lambda h, s: (0, h, 0)),
                pl.BlockSpec((1, 1, 2 * seq_len), lambda h, s: (h, 0, 0)),
            ],
            scratch_shapes=[
                pltpu.VMEM((KB, 2 * seq_len), jnp.float32),
                pltpu.VMEM((KB, 2 * seq_len), jnp.float32),
                pltpu.VMEM((seq_len, seq_len), jnp.bfloat16),
                pltpu.VMEM((seq_len, seq_len), jnp.bfloat16),
            ],
        ),
        out_shape=[
            jax.ShapeDtypeStruct((3, width, seq_len), jnp.bfloat16),
            jax.ShapeDtypeStruct((heads, 1, 2 * seq_len), jnp.float32),
        ],
        compiler_params=pltpu.CompilerParams(vmem_limit_bytes=48 * 2**20),
        name="attention_backward",
    )(seq, qkv, grads, lse, offsets)


CH = 16
TM = 128


def tile_limit(rows, shares, experts):
    chunks = rows // CH + shares * (experts - 1)
    return (chunks + experts * (TM // CH - 1)) // (TM // CH)


def plan_segments(counts):
    starts = jnp.cumsum(counts, axis=1) - counts
    first = starts // CH
    chunks = jnp.where(counts > 0, (starts + counts + CH - 1) // CH - first, 0)
    tiles = (jnp.sum(chunks, axis=0) * CH + TM - 1) // TM
    base = jnp.cumsum(tiles) - tiles
    return jnp.concatenate(
        [first, chunks, starts, starts + counts, tiles[None], base[None]], axis=0
    ).astype(jnp.int32)


def expert_kernel(
    plan_ref, x_ref, c_ref, router_ref, up_ref, down_ref,
    y_ref, back_ref, gate_ref, xs_ref, ms_ref, dys_ref, dus_ref,
    cs, ybuf, bbuf, gbuf, *, shares,
):
    expert = pl.program_id(0)
    share_rows = x_ref.shape[0] // shares
    tiles = plan_ref[4 * shares, expert]
    base = plan_ref[4 * shares + 1, expert] * TM

    @pl.when(expert == 0)
    def _():
        y_ref[...] = jnp.zeros_like(y_ref)
        back_ref[...] = jnp.zeros_like(back_ref)
        gate_ref[...] = jnp.zeros_like(gate_ref)

    filled = 0
    for share in range(shares):
        first = plan_ref[share, expert]
        chunks = plan_ref[shares + share, expert]
        start = plan_ref[2 * shares + share, expert]
        end = plan_ref[3 * shares + share, expert]

        def gather(index, carry, share=share, first=first, start=start, end=end, filled=filled):
            here = (first + index) * CH
            source = pl.ds(pl.multiple_of(here + share * share_rows, CH), CH)
            local = pl.multiple_of((filled + index) * CH, CH)
            row = here + lax.broadcasted_iota(jnp.int32, (CH, 1), 0)
            keep = (row >= start) & (row < end)
            zero = jnp.zeros((), jnp.bfloat16)
            xs_ref[pl.ds(pl.multiple_of(base + local, CH), CH)] = jnp.where(keep, x_ref[source], zero)
            cs[pl.ds(local, CH)] = jnp.where(keep, c_ref[source], zero)
            return carry

        lax.fori_loop(0, chunks, gather, 0)
        filled = filled + chunks

    def clear(index, carry):
        local = pl.multiple_of(index * CH, CH)
        xs_ref[pl.ds(pl.multiple_of(base + local, CH), CH)] = jnp.zeros((CH, xs_ref.shape[1]), jnp.bfloat16)
        cs[pl.ds(local, CH)] = jnp.zeros((CH, cs.shape[1]), jnp.bfloat16)
        return carry

    lax.fori_loop(filled, tiles * (TM // CH), clear, 0)

    def tile(index, carry):
        local = pl.ds(pl.multiple_of(index * TM, TM), TM)
        saved = pl.ds(pl.multiple_of(base + index * TM, TM), TM)
        x = xs_ref[saved]
        c = cs[local]
        logits = mm(x, router_ref[...], ((1,), (0,)))
        lane = lax.broadcasted_iota(jnp.int32, logits.shape, 1)
        logits = jnp.where(lane < EXPERTS, logits, -jnp.inf)
        expos = jnp.exp(logits - jnp.max(logits, axis=1, keepdims=True))
        mine = jnp.sum(jnp.where(lane == expert, expos, 0.0), axis=1, keepdims=True)
        gate = mine / jnp.sum(expos, axis=1, keepdims=True)
        c32 = c.astype(jnp.float32)
        dy = (gate * c32).astype(jnp.bfloat16)
        dys_ref[saved] = dy
        u = mm(x, up_ref[0], ((1,), (0,)))
        root = 0.7978845608028654
        square = u * u
        bent = jnp.tanh(root * (u * (1.0 + 0.044715 * square)))
        half = 0.5 * (1.0 + bent)
        m = (u * half).astype(jnp.bfloat16)
        ms_ref[saved] = m
        slope = half + (0.5 * root) * (u * ((1.0 - bent * bent) * (1.0 + (3 * 0.044715) * square)))
        y = mm(m, down_ref[0], ((1,), (1,)))
        ybuf[local] = y
        gbuf[local] = jnp.broadcast_to(jnp.sum(y * c32, axis=1, keepdims=True), (TM, gbuf.shape[1]))
        dm = mm(dy, down_ref[0], ((1,), (0,)))
        du = (slope * dm).astype(jnp.bfloat16)
        dus_ref[saved] = du
        bbuf[local] = mm(du, up_ref[0], ((1,), (1,)))
        return carry

    lax.fori_loop(0, tiles, tile, 0)

    filled = 0
    for share in range(shares):
        first = plan_ref[share, expert]
        chunks = plan_ref[shares + share, expert]

        def scatter(index, carry, share=share, first=first, filled=filled):
            target = pl.ds(pl.multiple_of((first + index) * CH + share * share_rows, CH), CH)
            local = pl.ds(pl.multiple_of((filled + index) * CH, CH), CH)
            y_ref[target] += ybuf[local]
            back_ref[target] += bbuf[local]
            gate_ref[target] += gbuf[local]
            return carry

        lax.fori_loop(0, chunks, scatter, 0)
        filled = filled + chunks

EXPERTS = 4

def run_experts(plan, x, c, router, up, down, shares):
    rows, width = x.shape
    experts, _, hidden = up.shape
    saved = tile_limit(rows, shares, experts) * TM
    most = -(-rows // TM) * TM
    whole = lambda shape: pl.BlockSpec(shape, lambda e, p: (0, 0))
    brain = jnp.bfloat16
    return pl.pallas_call(
        functools.partial(expert_kernel, shares=shares),
        grid_spec=pltpu.PrefetchScalarGridSpec(
            num_scalar_prefetch=1,
            grid=(experts,),
            in_specs=[
                whole((rows, width)),
                whole((rows, width)),
                whole(router.shape),
                pl.BlockSpec((1, width, hidden), lambda e, p: (e, 0, 0)),
                pl.BlockSpec((1, width, hidden), lambda e, p: (e, 0, 0)),
            ],
            out_specs=[
                whole((rows, width)), whole((rows, width)), whole((rows, 128)),
                whole((saved, width)), whole((saved, hidden)), whole((saved, width)), whole((saved, hidden)),
            ],
            scratch_shapes=[
                pltpu.VMEM((most, width), brain),
                pltpu.VMEM((most, width), jnp.float32),
                pltpu.VMEM((most, width), jnp.float32),
                pltpu.VMEM((most, 128), jnp.float32),
            ],
        ),
        out_shape=[
            jax.ShapeDtypeStruct((rows, width), jnp.float32),
            jax.ShapeDtypeStruct((rows, width), jnp.float32),
            jax.ShapeDtypeStruct((rows, 128), jnp.float32),
            jax.ShapeDtypeStruct((saved, width), brain),
            jax.ShapeDtypeStruct((saved, hidden), brain),
            jax.ShapeDtypeStruct((saved, width), brain),
            jax.ShapeDtypeStruct((saved, hidden), brain),
        ],
        compiler_params=pltpu.CompilerParams(vmem_limit_bytes=56 * 2**20),
        cost_estimate=pl.CostEstimate(flops=8 * rows * width * hidden, bytes_accessed=30 * 2**20, transcendentals=0),
        name="experts",
    )(plan, x, c, router, up, down)


def grads_kernel(*refs, halves, plan_row):
    plans = refs[:halves]
    data = refs[halves : halves + 4 * halves]
    up_out, down_out, up_acc, down_acc = refs[5 * halves :]
    expert = pl.program_id(0)
    up_acc[...] = jnp.zeros_like(up_acc)
    down_acc[...] = jnp.zeros_like(down_acc)
    for half in range(halves):
        x_ref, m_ref, dy_ref, du_ref = data[4 * half : 4 * half + 4]
        tiles = plans[half][plan_row, expert]
        base = plans[half][plan_row + 1, expert] * TM

        def tile(index, carry, x_ref=x_ref, m_ref=m_ref, dy_ref=dy_ref, du_ref=du_ref, base=base):
            here = pl.ds(pl.multiple_of(base + index * TM, TM), TM)
            up_acc[...] += mm(x_ref[here], du_ref[here], ((0,), (0,)))
            down_acc[...] += mm(dy_ref[here], m_ref[here], ((0,), (0,)))
            return carry

        lax.fori_loop(0, tiles, tile, 0)
    up_out[0] = up_acc[...].astype(jnp.bfloat16)
    down_out[0] = down_acc[...].astype(jnp.bfloat16)


def weight_grads(plans, saved, experts, plan_row):
    halves = len(plans)
    flat = [array for group in saved for array in group]
    width, hidden = flat[0].shape[1], flat[1].shape[1]
    block = pl.BlockSpec((1, width, hidden), lambda e, *p: (e, 0, 0))
    shape = jax.ShapeDtypeStruct((experts, width, hidden), jnp.bfloat16)
    return pl.pallas_call(
        functools.partial(grads_kernel, halves=halves, plan_row=plan_row),
        grid_spec=pltpu.PrefetchScalarGridSpec(
            num_scalar_prefetch=halves,
            grid=(experts,),
            in_specs=[pl.BlockSpec(memory_space=pltpu.VMEM)] * len(flat),
            out_specs=[block, block],
            scratch_shapes=[pltpu.VMEM((width, hidden), jnp.float32)] * 2,
        ),
        out_shape=[shape, shape],
        compiler_params=pltpu.CompilerParams(vmem_limit_bytes=56 * 2**20),
        cost_estimate=pl.CostEstimate(flops=8 * 2048 * width * hidden, bytes_accessed=30 * 2**20, transcendentals=0),
        name="expert_weight_grads",
    )(*plans, *flat)


EPS = 1e-06
F32 = jnp.float32
BF16 = jnp.bfloat16


def norm_rows(values, gain_vector):
    return values * lax.rsqrt(jnp.mean(values * values, axis=-1, keepdims=True) + EPS) * gain_vector


def swap(values, axis, bit):
    count = lax.axis_size(axis)
    return lax.ppermute(values, axis, [(i, i ^ bit) for i in range(count)])


def gather_shares(mine):
    far = swap(mine, "tensor", 2)
    near = swap(mine, "tensor", 1)
    return jnp.concatenate([mine, near]), jnp.concatenate([far, swap(far, "tensor", 1)])


def sum_shares(for_me, for_near, for_far, for_both):
    passed = swap(for_both.astype(BF16), "tensor", 1).astype(F32)
    far = swap((for_far + passed).astype(BF16), "tensor", 2).astype(F32)
    near = swap(for_near.astype(BF16), "tensor", 1).astype(F32)
    return for_me + near + far


def scatter_sum(values):
    count = lax.axis_size("dp")
    index = lax.axis_index("dp")
    experts, rows, width = values.shape
    piece = rows // count
    bit = 1
    while bit < count:
        values = values.reshape(experts, count // (2 * bit), 2, piece, width)
        mine = (index // bit) % 2
        keep = lax.dynamic_index_in_dim(values, mine, 2, keepdims=False)
        send = lax.dynamic_index_in_dim(values, 1 - mine, 2, keepdims=False)
        values = keep.astype(F32) + swap(send.astype(BF16), "dp", bit).astype(F32)
        bit *= 2
    return values.reshape(experts, piece, width)


def sum_everywhere(values):
    for axis in ("tensor", "dp"):
        bit = 1
        while bit < lax.axis_size(axis):
            values = values + swap(values, axis, bit)
            bit *= 2
    return values


def on_device(
    tokens,
    attn_gain,
    qkv_weight,
    proj_weight,
    bias_table,
    buckets,
    ffn_gain,
    router_weight,
    routes,
    up_weight,
    down_weight,
    cotangent,
):
    highest = lax.Precision.HIGHEST
    rank = lax.axis_index("tensor")
    core, chip = rank % 2, rank // 2
    tensor_count = lax.axis_size("tensor")
    rows, width = tokens.shape
    share = rows // tensor_count
    half = rows // 2
    seq_len = (buckets.shape[0] + 1) // 2
    heads, bucket_count = bias_table.shape
    experts = up_weight.shape[0]
    own_seq = chip.astype(jnp.int32).reshape(1)
    other_seq = 1 - own_seq

    flipped = buckets[::-1]
    cut = KB - 1
    turned = jnp.concatenate([flipped[cut:], jnp.full((1,), -1, flipped.dtype), flipped[:cut]])
    bucket_hot = (turned[:, None] == jnp.arange(bucket_count)[None, :]).astype(F32)
    offsets = jnp.dot(bias_table, bucket_hot.T, precision=highest)[:, None, :]

    all_routes = routes[:, 0].reshape(tensor_count, share)
    counts = jnp.sum((all_routes[:, :, None] == jnp.arange(experts)).astype(jnp.int32), axis=1)
    order = rank ^ jnp.arange(tensor_count)
    same = order[:, None] == jnp.arange(tensor_count)[None, :]
    counts = jnp.sum(jnp.where(same[:, :, None], counts[None], 0), axis=1)
    own_plan = plan_segments(counts[:2])
    other_plan = plan_segments(counts[2:])
    my_routes = lax.dynamic_slice_in_dim(routes[:, 0], rank * share, share, 0)
    my_hot = (my_routes[:, None] == jnp.arange(experts)[None, :]).astype(F32)
    earlier = (jnp.arange(share)[:, None] > jnp.arange(share)[None, :]).astype(BF16)
    ahead = jnp.dot(earlier, my_hot.astype(BF16), preferred_element_type=F32)
    starts = (jnp.cumsum(counts[0]) - counts[0]).astype(F32)
    position = jnp.sum(my_hot * (ahead + starts[None, :]), axis=1).astype(jnp.int32)
    place = jnp.arange(share)[:, None] == position[None, :]
    place_matrix = place.astype(BF16)

    def sort_rows(values):
        return jnp.dot(place_matrix, values, preferred_element_type=F32).astype(BF16)

    def unsort_rows(values):
        dims = (((0,), (0,)), ((), ()))
        high = lax.reduce_precision(values, 8, 7)
        low = (values - high).astype(BF16)
        return lax.dot_general(
            place_matrix, high.astype(BF16), dims, preferred_element_type=F32
        ) + lax.dot_general(place_matrix, low, dims, preferred_element_type=F32)

    own_grad_out, other_grad_out = gather_shares(sort_rows(cotangent))

    normed_one = norm_rows(tokens.astype(F32), attn_gain).astype(BF16)
    input_share = lax.dynamic_slice_in_dim(tokens, rank * share, share, 0).astype(F32)
    qkv = jnp.einsum("cdf,td->cft", qkv_weight, normed_one, preferred_element_type=F32).astype(BF16)

    def columns(values, core_index):
        return lax.dynamic_slice_in_dim(values, core_index * share, share, values.ndim - 1)

    def project(mixed, core_index):
        return jnp.einsum(
            "ft,df->td", columns(mixed, core_index), proj_weight, preferred_element_type=F32
        )

    mixed_other, lse_other = forward_attention(other_seq, qkv, offsets, seq_len)
    mixed_own, lse_own = forward_attention(own_seq, qkv, offsets, seq_len)
    attn_share = sum_shares(
        project(mixed_own, core),
        project(mixed_own, 1 - core),
        project(mixed_other, core),
        project(mixed_other, 1 - core),
    )
    hidden_share = input_share + attn_share
    normed_two = norm_rows(hidden_share, ffn_gain).astype(BF16)

    own_rows, other_rows = gather_shares(sort_rows(normed_two))
    padded_router = jnp.pad(router_weight, ((0, 0), (0, 128 - experts)))
    own_out, own_back, own_gate, *own_saved = run_experts(
        own_plan, own_rows, own_grad_out, padded_router, up_weight, down_weight, 2
    )
    other_out, other_back, other_gate, *other_saved = run_experts(
        other_plan, other_rows, other_grad_out, padded_router, up_weight, down_weight, 2
    )
    back_share = unsort_rows(
        sum_shares(own_back[:share], own_back[share:], other_back[:share], other_back[share:])
    )
    passed = swap(other_gate[share:, 0], "tensor", 1)
    gate_sorted = (
        own_gate[:share, 0]
        + swap(own_gate[share:, 0], "tensor", 1)
        + swap(other_gate[:share, 0] + passed, "tensor", 2)
    )
    gate_grad = jnp.sum(jnp.where(place, gate_sorted[:, None], 0.0), axis=0)
    up_grad, down_grad = weight_grads(
        [own_plan, other_plan], [own_saved, other_saved], experts, 8
    )

    logits = jnp.dot(normed_two, router_weight, preferred_element_type=F32)
    router_probs = jax.nn.softmax(logits, axis=-1)
    gate_prob = jnp.sum(router_probs * my_hot, axis=-1)
    grad_out = cotangent.astype(F32)
    logit_grad = ((gate_grad * gate_prob)[:, None] * (my_hot - router_probs)).astype(BF16)
    router_grad = jnp.einsum("td,te->de", normed_two, logit_grad, preferred_element_type=F32)
    normed_grad = back_share + jnp.einsum(
        "te,de->td", logit_grad, router_weight, preferred_element_type=F32
    )
    hidden_part, ffn_gain_grad = jax.vjp(norm_rows, hidden_share, ffn_gain)[1](normed_grad)
    hidden_grad = grad_out + hidden_part

    attn_grad = hidden_grad.astype(BF16)
    far_grad = swap(attn_grad, "tensor", 2)
    near_grad = swap(attn_grad, "tensor", 1)
    both_grad = swap(far_grad, "tensor", 1)

    def in_order(mine, partner):
        return jnp.concatenate(
            [jnp.where(core == 0, mine, partner), jnp.where(core == 0, partner, mine)]
        )

    own_attn_grad = in_order(attn_grad, near_grad)
    other_attn_grad = in_order(far_grad, both_grad)

    def mixed_grad(rows_grad):
        return jnp.einsum("df,td->ft", proj_weight, rows_grad, preferred_element_type=F32).astype(
            BF16
        )

    own_qkv_grad, own_diag = backward_attention(
        own_seq, qkv, mixed_grad(own_attn_grad), lse_own, offsets, seq_len
    )
    other_qkv_grad, other_diag = backward_attention(
        other_seq, qkv, mixed_grad(other_attn_grad), lse_other, offsets, seq_len
    )

    def input_part(qkv_rows, core_index):
        return jnp.einsum(
            "cft,cdf->td", columns(qkv_rows, core_index), qkv_weight, preferred_element_type=F32
        )

    input_share_grad = sum_shares(
        input_part(own_qkv_grad, core),
        input_part(own_qkv_grad, 1 - core),
        input_part(other_qkv_grad, core),
        input_part(other_qkv_grad, 1 - core),
    )
    own_normed = lax.dynamic_slice_in_dim(normed_one, chip * half, half, 0)
    other_normed = lax.dynamic_slice_in_dim(normed_one, (1 - chip) * half, half, 0)
    qkv_grad = jnp.einsum(
        "td,cft->cdf", own_normed, own_qkv_grad, preferred_element_type=F32
    ) + jnp.einsum("td,cft->cdf", other_normed, other_qkv_grad, preferred_element_type=F32)
    proj_grad = jnp.einsum(
        "td,ft->df", own_attn_grad, mixed_own, preferred_element_type=F32
    ) + jnp.einsum("td,ft->df", other_attn_grad, mixed_other, preferred_element_type=F32)
    token_part = jax.vjp(lambda rows_in: norm_rows(rows_in, attn_gain), input_share)[1](
        input_share_grad
    )[0]
    tokens_grad = hidden_grad + token_part
    attn_gain_grad = jnp.sum(qkv_weight.astype(F32) * qkv_grad, axis=(0, 2)) / attn_gain

    expert_share = unsort_rows(
        sum_shares(own_out[:share], own_out[share:], other_out[:share], other_out[share:])
    )
    layer_out = (hidden_share + gate_prob[:, None] * expert_share).astype(BF16)

    table_local = jnp.dot((own_diag + other_diag)[:, 0], bucket_hot, precision=highest)
    table_full = lax.dynamic_update_slice_in_dim(
        jnp.zeros((heads * tensor_count, bucket_count), F32), table_local, rank * heads, 0
    )
    small = [attn_gain_grad, ffn_gain_grad, router_grad.reshape(-1), table_full.reshape(-1)]
    sizes = [array.size for array in small]
    packed = jnp.concatenate(small)
    packed = jnp.pad(packed, (0, -packed.size % 1024)).reshape(-1, 128)
    packed = sum_everywhere(packed).reshape(-1)
    ends = [sum(sizes[:i]) for i in range(5)]
    attn_gain_grad, ffn_gain_grad, router_grad, table_grad = [
        packed[ends[i] : ends[i + 1]] for i in range(4)
    ]
    split = experts // 2
    down_grad = jnp.concatenate([scatter_sum(down_grad[:split]), scatter_sum(down_grad[split:])])
    up_grad = jnp.concatenate([scatter_sum(up_grad[:split]), scatter_sum(up_grad[split:])])
    return (
        layer_out,
        tokens_grad,
        attn_gain_grad,
        scatter_sum(qkv_grad),
        scatter_sum(proj_grad[None])[0],
        table_grad.reshape(heads * tensor_count, bucket_count),
        ffn_gain_grad,
        router_grad.reshape(router_weight.shape),
        up_grad,
        down_grad,
    )


def solution(mesh):
    placed = (
        P("dp", None),
        P(),
        P(None, None, "tensor"),
        P(None, "tensor"),
        P("tensor", None),
        P(),
        P(),
        P(),
        P("dp", None),
        P(None, None, "tensor"),
        P(None, None, "tensor"),
        P(("dp", "tensor"), None),
    )
    return jax.shard_map(
        on_device,
        mesh=mesh,
        in_specs=placed,
        out_specs=(
            P(("dp", "tensor"), None),
            P(("dp", "tensor"), None),
            P(),
            P(None, "dp", "tensor"),
            P("dp", "tensor"),
            P(),
            P(),
            P(),
            P(None, "dp", "tensor"),
            P(None, "dp", "tensor"),
        ),
        check_vma=False,
    )
```

profile of v0, /device:TPU:0, one launch (start us, length us, event | category | flops | bytes accessed | tf_op | source)
XLA Modules:
  0.0 514.0 jit_solution(7844382427650597543)
XLA Ops:
  8.5 10.7 %attention_forward.3 = (bf16[192,1024]{1,0:T(8,128)(2,1)S(1)}, f32[3,1,1024]{2,1,0:T(1,128)S(1)}) custom-call(s32[1]{0:T(128)S(6)} %sub.157.seq_ref, bf16[3,192,2048]{2,1,0:T(8,128)(2,1)S(1)} %convert_bitcast_fusion.qkv_ref, f32[3,1,2048]{2,1,0:T(1,128)S(1)} %broadcast_in_dim.39.offset_ref), custom_call_target="tpu_custom_call" | custom-call | tf_op jit(solution)/shard_map/attention_forward/pallas_call | solution.py:53
  28.4 10.5 %attention_forward.2 = (bf16[192,1024]{1,0:T(8,128)(2,1)S(1)}, f32[3,1,1024]{2,1,0:T(1,128)S(1)}) custom-call(s32[1]{0:T(128)} %bitcast.seq_ref, bf16[3,192,2048]{2,1,0:T(8,128)(2,1)S(1)} %convert_bitcast_fusion.qkv_ref, f32[3,1,2048]{2,1,0:T(1,128)S(1)} %broadcast_in_dim.39.offset_ref), custom_call_target="tpu_custom_call" | custom-call | tf_op jit(solution)/shard_map/attention_forward/pallas_call | solution.py:53
  46.9 16.7 %collective-permute-done.2 = bf16[512,768]{1,0:T(8,128)(2,1)} collective-permute-done((bf16[512,768]{1,0:T(8,128)(2,1)}, bf16[512,768]{1,0:T(8,128)(2,1)}, u32[]{:S(2)}, u32[]{:S(2)}) %collective-permute-start.2) | collective-permute-done | bytes 786464 | tf_op jit(solution)/shard_map/ppermute | solution.py:372
  81.7 5.3 %collective-permute-done.6 = bf16[512,768]{1,0:T(8,128)(2,1)} collective-permute-done((bf16[512,768]{1,0:T(8,128)(2,1)}, bf16[512,768]{1,0:T(8,128)(2,1)}, u32[]{:S(2)}, u32[]{:S(2)}) %collective-permute-start.6) | collective-permute-done | bytes 786464 | tf_op jit(solution)/shard_map/ppermute | solution.py:372
  89.7 26.8 %experts.2 = (f32[1024,768]{1,0:T(8,128)}, f32[1024,768]{1,0:T(8,128)}, f32[1024,128]{1,0:T(8,128)}, bf16[1536,768]{1,0:T(8,128)(2,1)}, bf16[1536,768]{1,0:T(8,1...) custom-call(s32[10,4]{1,0:T(8,128)} %concatenate.37.plan_ref.refs_0_, ...), custom_call_target="tpu_custom_call" | custom-call | flops 4831838208 | bytes 31457280 | tf_op jit(solution)/shard_map/experts/pallas_call | solution.py:278
  124.5 26.6 %experts.3 = (f32[1024,768]{1,0:T(8,128)}, f32[1024,768]{1,0:T(8,128)}, f32[1024,128]{1,0:T(8,128)}, bf16[1536,768]{1,0:T(8,128)(2,1)}, bf16[1536,768]{1,0:T(8,1...) custom-call(s32[10,4]{1,0:T(8,128)} %concatenate.40.plan_ref.refs_1_, ...), custom_call_target="tpu_custom_call" | custom-call | flops 4831838208 | bytes 31457280 | tf_op jit(solution)/shard_map/experts/pallas_call | solution.py:278
  157.2 29.0 %expert_weight_grads.1 = (bf16[4,768,768]{2,1,0:T(8,128)(2,1)}, bf16[4,768,768]{2,1,0:T(8,128)(2,1)}) custom-call(s32[10,4]{1,0:T(8,128)} %concatenate.37.plan_ref.refs_0_, s32[10,4]{1,0:T(8,128)} %concatenate.40.plan_ref.refs_1_, bf16[1536,768]{1,0:T(8,128)(2,1)} %get-tuple-element.48.refs_2_, bf16[1536,768]{1,0:T(8,128)(2,1)} %get-tuple-element.49.refs_3_, ...), custom_call_target="tpu_custom_call" | custom-call | flops 9663676416 | bytes 31457280 | tf_op jit(solution)/shard_map/expert_weight_grads/pallas_call | solution.py:345
  209.1 18.3 %collective-permute-done.38 = bf16[2,4,96,768]{3,2,1,0:T(8,128)(2,1)} collective-permute-done((bf16[2,4,96,768]{3,2,1,0:T(8,128)(2,1)}, bf16[2,4,96,768]{3,2,1,0:T(8,128)(2,1)}, u32[]{:S(2)}, u32[]{:S(2)}) %collective-permute-start.38) | collective-permute-done | bytes 1179680 | tf_op jit(solution)/shard_map/ppermute | solution.py:372
  230.5 22.2 %collective-permute-done.35 = bf16[2,4,96,768]{3,2,1,0:T(8,128)(2,1)} collective-permute-done((bf16[2,4,96,768]{3,2,1,0:T(8,128)(2,1)}, bf16[2,4,96,768]{3,2,1,0:T(8,128)(2,1)}, u32[]{:S(2)}, u32[]{:S(2)}) %collective-permute-start.35) | collective-permute-done | bytes 1179680 | tf_op jit(solution)/shard_map/ppermute | solution.py:372
  254.7 23.2 %collective-permute-done.44 = bf16[2,4,96,768]{3,2,1,0:T(8,128)(2,1)S(1)} collective-permute-done((bf16[2,4,96,768]{3,2,1,0:T(8,128)(2,1)S(1)}, bf16[2,4,96,768]{3,2,1,0:T(8,128)(2,1)S(1)}, u32[]{:S(2)}, u32[]{:S(2)}) %collective-permute-start.44) | collective-permute-done | bytes 1179680 | tf_op jit(solution)/shard_map/ppermute | solution.py:372
  278.8 23.0 %collective-permute-done.41 = bf16[2,4,96,768]{3,2,1,0:T(8,128)(2,1)S(1)} collective-permute-done((bf16[2,4,96,768]{3,2,1,0:T(8,128)(2,1)}, bf16[2,4,96,768]{3,2,1,0:T(8,128)(2,1)S(1)}, u32[]{:S(2)}, u32[]{:S(2)}) %collective-permute-start.41) | collective-permute-done | bytes 1179680 | tf_op jit(solution)/shard_map/ppermute | solution.py:372
  318.3 15.6 %collective-permute-done.36 = bf16[2,2,96,768]{3,2,1,0:T(8,128)(2,1)S(1)} collective-permute-done((bf16[2,2,96,768]{3,2,1,0:T(8,128)(2,1)S(1)}, bf16[2,2,96,768]{3,2,1,0:T(8,128)(2,1)S(1)}, u32[]{:S(2)}, u32[]{:S(2)}) %collective-permute-start.36) | collective-permute-done | bytes 589856 | tf_op jit(solution)/shard_map/ppermute | solution.py:372
  334.1 18.8 %collective-permute-done.45 = bf16[2,2,96,768]{3,2,0,1:T(8,128)(2,1)S(1)} collective-permute-done((bf16[2,2,96,768]{3,2,0,1:T(8,128)(2,1)S(1)}, bf16[2,2,96,768]{3,2,0,1:T(8,128)(2,1)S(1)}, u32[]{:S(2)}, u32[]{:S(2)}) %collective-permute-start.45) | collective-permute-done | bytes 589856 | tf_op jit(solution)/shard_map/ppermute | solution.py:372
  353.1 10.6 %collective-permute-done.42 = bf16[2,2,96,768]{3,2,1,0:T(8,128)(2,1)S(1)} collective-permute-done((bf16[2,2,96,768]{3,2,1,0:T(8,128)(2,1)S(1)}, bf16[2,2,96,768]{3,2,1,0:T(8,128)(2,1)S(1)}, u32[]{:S(2)}, u32[]{:S(2)}) %collective-permute-start.42) | collective-permute-done | bytes 589856 | tf_op jit(solution)/shard_map/ppermute | solution.py:372
  367.0 20.0 %collective-permute-done.37 = bf16[2,1,96,768]{3,2,1,0:T(8,128)(2,1)S(1)} collective-permute-done((bf16[2,1,96,768]{3,2,1,0:T(8,128)(2,1)S(1)}, bf16[2,1,96,768]{3,2,1,0:T(8,128)(2,1)S(1)}, u32[]{:S(2)}, u32[]{:S(2)}) %collective-permute-start.37) | collective-permute-done | bytes 294944 | tf_op jit(solution)/shard_map/ppermute | solution.py:372
  388.1 5.1 %collective-permute-done.46 = bf16[2,1,96,768]{3,2,0,1:T(8,128)(2,1)S(1)} collective-permute-done((bf16[2,1,96,768]{3,2,0,1:T(8,128)(2,1)S(1)}, bf16[2,1,96,768]{3,2,0,1:T(8,128)(2,1)S(1)}, u32[]{:S(2)}, u32[]{:S(2)}) %collective-permute-start.46) | collective-permute-done | bytes 294944 | tf_op jit(solution)/shard_map/ppermute | solution.py:372
  398.8 12.7 %attention_backward.2 = (bf16[3,192,1024]{2,1,0:T(8,128)(2,1)S(1)}, f32[3,1,2048]{2,1,0:T(1,128)S(1)}) custom-call(s32[1]{0:T(128)} %bitcast.seq_ref, bf16[3,192,2048]{2,1,0:T(8,128)(2,1)S(1)} %convert_bitcast_fusion.qkv_ref, bf16[192,1024]{1,0:T(8,128)(2,1)S(1)} %fusion.20.grad_ref, f32[3,1,1024]{2,1,0:T(1,128)S(1)} %get-tuple-element.42.lse_ref, ...), custom_call_target="tpu_custom_call" | custom-call | tf_op jit(solution)/shard_map/attention_backward/pallas_call | solution.py:124
  416.4 12.5 %attention_backward.3 = (bf16[3,192,1024]{2,1,0:T(8,128)(2,1)S(1)}, f32[3,1,2048]{2,1,0:T(1,128)S(1)}) custom-call(s32[1]{0:T(128)S(6)} %sub.157.seq_ref, bf16[3,192,2048]{2,1,0:T(8,128)(2,1)S(1)} %convert_bitcast_fusion.qkv_ref, bf16[192,1024]{1,0:T(8,128)(2,1)S(1)} %fusion.21.grad_ref, f32[3,1,1024]{2,1,0:T(1,128)S(1)} %get-tuple-element.44.lse_ref, ...), custom_call_target="tpu_custom_call" | custom-call | tf_op jit(solution)/shard_map/attention_backward/pallas_call | solution.py:124
  438.7 5.4 %reshape.457 = f32[3,4,2,96,192]{3,2,1,4,0:T(2,128)} reshape(f32[3,768,192]{1,2,0:T(8,128)} %get-tuple-element.139) | data formatting | bytes 3538944 | tf_op jit(solution)/shard_map/reshape | solution.py:395
  456.0 3.8 constant_dynamic-slice_fusion.6
  478.5 5.0 collective-permute-done.29
  490.1 3.7 collective-permute-done.30
  497.5 5.7 %collective-permute-done.31 = bf16[3,1,96,192]{3,2,1,0:T(8,128)(2,1)S(1)} collective-permute-done((bf16[3,1,96,192]{3,2,1,0:T(8,128)(2,1)S(1)}, bf16[3,1,96,192]{3,2,1,0:T(8,128)(2,1)S(1)}, u32[]{:S(2)}, u32[]{:S(2)}) %collective-permute-start.31) | collective-permute-done | bytes 110624 | tf_op jit(solution)/shard_map/ppermute | solution.py:372
  504.0 4.0 collective-permute-done.23
  (349 shorter events, 176.5 us)
Async XLA Ops:
  28.2 47.8 %collective-permute-start.4 = (bf16[512,768]{1,0:T(8,128)(2,1)}, bf16[512,768]{1,0:T(8,128)(2,1)}, u32[]{:S(2)}, u32[]{:S(2)}) collective-permute-start(bf16[512,768]{1,0:T(8,128)(2,1)} %convolution_convert_fusion.2), channel_id=1, source_target_pairs={{0,1},{1,0},{2,3},{3,2},{4,5},{5,4},{6,7},{7,6},{8,9},{9,8},{10,11... | collective-permute-start | bytes 2359304 | tf_op jit(solution)/shard_map/ppermute | solution.py:372
  46.9 32.2 %collective-permute-start.9 = (bf16[512,768]{1,0:T(8,128)(2,1)}, bf16[512,768]{1,0:T(8,128)(2,1)}, u32[]{:S(2)}, u32[]{:S(2)}) collective-permute-start(bf16[512,768]{1,0:T(8,128)(2,1)} %collective-permute-done.8), channel_id=1, source_target_pairs={{0,1},{1,0},{2,3},{3,2},{4,5},{5,4},{6,7},{7,6},{8,9},{9,8},{10,11... | collective-permute-start | bytes 2359304 | tf_op jit(solution)/shard_map/ppermute | solution.py:372
  87.0 35.1 %collective-permute-start.7 = (bf16[512,768]{1,0:T(8,128)(2,1)}, bf16[512,768]{1,0:T(8,128)(2,1)S(1)}, u32[]{:S(2)}, u32[]{:S(2)}) collective-permute-start(bf16[512,768]{1,0:T(8,128)(2,1)} %collective-permute-done.6), channel_id=1, source_target_pairs={{0,1},{1,0},{2,3},{3,2},{4,5},{5,4},{6,7},{7,6},{8,9},{9,8},{10,11... | collective-permute-start | bytes 2359304 | tf_op jit(solution)/shard_map/ppermute | solution.py:372
  118.9 188.6 %collective-permute-start.5 = (bf16[512,768]{1,0:T(8,128)(2,1)}, bf16[512,768]{1,0:T(8,128)(2,1)}, u32[]{:S(2)}, u32[]{:S(2)}) collective-permute-start(bf16[512,768]{1,0:T(8,128)(2,1)} %slice.165), channel_id=1, source_target_pairs={{0,1},{1,0},{2,3},{3,2},{4,5},{5,4},{6,7},{7,6},{8,9},{9,8},{10,11... | collective-permute-start | bytes 2359304 | tf_op jit(solution)/shard_map/ppermute | solution.py:372
  119.6 78.5 %collective-permute-start.15 = (f32[512]{0:T(512)S(1)}, f32[512]{0:T(512)S(1)}, u32[]{:S(2)}, u32[]{:S(2)}) collective-permute-start(f32[512]{0:T(512)S(1)} %get-tuple-element.102), channel_id=1, source_target_pairs={{0,1},{1,0},{2,3},{3,2},{4,5},{5,4},{6,7},{7,6},{8,9},{9,8},{10,11... | collective-permute-start | bytes 6152 | tf_op jit(solution)/shard_map/ppermute | solution.py:372
  153.5 50.2 %collective-permute-start.10 = (bf16[512,768]{1,0:T(8,128)(2,1)}, bf16[512,768]{1,0:T(8,128)(2,1)}, u32[]{:S(2)}, u32[]{:S(2)}) collective-permute-start(bf16[512,768]{1,0:T(8,128)(2,1)} %slice.164), channel_id=1, source_target_pairs={{0,1},{1,0},{2,3},{3,2},{4,5},{5,4},{6,7},{7,6},{8,9},{9,8},{10,11... | collective-permute-start | bytes 2359304 | tf_op jit(solution)/shard_map/ppermute | solution.py:372
  154.2 41.1 %collective-permute-start.16 = (f32[512]{0:T(512)S(1)}, f32[512]{0:T(512)S(1)}, u32[]{:S(2)}, u32[]{:S(2)}) collective-permute-start(f32[512]{0:T(512)S(1)} %get-tuple-element.104), channel_id=1, source_target_pairs={{0,1},{1,0},{2,3},{3,2},{4,5},{5,4},{6,7},{7,6},{8,9},{9,8},{10,11... | collective-permute-start | bytes 6152 | tf_op jit(solution)/shard_map/ppermute | solution.py:372
  156.7 50.8 %collective-permute-start.13 = (bf16[512,768]{1,0:T(8,128)(2,1)}, bf16[512,768]{1,0:T(8,128)(2,1)}, u32[]{:S(2)}, u32[]{:S(2)}) collective-permute-start(bf16[512,768]{1,0:T(8,128)(2,1)} %slice.162), channel_id=1, source_target_pairs={{0,1},{1,0},{2,3},{3,2},{4,5},{5,4},{6,7},{7,6},{8,9},{9,8},{10,11... | collective-permute-start | bytes 2359304 | tf_op jit(solution)/shard_map/ppermute | solution.py:372
  198.2 29.3 %collective-permute-start.38 = (bf16[2,4,96,768]{3,2,1,0:T(8,128)(2,1)}, bf16[2,4,96,768]{3,2,1,0:T(8,128)(2,1)}, u32[]{:S(2)}, u32[]{:S(2)}) collective-permute-start(bf16[2,4,96,768]{3,2,1,0:T(8,128)(2,1)} %dynamic-slice_bitcast_fusion.2), channel_id=1, source_target_pairs={{0,4},{4,0},{8,12},{12,8},{16,20},{20,16},{24,28},{28,24},{1,5},{5... | collective-permute-start | bytes 3538952 | tf_op jit(solution)/shard_map/ppermute | solution.py:372
  199.8 52.9 %collective-permute-start.35 = (bf16[2,4,96,768]{3,2,1,0:T(8,128)(2,1)}, bf16[2,4,96,768]{3,2,1,0:T(8,128)(2,1)}, u32[]{:S(2)}, u32[]{:S(2)}) collective-permute-start(bf16[2,4,96,768]{3,2,1,0:T(8,128)(2,1)} %dynamic-slice_bitcast_fusion.3), channel_id=1, source_target_pairs={{0,4},{4,0},{8,12},{12,8},{16,20},{20,16},{24,28},{28,24},{1,5},{5... | collective-permute-start | bytes 3538952 | tf_op jit(solution)/shard_map/ppermute | solution.py:372
  204.6 73.3 %collective-permute-start.44 = (bf16[2,4,96,768]{3,2,1,0:T(8,128)(2,1)S(1)}, bf16[2,4,96,768]{3,2,1,0:T(8,128)(2,1)S(1)}, u32[]{:S(2)}, u32[]{:S(2)}) collective-permute-start(bf16[2,4,96,768]{3,2,1,0:T(8,128)(2,1)S(1)} %copy-done.31), channel_id=1, source_target_pairs={{0,4},{4,0},{8,12},{12,8},{16,20},{20,16},{24,28},{28,24},{1,5},{5... | collective-permute-start | bytes 3538952 | tf_op jit(solution)/shard_map/ppermute | solution.py:372
  207.5 94.7 %collective-permute-start.12 = (bf16[512,768]{1,0:T(8,128)(2,1)}, bf16[512,768]{1,0:T(8,128)(2,1)S(1)}, u32[]{:S(2)}, u32[]{:S(2)}) collective-permute-start(bf16[512,768]{1,0:T(8,128)(2,1)} %slice.163), channel_id=1, source_target_pairs={{0,1},{1,0},{2,3},{3,2},{4,5},{5,4},{6,7},{7,6},{8,9},{9,8},{10,11... | collective-permute-start | bytes 2359304 | tf_op jit(solution)/shard_map/ppermute | solution.py:372
  227.4 74.5 %collective-permute-start.41 = (bf16[2,4,96,768]{3,2,1,0:T(8,128)(2,1)}, bf16[2,4,96,768]{3,2,1,0:T(8,128)(2,1)S(1)}, u32[]{:S(2)}, u32[]{:S(2)}) collective-permute-start(bf16[2,4,96,768]{3,2,1,0:T(8,128)(2,1)} %dynamic-slice_bitcast_fusion.1), channel_id=1, source_target_pairs={{0,4},{4,0},{8,12},{12,8},{16,20},{20,16},{24,28},{28,24},{1,5},{5... | collective-permute-start | bytes 3538952 | tf_op jit(solution)/shard_map/ppermute | solution.py:372
  252.7 56.8 %collective-permute-start.11 = (bf16[512,768]{1,0:T(8,128)(2,1)S(1)}, bf16[512,768]{1,0:T(8,128)(2,1)S(1)}, u32[]{:S(2)}, u32[]{:S(2)}) collective-permute-start(bf16[512,768]{1,0:T(8,128)(2,1)S(1)} %add_convert_fusion.2), channel_id=1, source_target_pairs={{0,2},{1,3},{2,0},{3,1},{4,6},{5,7},{6,4},{7,5},{8,10},{9,11},{10,... | collective-permute-start | bytes 2359304 | tf_op jit(solution)/shard_map/ppermute | solution.py:372
  302.3 31.7 %collective-permute-start.36 = (bf16[2,2,96,768]{3,2,1,0:T(8,128)(2,1)S(1)}, bf16[2,2,96,768]{3,2,1,0:T(8,128)(2,1)S(1)}, u32[]{:S(2)}, u32[]{:S(2)}) collective-permute-start(bf16[2,2,96,768]{3,2,1,0:T(8,128)(2,1)S(1)} %fusion.30), channel_id=1, source_target_pairs={{0,8},{4,12},{8,0},{12,4},{16,24},{20,28},{24,16},{28,20},{1,9},{5... | collective-permute-start | bytes 1769480 | tf_op jit(solution)/shard_map/ppermute | solution.py:372
  304.4 48.6 %collective-permute-start.45 = (bf16[2,2,96,768]{3,2,0,1:T(8,128)(2,1)S(1)}, bf16[2,2,96,768]{3,2,0,1:T(8,128)(2,1)S(1)}, u32[]{:S(2)}, u32[]{:S(2)}) collective-permute-start(bf16[2,2,96,768]{3,2,0,1:T(8,128)(2,1)S(1)} %fusion.33), channel_id=1, source_target_pairs={{0,8},{4,12},{8,0},{12,4},{16,24},{20,28},{24,16},{28,20},{1,9},{5... | collective-permute-start | bytes 1769480 | tf_op jit(solution)/shard_map/ppermute | solution.py:372
  307.5 56.2 %collective-permute-start.42 = (bf16[2,2,96,768]{3,2,1,0:T(8,128)(2,1)S(1)}, bf16[2,2,96,768]{3,2,1,0:T(8,128)(2,1)S(1)}, u32[]{:S(2)}, u32[]{:S(2)}) collective-permute-start(bf16[2,2,96,768]{3,2,1,0:T(8,128)(2,1)S(1)} %fusion.31), channel_id=1, source_target_pairs={{0,8},{4,12},{8,0},{12,4},{16,24},{20,28},{24,16},{28,20},{1,9},{5... | collective-permute-start | bytes 1769480 | tf_op jit(solution)/shard_map/ppermute | solution.py:372
  309.5 88.6 %collective-permute-start.20 = (bf16[512,768]{1,0:T(8,128)(2,1)S(1)}, bf16[512,768]{1,0:T(8,128)(2,1)S(1)}, u32[]{:S(2)}, u32[]{:S(2)}) collective-permute-start(bf16[512,768]{1,0:T(8,128)(2,1)S(1)} %fusion.89), channel_id=1, source_target_pairs={{0,2},{1,3},{2,0},{3,1},{4,6},{5,7},{6,4},{7,5},{8,10},{9,11},{10,... | collective-permute-start | bytes 2359304 | tf_op jit(solution)/shard_map/ppermute | solution.py:372
  318.2 79.9 %collective-permute-start.18 = (bf16[512,768]{1,0:T(8,128)(2,1)S(1)}, bf16[512,768]{1,0:T(8,128)(2,1)S(1)}, u32[]{:S(2)}, u32[]{:S(2)}) collective-permute-start(bf16[512,768]{1,0:T(8,128)(2,1)S(1)} %fusion.89), channel_id=1, source_target_pairs={{0,1},{1,0},{2,3},{3,2},{4,5},{5,4},{6,7},{7,6},{8,9},{9,8},{10,11... | collective-permute-start | bytes 2359304 | tf_op jit(solution)/shard_map/ppermute | solution.py:372
  334.0 30.9 %collective-permute-start.40 = (bf16[2,1,96,768]{3,2,0,1:T(8,128)(2,1)S(1)}, bf16[2,1,96,768]{3,2,0,1:T(8,128)(2,1)S(1)}, u32[]{:S(2)}, u32[]{:S(2)}) collective-permute-start(bf16[2,1,96,768]{3,2,0,1:T(8,128)(2,1)S(1)} %dynamic-slice_convert_fusion.4), channel_id=1, source_target_pairs={{0,16},{4,20},{8,24},{12,28},{16,0},{20,4},{24,8},{28,12},{1,17},{... | collective-permute-start | bytes 884744 | tf_op jit(solution)/shard_map/ppermute | solution.py:372
  352.9 34.0 %collective-permute-start.37 = (bf16[2,1,96,768]{3,2,1,0:T(8,128)(2,1)S(1)}, bf16[2,1,96,768]{3,2,1,0:T(8,128)(2,1)S(1)}, u32[]{:S(2)}, u32[]{:S(2)}) collective-permute-start(bf16[2,1,96,768]{3,2,1,0:T(8,128)(2,1)S(1)} %dynamic-slice_convert_fusion.5), channel_id=1, source_target_pairs={{0,16},{4,20},{8,24},{12,28},{16,0},{20,4},{24,8},{28,12},{1,17},{... | collective-permute-start | bytes 884744 | tf_op jit(solution)/shard_map/ppermute | solution.py:372
  363.7 29.6 %collective-permute-start.46 = (bf16[2,1,96,768]{3,2,0,1:T(8,128)(2,1)S(1)}, bf16[2,1,96,768]{3,2,0,1:T(8,128)(2,1)S(1)}, u32[]{:S(2)}, u32[]{:S(2)}) collective-permute-start(bf16[2,1,96,768]{3,2,0,1:T(8,128)(2,1)S(1)} %dynamic-slice_convert_fusion.2), channel_id=1, source_target_pairs={{0,16},{4,20},{8,24},{12,28},{16,0},{20,4},{24,8},{28,12},{1,17},{... | collective-permute-start | bytes 884744 | tf_op jit(solution)/shard_map/ppermute | solution.py:372
  364.9 32.0 %collective-permute-start.43 = (bf16[2,1,96,768]{3,2,1,0:T(8,128)(2,1)S(1)}, bf16[2,1,96,768]{3,2,1,0:T(8,128)(2,1)S(1)}, u32[]{:S(2)}, u32[]{:S(2)}) collective-permute-start(bf16[2,1,96,768]{3,2,1,0:T(8,128)(2,1)S(1)} %dynamic-slice_convert_fusion.3), channel_id=1, source_target_pairs={{0,16},{4,20},{8,24},{12,28},{16,0},{20,4},{24,8},{28,12},{1,17},{... | collective-permute-start | bytes 884744 | tf_op jit(solution)/shard_map/ppermute | solution.py:372
  413.3 90.7 %collective-permute-start.19 = (bf16[512,768]{1,0:T(8,128)(2,1)}, bf16[512,768]{1,0:T(8,128)(2,1)}, u32[]{:S(2)}, u32[]{:S(2)}) collective-permute-start(bf16[512,768]{1,0:T(8,128)(2,1)} %bitcast_convert_fusion.1), channel_id=1, source_target_pairs={{0,1},{1,0},{2,3},{3,2},{4,5},{5,4},{6,7},{7,6},{8,9},{9,8},{10,11... | collective-permute-start | bytes 2359304 | tf_op jit(solution)/shard_map/ppermute | solution.py:372
  (82 other events, 912.8 us)
where the time goes:
time: 519 us; the launch traced here: 514 us
  waiting for transfers between devices  206 us (40%)
  Pallas kernels  129 us (25%)
  local copies, waits for them, and re-layouts  60.1 us (12%)
  other arithmetic  39.5 us (8%)
  matrix products  38.8 us (7%)
  starting transfers between devices  38.7 us (7%)
    ppermute x47, waiting for transfers between devices, swap(): return lax.ppermute(values, axis, [(i, i ^ bit) for i in range(count)])  206 us
    pallas_call x2, Pallas kernels, run_experts(): pl.pallas_call(functools.partial(expert_kernel, shares=shares), grid_spec...  53.4 us
    ppermute x47, starting transfers between devices, swap(): return lax.ppermute(values, axis, [(i, i ^ bit) for i in range(count)])  38.7 us
    pallas_call x1, Pallas kernels, weight_grads(): pl.pallas_call(functools.partial(grads_kernel, halves=halves, plan_row=pl...  29 us
    pallas_call x2, Pallas kernels, backward_attention(): pl.pallas_call(backward_kernel, grid_spec=pltpu.PrefetchScalarGridSpec(nu...  25.2 us
    pallas_call x2, Pallas kernels, forward_attention(): pl.pallas_call(forward_kernel, grid_spec=pltpu.PrefetchScalarGridSpec(num...  21.3 us
    unnamed x123, local copies, waits for them, and re-layouts  13.5 us
  transfers between devices with their start and end apart: 47, of which 19 were waited for; matrix products, arithmetic and copies ran while one was open for 23% of the time, Pallas kernels for 23%

commit v1 on v0

v1 whole, which is shorter than its diff:
```python
import functools
import jax, jax.numpy as jnp
from jax import lax
from jax.experimental import pallas as pl
from jax.experimental.pallas import tpu as pltpu
from jax.sharding import PartitionSpec as P

QB = 256
KB = 128


def mm(a, b, dims):
    return lax.dot_general(a, b, (dims, ((), ())), preferred_element_type=jnp.float32)


def score_block(keys, queries, skew, first_query, seq_len):
    scores = mm(keys, queries, ((1,), (0,)))
    bias = [
        skew[:, pl.ds(pl.multiple_of(first_query - first_key + seq_len - KB, KB), QB)]
        for first_key in range(0, seq_len, KB)
    ]
    return scores + jnp.concatenate(bias, axis=0)


def forward_kernel(seq_ref, qkv_ref, offset_ref, mixed_ref, lse_ref, skew):
    seq_len = qkv_ref.shape[2]
    scale = qkv_ref.shape[1] ** -0.5
    skew[...] = pltpu.roll(
        jnp.broadcast_to(offset_ref[0], (KB, 2 * seq_len)), 0, 1, stride=1, stride_axis=0
    )
    keys = qkv_ref[1].T
    values = qkv_ref[2]

    def block(index, carry):
        first = pl.multiple_of(index * QB, QB)
        queries = qkv_ref[0, :, pl.ds(first, QB)] * jnp.bfloat16(scale)
        scores = score_block(keys, queries, skew, first, seq_len)
        largest = jnp.max(scores, axis=0, keepdims=True)
        expos = jnp.exp(scores - largest)
        total = jnp.sum(expos, axis=0, keepdims=True)
        weights = (expos * (1.0 / total)).astype(jnp.bfloat16)
        mixed_ref[:, pl.ds(first, QB)] = mm(values, weights, ((1,), (0,))).astype(jnp.bfloat16)
        lse_ref[0, :, pl.ds(first, QB)] = largest + jnp.log(total)
        return carry

    lax.fori_loop(0, seq_len // QB, block, 0, unroll=True)


def forward_attention(seq, qkv, offsets, seq_len):
    _, width, rows = qkv.shape
    heads = offsets.shape[0]
    size = width // heads
    return pl.pallas_call(
        forward_kernel,
        grid_spec=pltpu.PrefetchScalarGridSpec(
            num_scalar_prefetch=1,
            grid=(heads,),
            in_specs=[
                pl.BlockSpec((3, size, seq_len), lambda h, s: (0, h, s[0])),
                pl.BlockSpec((1, 1, 2 * seq_len), lambda h, s: (h, 0, 0)),
            ],
            out_specs=[
                pl.BlockSpec((size, seq_len), lambda h, s: (h, 0)),
                pl.BlockSpec((1, 1, seq_len), lambda h, s: (h, 0, 0)),
            ],
            scratch_shapes=[pltpu.VMEM((KB, 2 * seq_len), jnp.float32)],
        ),
        out_shape=[
            jax.ShapeDtypeStruct((width, seq_len), jnp.bfloat16),
            jax.ShapeDtypeStruct((heads, 1, seq_len), jnp.float32),
        ],
        compiler_params=pltpu.CompilerParams(vmem_limit_bytes=48 * 2**20),
        cost_estimate=pl.CostEstimate(
            flops=60 * heads * seq_len * seq_len * size,
            bytes_accessed=30 * 2**20,
            transcendentals=heads * seq_len * seq_len,
        ),
        name="attention_forward",
    )(seq, qkv, offsets)


def backward_kernel(
    seq_ref, qkv_ref, grad_ref, lse_ref, offset_ref, out_ref, diag_ref, skew, sums, probs_all, score_all
):
    seq_len = qkv_ref.shape[2]
    scale = qkv_ref.shape[1] ** -0.5
    skew[...] = pltpu.roll(
        jnp.broadcast_to(offset_ref[0], (KB, 2 * seq_len)), 0, 1, stride=1, stride_axis=0
    )
    sums[...] = jnp.zeros_like(sums)
    keys_t = qkv_ref[1]
    keys = keys_t.T
    values = qkv_ref[2].T

    def block(index, carry):
        first = pl.multiple_of(index * QB, QB)
        here = pl.ds(first, QB)
        queries = qkv_ref[0, :, here] * jnp.bfloat16(scale)
        scores = score_block(keys, queries, skew, first, seq_len)
        probs = jnp.exp(scores - lse_ref[0, :, here])
        probs_all[:, here] = probs.astype(jnp.bfloat16)
        prob_grad = mm(values, grad_ref[:, here], ((1,), (0,)))
        centre = jnp.sum(probs * prob_grad, axis=0, keepdims=True)
        score_grad = probs * (prob_grad - centre)
        rounded = score_grad.astype(jnp.bfloat16)
        score_all[:, here] = rounded
        for first_key in range(0, seq_len, KB):
            spot = pl.ds(pl.multiple_of(first - first_key + seq_len - KB, KB), QB)
            sums[:, spot] += score_grad[first_key : first_key + KB]
        out_ref[0, :, here] = (mm(keys_t, rounded, ((1,), (0,))) * scale).astype(jnp.bfloat16)
        return carry

    lax.fori_loop(0, seq_len // QB, block, 0, unroll=True)
    queries = qkv_ref[0] * jnp.bfloat16(scale)
    out_ref[1] = mm(queries, score_all[...], ((1,), (1,))).astype(jnp.bfloat16)
    out_ref[2] = mm(grad_ref[...], probs_all[...], ((1,), (1,))).astype(jnp.bfloat16)
    part = sums[...]
    half = KB // 2
    while half >= 1:
        part = part[:half] + pltpu.roll(part[half:], 2 * seq_len - half, 1)
        half //= 2
    diag_ref[0] = part


def backward_attention(seq, qkv, grads, lse, offsets, seq_len):
    _, width, rows = qkv.shape
    heads = offsets.shape[0]
    size = width // heads
    return pl.pallas_call(
        backward_kernel,
        grid_spec=pltpu.PrefetchScalarGridSpec(
            num_scalar_prefetch=1,
            grid=(heads,),
            in_specs=[
                pl.BlockSpec((3, size, seq_len), lambda h, s: (0, h, s[0])),
                pl.BlockSpec((size, seq_len), lambda h, s: (h, 0)),
                pl.BlockSpec((1, 1, seq_len), lambda h, s: (h, 0, 0)),
                pl.BlockSpec((1, 1, 2 * seq_len), lambda h, s: (h, 0, 0)),
            ],
            out_specs=[
                pl.BlockSpec((3, size, seq_len), lambda h, s: (0, h, 0)),
                pl.BlockSpec((1, 1, 2 * seq_len), lambda h, s: (h, 0, 0)),
            ],
            scratch_shapes=[
                pltpu.VMEM((KB, 2 * seq_len), jnp.float32),
                pltpu.VMEM((KB, 2 * seq_len), jnp.float32),
                pltpu.VMEM((seq_len, seq_len), jnp.bfloat16),
                pltpu.VMEM((seq_len, seq_len), jnp.bfloat16),
            ],
        ),
        out_shape=[
            jax.ShapeDtypeStruct((3, width, seq_len), jnp.bfloat16),
            jax.ShapeDtypeStruct((heads, 1, 2 * seq_len), jnp.float32),
        ],
        compiler_params=pltpu.CompilerParams(vmem_limit_bytes=48 * 2**20),
        cost_estimate=pl.CostEstimate(
            flops=70 * heads * seq_len * seq_len * size,
            bytes_accessed=40 * 2**20,
            transcendentals=heads * seq_len * seq_len,
        ),
        name="attention_backward",
    )(seq, qkv, grads, lse, offsets)


CH = 16
UNIT = 128
FIELDS = 4


def unit_limit(rows, shares, experts):
    chunks = rows // CH + shares * (experts - 1)
    return (chunks + experts * (UNIT // CH - 1)) // (UNIT // CH)


def plan_segments(counts):
    starts = jnp.cumsum(counts, axis=1) - counts
    first = starts // CH
    chunks = jnp.where(counts > 0, (starts + counts + CH - 1) // CH - first, 0)
    units = (jnp.sum(chunks, axis=0) * CH + UNIT - 1) // UNIT
    base = jnp.cumsum(units) - units
    return jnp.concatenate(
        [first, chunks, starts, starts + counts, units[None], base[None]], axis=0
    ).astype(jnp.int32)


def for_units(units, step):
    def double(index, carry):
        step(index * (2 * UNIT), 2 * UNIT)
        return carry

    lax.fori_loop(0, units // 2, double, 0)

    @pl.when(units % 2 == 1)
    def _():
        step((units - 1) * UNIT, UNIT)


def at_rows(start, size):
    return pl.ds(pl.multiple_of(start, size if size < UNIT else UNIT), size)


def gather_rows(plan_ref, expert, shares, units, rows_refs, grad_refs, xs, cs, base):
    filled = 0
    for share in range(shares):
        first = plan_ref[share, expert]
        chunks = plan_ref[shares + share, expert]
        start = plan_ref[2 * shares + share, expert]
        end = plan_ref[3 * shares + share, expert]
        x_ref, c_ref = rows_refs[share], grad_refs[share]

        def gather(index, carry):
            here = (first + index) * CH
            local = (filled + index) * CH
            row = here + lax.broadcasted_iota(jnp.int32, (CH, 1), 0)
            keep = (row >= start) & (row < end)
            zero = jnp.zeros((), jnp.bfloat16)
            xs[at_rows(base + local, CH)] = jnp.where(keep, x_ref[at_rows(here, CH)], zero)
            cs[at_rows(local, CH)] = jnp.where(keep, c_ref[at_rows(here, CH)], zero)
            return carry

        lax.fori_loop(0, chunks, gather, 0)
        filled = filled + chunks

    def clear(index, carry):
        xs[at_rows(base + index * CH, CH)] = jnp.zeros((CH, xs.shape[1]), jnp.bfloat16)
        cs[at_rows(index * CH, CH)] = jnp.zeros((CH, cs.shape[1]), jnp.bfloat16)
        return carry

    lax.fori_loop(filled, units * (UNIT // CH), clear, 0)


def scatter_rows(plan_ref, expert, shares, buffers, outs):
    filled = 0
    for share in range(shares):
        first = plan_ref[share, expert]
        chunks = plan_ref[shares + share, expert]

        def scatter(index, carry):
            target = at_rows((first + index) * CH, CH)
            local = at_rows((filled + index) * CH, CH)
            for buffer, targets in zip(buffers, outs):
                out = targets[share]
                out[target] = (out[target].astype(jnp.float32) + buffer[local]).astype(out.dtype)
            return carry

        lax.fori_loop(0, chunks, scatter, 0)
        filled = filled + chunks


def expert_kernel(*refs, shares, first_expert, expert_count, with_grads):
    plan_ref, refs = refs[0], refs[1:]
    if with_grads:
        past_plan, refs = refs[0], refs[1:]
    x_refs, refs = refs[:shares], refs[shares:]
    c_refs, refs = refs[:shares], refs[shares:]
    router_ref, up_ref, down_ref, *refs = refs
    if with_grads:
        past, refs = refs[:4], refs[4:]
    y_refs, refs = refs[:shares], refs[shares:]
    back_refs, refs = refs[:shares], refs[shares:]
    gate_refs, refs = refs[:shares], refs[shares:]
    if with_grads:
        up_out, down_out, *refs = refs
        xs, ms, dys, dus, cs, ybuf, bbuf, gbuf, *refs = refs
        old, up_acc, down_acc, sems = refs[:4], refs[4], refs[5], refs[6]
    else:
        xs, ms, dys, dus, cs, ybuf, bbuf, gbuf = refs
    step = pl.program_id(0)
    expert = step + first_expert
    units = plan_ref[4 * shares, expert]
    base = 0 if with_grads else plan_ref[4 * shares + 1, expert] * UNIT

    @pl.when(step == 0)
    def _():
        for out in (*y_refs, *back_refs, *gate_refs):
            out[...] = jnp.zeros_like(out)

    if with_grads:
        past_units = past_plan[4 * shares, expert]
        past_base = past_plan[4 * shares + 1, expert] * UNIT

        def copies(index):
            return [
                pltpu.make_async_copy(
                    source.at[at_rows(past_base + index * UNIT, UNIT)],
                    target.at[at_rows(index * UNIT, UNIT)],
                    sems.at[which, index],
                )
                for which, (source, target) in enumerate(zip(past, old))
            ]

        def begin(index, carry):
            for copy in copies(index):
                copy.start()
            return carry

        def finish(index, carry):
            for copy in copies(index):
                copy.wait()
            return carry

        lax.fori_loop(0, past_units, begin, 0)

    gather_rows(plan_ref, expert, shares, units, x_refs, c_refs, xs, cs, base)

    def tile(start, size):
        local = at_rows(start, size)
        saved = at_rows(base + start, size)
        x = xs[saved]
        c = cs[local].astype(jnp.float32)
        logits = mm(x, router_ref[...], ((1,), (0,)))
        lane = lax.broadcasted_iota(jnp.int32, logits.shape, 1)
        logits = jnp.where(lane < expert_count, logits, -jnp.inf)
        expos = jnp.exp(logits - jnp.max(logits, axis=1, keepdims=True))
        mine = jnp.sum(jnp.where(lane == expert, expos, 0.0), axis=1, keepdims=True)
        gate = mine / jnp.sum(expos, axis=1, keepdims=True)
        dy = (gate * c).astype(jnp.bfloat16)
        dys[saved] = dy
        u = mm(x, up_ref[0], ((1,), (0,)))
        dm = mm(dy, down_ref[0], ((1,), (0,)))
        root = 0.7978845608028654
        square = u * u
        bent = jnp.tanh(root * (u * (1.0 + 0.044715 * square)))
        half = 0.5 * (1.0 + bent)
        m = (u * half).astype(jnp.bfloat16)
        ms[saved] = m
        slope = half + (0.5 * root) * (u * ((1.0 - bent * bent) * (1.0 + (3 * 0.044715) * square)))
        du = (slope * dm).astype(jnp.bfloat16)
        dus[saved] = du
        y = mm(m, down_ref[0], ((1,), (1,)))
        ybuf[local] = y
        gbuf[local] = jnp.broadcast_to(jnp.sum(y * c, axis=1, keepdims=True), (size, gbuf.shape[1]))
        bbuf[local] = mm(du, up_ref[0], ((1,), (1,)))

    for_units(units, tile)
    scatter_rows(
        plan_ref, expert, shares, (ybuf, bbuf, gbuf), (y_refs, back_refs, gate_refs)
    )

    if with_grads:
        up_acc[...] = jnp.zeros_like(up_acc)
        down_acc[...] = jnp.zeros_like(down_acc)

        def add(arrays):
            def part(start, size):
                here = at_rows(start, size)
                x, m, dy, du = [array[here] for array in arrays]
                up_acc[...] += mm(x, du, ((0,), (0,)))
                down_acc[...] += mm(dy, m, ((0,), (0,)))

            return part

        for_units(units, add((xs, ms, dys, dus)))
        lax.fori_loop(0, past_units, finish, 0)
        for_units(past_units, add(old))
        up_out[0] = up_acc[...].astype(jnp.bfloat16)
        down_out[0] = down_acc[...].astype(jnp.bfloat16)


def run_experts(plan, x, c, router, up, down, past=None, first_expert=0, step_count=None):
    shares = len(x)
    rows, width = x[0].shape
    experts, _, hidden = up.shape
    steps = step_count or experts
    with_grads = past is not None
    saved = unit_limit(rows * shares, shares, experts) * UNIT
    most = rows * shares
    brain, full = jnp.bfloat16, jnp.float32
    whole = lambda shape: pl.BlockSpec(shape, lambda e, *p: (0, 0))
    block = pl.BlockSpec((1, width, hidden), lambda e, *p: (first_expert + e, 0, 0))
    scalars = [plan]
    inputs = [*x, *c, router, up, down]
    in_specs = [whole((rows, width))] * (2 * shares) + [whole(router.shape), block, block]
    row_types = [full] + [brain] * (shares - 1)
    out_shape = [jax.ShapeDtypeStruct((rows, width), kind) for kind in row_types * 2]
    out_specs = [whole((rows, width))] * (2 * shares) + [whole((rows, 128))] * shares
    out_shape += [jax.ShapeDtypeStruct((rows, 128), full)] * shares
    scratch = [
        pltpu.VMEM((most, width), brain),
        pltpu.VMEM((most, width), full),
        pltpu.VMEM((most, width), full),
        pltpu.VMEM((most, 128), full),
    ]
    widths = (width, hidden, width, hidden)
    if with_grads:
        past_plan, past_arrays = past
        scalars.append(past_plan)
        inputs += past_arrays
        in_specs += [pl.BlockSpec(memory_space=pl.ANY)] * 4
        grad_block = pl.BlockSpec((1, width, hidden), lambda e, *p: (e, 0, 0))
        out_specs += [grad_block, grad_block]
        out_shape += [jax.ShapeDtypeStruct((steps, width, hidden), brain)] * 2
        buffers = [pltpu.VMEM((most, size), brain) for size in widths]
        scratch = (
            buffers
            + scratch
            + buffers
            + [pltpu.VMEM((width, hidden), full)] * 2
            + [pltpu.SemaphoreType.DMA((4, most // UNIT))]
        )
    else:
        out_specs += [whole((saved, size)) for size in widths]
        out_shape += [jax.ShapeDtypeStruct((saved, size), brain) for size in widths]
    return pl.pallas_call(
        functools.partial(
            expert_kernel,
            shares=shares,
            first_expert=first_expert,
            expert_count=experts,
            with_grads=with_grads,
        ),
        grid_spec=pltpu.PrefetchScalarGridSpec(
            num_scalar_prefetch=len(scalars),
            grid=(steps,),
            in_specs=in_specs,
            out_specs=out_specs,
            scratch_shapes=scratch,
        ),
        out_shape=out_shape,
        compiler_params=pltpu.CompilerParams(vmem_limit_bytes=58 * 2**20),
        cost_estimate=pl.CostEstimate(
            flops=20 * rows * shares * width * hidden * steps // experts,
            bytes_accessed=30 * 2**20,
            transcendentals=0,
        ),
        name="experts_and_grads" if with_grads else "experts",
    )(*scalars, *inputs)


EPS = 1e-06
F32 = jnp.float32
BF16 = jnp.bfloat16


def norm_rows(values, gain_vector):
    return values * lax.rsqrt(jnp.mean(values * values, axis=-1, keepdims=True) + EPS) * gain_vector


def swap(values, axis, bit):
    count = lax.axis_size(axis)
    return lax.ppermute(values, axis, [(i, i ^ bit) for i in range(count)])


def after(value, *milestones):
    return lax.optimization_barrier((value, milestones))[0]


class ScatterSum:
    def __init__(self, values):
        self.values = values
        self.bit = 1
        self.count = lax.axis_size("dp")
        self.piece = values.shape[1] // self.count
        self.moving = None

    def start(self, *milestones):
        if self.moving is not None:
            keep, received = after((self.keep, self.moving), *milestones)
            self.values = keep.astype(F32) + received.astype(F32)
            self.moving = None
        if self.bit >= self.count:
            return
        experts, width = self.values.shape[0], self.values.shape[-1]
        shape = (experts, self.count // (2 * self.bit), 2, self.piece, width)
        values = after(self.values, *milestones).reshape(shape)
        mine = (lax.axis_index("dp") // self.bit) % 2
        self.keep = lax.dynamic_index_in_dim(values, mine, 2, keepdims=False)
        send = lax.dynamic_index_in_dim(values, 1 - mine, 2, keepdims=False)
        self.sent = send.astype(BF16)
        self.moving = swap(self.sent, "dp", self.bit)
        self.bit *= 2

    def finish(self):
        while self.moving is not None or self.bit < self.count:
            self.start()
        return self.values.reshape(self.values.shape[0], self.piece, self.values.shape[-1])


def sum_everywhere(values):
    for axis in ("tensor", "dp"):
        bit = 1
        while bit < lax.axis_size(axis):
            values = values + swap(values, axis, bit)
            bit *= 2
    return values


def on_device(
    tokens,
    attn_gain,
    qkv_weight,
    proj_weight,
    bias_table,
    buckets,
    ffn_gain,
    router_weight,
    routes,
    up_weight,
    down_weight,
    cotangent,
):
    highest = lax.Precision.HIGHEST
    rank = lax.axis_index("tensor")
    core, chip = rank % 2, rank // 2
    tensor_count = lax.axis_size("tensor")
    rows, width = tokens.shape
    share = rows // tensor_count
    half = rows // 2
    seq_len = (buckets.shape[0] + 1) // 2
    heads, bucket_count = bias_table.shape
    experts = up_weight.shape[0]
    own_seq = chip.astype(jnp.int32).reshape(1)
    other_seq = 1 - own_seq

    flipped = buckets[::-1]
    cut = KB - 1
    turned = jnp.concatenate([flipped[cut:], jnp.full((1,), -1, flipped.dtype), flipped[:cut]])
    bucket_hot = (turned[:, None] == jnp.arange(bucket_count)[None, :]).astype(F32)
    offsets = jnp.dot(bias_table, bucket_hot.T, precision=highest)[:, None, :]

    all_routes = routes[:, 0].reshape(tensor_count, share)
    counts = jnp.sum((all_routes[:, :, None] == jnp.arange(experts)).astype(jnp.int32), axis=1)
    order = rank ^ jnp.arange(tensor_count)
    same = order[:, None] == jnp.arange(tensor_count)[None, :]
    counts = jnp.sum(jnp.where(same[:, :, None], counts[None], 0), axis=1)
    own_plan = plan_segments(counts[:2])
    other_plan = plan_segments(counts[2:])
    my_routes = lax.dynamic_slice_in_dim(routes[:, 0], rank * share, share, 0)
    my_hot = (my_routes[:, None] == jnp.arange(experts)[None, :]).astype(F32)
    earlier = (jnp.arange(share)[:, None] > jnp.arange(share)[None, :]).astype(BF16)
    ahead = jnp.dot(earlier, my_hot.astype(BF16), preferred_element_type=F32)
    starts = (jnp.cumsum(counts[0]) - counts[0]).astype(F32)
    position = jnp.sum(my_hot * (ahead + starts[None, :]), axis=1).astype(jnp.int32)
    place = jnp.arange(share)[:, None] == position[None, :]
    place_matrix = place.astype(BF16)

    def sort_rows(values):
        return jnp.dot(place_matrix, values, preferred_element_type=F32).astype(BF16)

    def unsort_rows(values):
        dims = (((0,), (0,)), ((), ()))
        high = lax.reduce_precision(values, 8, 7)
        low = (values - high).astype(BF16)
        return lax.dot_general(
            place_matrix, high.astype(BF16), dims, preferred_element_type=F32
        ) + lax.dot_general(place_matrix, low, dims, preferred_element_type=F32)

    grad_mine = sort_rows(cotangent)
    grad_far = swap(grad_mine, "tensor", 2)
    grad_near = swap(grad_mine, "tensor", 1)

    normed_one = norm_rows(tokens.astype(F32), attn_gain).astype(BF16)
    input_share = lax.dynamic_slice_in_dim(tokens, rank * share, share, 0).astype(F32)
    qkv = jnp.einsum("cdf,td->cft", qkv_weight, normed_one, preferred_element_type=F32).astype(BF16)

    def columns(values, core_index):
        return lax.dynamic_slice_in_dim(values, core_index * share, share, values.ndim - 1)

    def project(mixed, core_index):
        return jnp.einsum(
            "ft,df->td", columns(mixed, core_index), proj_weight, preferred_element_type=F32
        )

    mixed_other, lse_other = forward_attention(other_seq, qkv, offsets, seq_len)
    passed = swap(project(mixed_other, 1 - core).astype(BF16), "tensor", 1)
    attn_sent = (project(mixed_other, core) + passed.astype(F32)).astype(BF16)
    attn_far = swap(attn_sent, "tensor", 2)
    mixed_own, lse_own = forward_attention(after(own_seq, attn_sent), qkv, offsets, seq_len)
    attn_near = swap(project(mixed_own, 1 - core).astype(BF16), "tensor", 1)
    attn_share = project(mixed_own, core) + attn_near.astype(F32) + attn_far.astype(F32)
    grad_far = after(grad_far, mixed_own)
    grad_both = swap(grad_far, "tensor", 1)
    hidden_share = input_share + attn_share
    normed_two = norm_rows(hidden_share, ffn_gain).astype(BF16)

    rows_mine = sort_rows(normed_two)
    rows_far = swap(rows_mine, "tensor", 2)
    rows_near = swap(rows_mine, "tensor", 1)
    padded_router = jnp.pad(router_weight, ((0, 0), (0, 128 - experts)))
    own = run_experts(
        own_plan, [rows_mine, rows_near], [grad_mine, grad_near], padded_router, up_weight, down_weight
    )
    past = (own_plan, own[6:])
    rows_far = after(rows_far, own[0])
    other_rows = [rows_far, swap(rows_far, "tensor", 1)]
    split = experts // 2

    def run_other(plan, start):
        return run_experts(
            plan, other_rows, [grad_far, grad_both], padded_router, up_weight, down_weight,
            past, start, split,
        )

    first = run_other(other_plan, 0)
    down_one, up_one = ScatterSum(first[7]), ScatterSum(first[6])
    down_one.start()
    second = run_other(after(other_plan, down_one.sent), split)
    down_two, up_two = ScatterSum(second[7]), ScatterSum(second[6])
    other = [one.astype(F32) + two.astype(F32) for one, two in zip(first[:6], second[:6])]
    back_passed = swap(other[3].astype(BF16), "tensor", 1)
    passed = swap(other[5][:, 0], "tensor", 1)
    back_sent = (other[2] + back_passed.astype(F32)).astype(BF16)
    back_far = swap(back_sent, "tensor", 2)
    gate_sorted = (
        own[4][:, 0]
        + swap(own[5][:, 0], "tensor", 1)
        + swap(other[4][:, 0] + passed, "tensor", 2)
    )
    back_near = swap(own[3], "tensor", 1)
    up_one.start(back_sent)
    back_far = after(back_far, up_one.sent)
    back_share = unsort_rows(own[2] + back_near.astype(F32) + back_far.astype(F32))
    gate_grad = jnp.sum(jnp.where(place, gate_sorted[:, None], 0.0), axis=0)

    logits = jnp.dot(normed_two, router_weight, preferred_element_type=F32)
    router_probs = jax.nn.softmax(logits, axis=-1)
    gate_prob = jnp.sum(router_probs * my_hot, axis=-1)
    grad_out = cotangent.astype(F32)
    logit_grad = ((gate_grad * gate_prob)[:, None] * (my_hot - router_probs)).astype(BF16)
    router_grad = jnp.einsum("td,te->de", normed_two, logit_grad, preferred_element_type=F32)
    normed_grad = back_share + jnp.einsum(
        "te,de->td", logit_grad, router_weight, preferred_element_type=F32
    )
    hidden_part, ffn_gain_grad = jax.vjp(norm_rows, hidden_share, ffn_gain)[1](normed_grad)
    hidden_grad = grad_out + hidden_part

    attn_grad = hidden_grad.astype(BF16)
    far_grad = swap(attn_grad, "tensor", 2)
    near_grad = swap(attn_grad, "tensor", 1)
    down_one.start(attn_grad)
    down_two.start(attn_grad)

    def in_order(mine, partner):
        return jnp.concatenate(
            [jnp.where(core == 0, mine, partner), jnp.where(core == 0, partner, mine)]
        )

    def mixed_grad(rows_grad):
        return jnp.einsum("df,td->ft", proj_weight, rows_grad, preferred_element_type=F32).astype(
            BF16
        )

    own_attn_grad = in_order(attn_grad, near_grad)
    own_mixed_grad = after(mixed_grad(own_attn_grad), down_one.sent, down_two.sent)
    own_qkv_grad, own_diag = backward_attention(
        own_seq, qkv, own_mixed_grad, lse_own, offsets, seq_len
    )
    far_grad = after(far_grad, own_qkv_grad)
    other_attn_grad = in_order(far_grad, swap(far_grad, "tensor", 1))
    held = after((own[0], own[1], other[0], other[1]), own_qkv_grad)
    out_passed = swap(held[3].astype(BF16), "tensor", 1)
    out_sent = (held[2] + out_passed.astype(F32)).astype(BF16)
    out_far = swap(out_sent, "tensor", 2)
    out_near = swap(held[1], "tensor", 1)
    up_one.start(own_qkv_grad)
    down_one.start(own_qkv_grad)
    up_two.start(own_qkv_grad)
    other_mixed_grad = after(
        mixed_grad(other_attn_grad), out_sent, up_one.sent, down_one.sent, up_two.sent
    )
    other_qkv_grad, other_diag = backward_attention(
        other_seq, qkv, other_mixed_grad, lse_other, offsets, seq_len
    )

    def input_part(qkv_rows, core_index):
        return jnp.einsum(
            "cft,cdf->td", columns(qkv_rows, core_index), qkv_weight, preferred_element_type=F32
        )

    input_passed = swap(input_part(other_qkv_grad, 1 - core).astype(BF16), "tensor", 1)
    input_sent = (input_part(other_qkv_grad, core) + input_passed.astype(F32)).astype(BF16)
    input_far = swap(input_sent, "tensor", 2)
    own_late = after(own_qkv_grad, input_sent)
    input_near = swap(input_part(own_late, 1 - core).astype(BF16), "tensor", 1)
    down_two.start(input_sent)
    up_one.start(input_sent)
    own_normed = lax.dynamic_slice_in_dim(normed_one, chip * half, half, 0)
    other_normed = lax.dynamic_slice_in_dim(normed_one, (1 - chip) * half, half, 0)
    qkv_grad = jnp.einsum(
        "td,cft->cdf", own_normed, own_late, preferred_element_type=F32
    ) + jnp.einsum("td,cft->cdf", other_normed, other_qkv_grad, preferred_element_type=F32)
    proj_grad = jnp.einsum(
        "td,ft->df", own_attn_grad, mixed_own, preferred_element_type=F32
    ) + jnp.einsum("td,ft->df", other_attn_grad, mixed_other, preferred_element_type=F32)
    projections = ScatterSum(jnp.concatenate([qkv_grad, proj_grad[None]]))
    projections.start(down_two.sent, up_one.sent)
    input_share_grad = (
        input_part(own_late, core)
        + input_near.astype(F32)
        + after(input_far, projections.sent).astype(F32)
    )
    token_part = jax.vjp(lambda rows_in: norm_rows(rows_in, attn_gain), input_share)[1](
        input_share_grad
    )[0]
    tokens_grad = hidden_grad + token_part
    attn_gain_grad = jnp.sum(qkv_weight.astype(F32) * qkv_grad, axis=(0, 2)) / attn_gain

    out_far = after(out_far, input_sent)
    expert_share = unsort_rows(held[0] + out_near.astype(F32) + out_far.astype(F32))
    layer_out = (hidden_share + gate_prob[:, None] * expert_share).astype(BF16)

    table_local = jnp.dot((own_diag + other_diag)[:, 0], bucket_hot, precision=highest)
    table_full = lax.dynamic_update_slice_in_dim(
        jnp.zeros((heads * tensor_count, bucket_count), F32), table_local, rank * heads, 0
    )
    small = [attn_gain_grad, ffn_gain_grad, router_grad.reshape(-1), table_full.reshape(-1)]
    sizes = [array.size for array in small]
    packed = jnp.concatenate(small)
    packed = jnp.pad(packed, (0, -packed.size % 1024)).reshape(-1, 128)
    packed = sum_everywhere(after(packed, projections.sent)).reshape(-1)
    ends = [sum(sizes[:i]) for i in range(5)]
    attn_gain_grad, ffn_gain_grad, router_grad, table_grad = [
        packed[ends[i] : ends[i + 1]] for i in range(4)
    ]
    up_two.start(input_share_grad)
    projections.start(input_share_grad)
    down_grad = jnp.concatenate([down_one.finish(), down_two.finish()])
    up_grad = jnp.concatenate([up_one.finish(), up_two.finish()])
    qkv_proj = projections.finish()
    return (
        layer_out,
        tokens_grad,
        attn_gain_grad,
        qkv_proj[:3],
        qkv_proj[3],
        table_grad.reshape(heads * tensor_count, bucket_count),
        ffn_gain_grad,
        router_grad.reshape(router_weight.shape),
        up_grad,
        down_grad,
    )


def solution(mesh):
    placed = (
        P("dp", None),
        P(),
        P(None, None, "tensor"),
        P(None, "tensor"),
        P("tensor", None),
        P(),
        P(),
        P(),
        P("dp", None),
        P(None, None, "tensor"),
        P(None, None, "tensor"),
        P(("dp", "tensor"), None),
    )
    return jax.shard_map(
        on_device,
        mesh=mesh,
        in_specs=placed,
        out_specs=(
            P(("dp", "tensor"), None),
            P(("dp", "tensor"), None),
            P(),
            P(None, "dp", "tensor"),
            P("dp", "tensor"),
            P(),
            P(),
            P(),
            P(None, "dp", "tensor"),
            P(None, "dp", "tensor"),
        ),
        check_vma=False,
    )
```

time: 519 us -> 388 us (0.75)
  waiting for transfers between devices: 206 us -> 92.3 us
  Pallas kernels: 129 us -> 106 us
    ppermute x47 -> x44, waiting for transfers between devices: 206 us -> 92.3 us  [swap(): return lax.ppermute(values, axis, [(i, i ^ bit) for i in range(count)])]
    pallas_call x3, Pallas kernels: 82.4 us -> 59.6 us  [run_experts(): pl.pallas_call(functools.partial(expert_kernel, shares=shares, first_expe...]
    slice x9 -> x4, local copies, waits for them, and re-layouts: 13 us -> 1.02 us  [the longest x1 0.74 us: on_device(): qkv_proj[:3]]
    concatenate x6 -> x3, other arithmetic: 12.6 us -> 3.83 us  [the longest x1 1.63 us: on_device(): projections = ScatterSum(jnp.concatenate([qkv_grad, proj_grad[None]]))]
    squeeze x4 -> x13, local copies, waits for them, and re-layouts: 4.58 us -> 12.2 us  [the longest x12 11.5 us: start(): self.keep = lax.dynamic_index_in_dim(values, mine, 2, keepdims=False)]
    add x14 -> x15, other arithmetic: 6.6 us -> 11 us  [the longest x11 8.57 us: start(): self.values = keep.astype(F32) + received.astype(F32)]
    unnamed x123 -> x140, local copies, waits for them, and re-layouts: 13.5 us -> 15.6 us
    dynamic_slice x6 -> x3, local copies, waits for them, and re-layouts: 12 us -> 10.8 us  [the longest x2 7.52 us: start(): self.keep = lax.dynamic_index_in_dim(values, mine, 2, keepdims=False)]
  transfers between devices with their start and end apart: 47 -> 44, of which waited for: 19 -> 13; matrix products, arithmetic and copies ran while one was open for 23% -> 31% of each run, Pallas kernels for 23% -> 15%
where the time goes in v1:
time: 388 us; the launch traced here: 383 us
  Pallas kernels  106 us (27%)
  waiting for transfers between devices  92.3 us (24%)
  local copies, waits for them, and re-layouts  61.6 us (16%)
  other arithmetic  41.3 us (11%)
  matrix products  40.9 us (11%)
  starting transfers between devices  38 us (10%)
    ppermute x44, waiting for transfers between devices, swap(): return lax.ppermute(values, axis, [(i, i ^ bit) for i in range(count)])  92.3 us
    pallas_call x3, Pallas kernels, run_experts(): pl.pallas_call(functools.partial(expert_kernel, shares=shares, first_expe...  59.6 us
    ppermute x44, starting transfers between devices, swap(): return lax.ppermute(values, axis, [(i, i ^ bit) for i in range(count)])  38 us
    pallas_call x2, Pallas kernels, backward_attention(): pl.pallas_call(backward_kernel, grid_spec=pltpu.PrefetchScalarGridSpec(nu...  25.2 us
    pallas_call x2, Pallas kernels, forward_attention(): pl.pallas_call(forward_kernel, grid_spec=pltpu.PrefetchScalarGridSpec(num...  21.3 us
    unnamed x140, local copies, waits for them, and re-layouts  15.6 us
    squeeze x12, local copies, waits for them, and re-layouts, start(): self.keep = lax.dynamic_index_in_dim(values, mine, 2, keepdims=False)  11.5 us
    dot_general x4, matrix products, input_part(): jnp.einsum('cft,cdf->td', columns(qkv_rows, core_index), qkv_weight, pref...  9.43 us
  transfers between devices with their start and end apart: 44, of which 13 were waited for; matrix products, arithmetic and copies ran while one was open for 31% of the time, Pallas kernels for 15%

profile of v1, /device:TPU:0, one launch (start us, length us, event | category | flops | bytes accessed | tf_op | source)
XLA Modules:
  0.0 382.7 jit_solution(10506047347328438235)
XLA Ops:
  9.5 10.8 %attention_forward.2 = (bf16[192,1024]{1,0:T(8,128)(2,1)S(1)}, f32[3,1,1024]{2,1,0:T(1,128)S(1)}) custom-call(s32[1]{0:T(128)S(6)} %sub.150.seq_ref, bf16[3,192,2048]{2,1,0:T(8,128)(2,1)S(1)} %convert_bitcast_fusion.qkv_ref, f32[3,1,2048]{2,1,0:T(1,128)S(1)} %broadcast_in_dim.41.offset_ref), custom_call_target="tpu_custom_call" | custom-call | flops 12079595520 | bytes 31457280 | tf_op jit(solution)/shard_map/attention_forward/pallas_call | solution.py:53
  29.6 10.5 %attention_forward.3 = (bf16[192,1024]{1,0:T(8,128)(2,1)S(1)}, f32[3,1,1024]{2,1,0:T(1,128)S(1)}) custom-call(s32[1]{0:T(128)} %bitcast.seq_ref, bf16[3,192,2048]{2,1,0:T(8,128)(2,1)S(1)} %convert_bitcast_fusion.qkv_ref, f32[3,1,2048]{2,1,0:T(1,128)S(1)} %broadcast_in_dim.41.offset_ref), custom_call_target="tpu_custom_call" | custom-call | flops 12079595520 | bytes 31457280 | tf_op jit(solution)/shard_map/attention_forward/pallas_call | solution.py:53
  60.7 4.0 %collective-permute-done.7.refs_4_ = bf16[512,768]{1,0:T(8,128)(2,1)} collective-permute-done((bf16[512,768]{1,0:T(8,128)(2,1)}, bf16[512,768]{1,0:T(8,128)(2,1)}, u32[]{:S(2)}, u32[]{:S(2)}) %collective-permute-start.7) | collective-permute-done | bytes 786464 | tf_op jit(solution)/shard_map/ppermute | solution.py:441
  66.4 20.8 %experts.1 = (f32[512,768]{1,0:T(8,128)}, bf16[512,768]{1,0:T(8,128)(2,1)}, f32[512,768]{1,0:T(8,128)}, bf16[512,768]{1,0:T(8,128)(2,1)}, f32[512,128]{1,0:T(8,1...) custom-call(s32[10,4]{1,0:T(8,128)} %concatenate.28.refs_0_.refs_1_,, ...), custom_call_target="tpu_custom_call" | custom-call | flops 12079595520 | bytes 31457280 | tf_op jit(solution)/shard_map/experts/pallas_call | solution.py:404
  92.9 15.6 %experts_and_grads.2 = (f32[512,768]{1,0:T(8,128)}, bf16[512,768]{1,0:T(8,128)(2,1)}, f32[512,768]{1,0:T(8,128)}, bf16[512,768]{1,0:T(8,128)(2,1)}, f32[512,128]...) custom-call(s32[10,4]{1,0:T(8,128)} %concatenate.29.refs_0_, ...), custom_call_target="tpu_custom_call" | custom-call | flops 6039797760 | bytes 31457280 | tf_op jit(solution)/shard_map/experts_and_grads/pallas_call | solution.py:404
  108.5 3.2 dynamic-slice_bitcast_fusion.7
  111.7 23.1 %experts_and_grads.3 = (f32[512,768]{1,0:T(8,128)}, bf16[512,768]{1,0:T(8,128)(2,1)}, f32[512,768]{1,0:T(8,128)}, bf16[512,768]{1,0:T(8,128)(2,1)}, f32[512,128]...) custom-call(s32[10,4]{1,0:T(8,128)} %concatenate.29.refs_0_, ...), custom_call_target="tpu_custom_call" | custom-call | flops 6039797760 | bytes 31457280 | tf_op jit(solution)/shard_map/experts_and_grads/pallas_call | solution.py:404
  137.6 3.2 collective-permute-start.16
  150.3 14.7 %collective-permute-done.11 = bf16[512,768]{1,0:T(8,128)(2,1)S(1)} collective-permute-done((bf16[512,768]{1,0:T(8,128)(2,1)S(1)}, bf16[512,768]{1,0:T(8,128)(2,1)S(1)}, u32[]{:S(2)}, u32[]{:S(2)}) %collective-permute-start.11) | collective-permute-done | bytes 786464 | tf_op jit(solution)/shard_map/ppermute | solution.py:441
  181.2 12.7 %attention_backward.2 = (bf16[3,192,1024]{2,1,0:T(8,128)(2,1)S(1)}, f32[3,1,2048]{2,1,0:T(1,128)S(1)}) custom-call(s32[1]{0:T(128)} %bitcast.seq_ref, bf16[3,192,2048]{2,1,0:T(8,128)(2,1)S(1)} %convert_bitcast_fusion.qkv_ref, bf16[192,1024]{1,0:T(8,128)(2,1)S(1)} %fusion.20.grad_ref, f32[3,1,1024]{2,1,0:T(1,128)S(1)} %get-tuple-element.139.lse_ref, ...), custom_call_target="tpu_custom_call" | custom-call | flops 14092861440 | bytes 41943040 | tf_op jit(solution)/shard_map/attention_backward/pallas_call | solution.py:129
  194.1 6.6 %collective-permute-done.22 = bf16[2,4,96,768]{3,2,1,0:T(8,128)(2,1)S(1)} collective-permute-done((bf16[2,4,96,768]{3,2,1,0:T(8,128)(2,1)}, bf16[2,4,96,768]{3,2,1,0:T(8,128)(2,1)S(1)}, u32[]{:S(2)}, u32[]{:S(2)}) %collective-permute-start.22) | collective-permute-done | bytes 1179680 | tf_op jit(solution)/shard_map/ppermute | solution.py:441
  202.3 4.8 %collective-permute-start.41 = (bf16[2,1,96,768]{3,2,1,0:T(8,128)(2,1)}, bf16[2,1,96,768]{3,2,1,0:T(8,128)(2,1)}, u32[]{:S(2)}, u32[]{:S(2)}) collective-permute-start(bf16[2,1,96,768]{3,2,1,0:T(8,128)(2,1)} %dynamic-slice_convert_fusion.6), channel_id=1, source_target_pairs={{0,16},{4,20},{8,24},{12,28},{16,0},{20,4},{24,8},{28,12},{1,17},{... | collective-permute-start | bytes 884744 | tf_op jit(solution)/shard_map/ppermute | solution.py:441
  213.8 12.5 %attention_backward.3 = (bf16[3,192,1024]{2,1,0:T(8,128)(2,1)S(1)}, f32[3,1,2048]{2,1,0:T(1,128)S(1)}) custom-call(s32[1]{0:T(128)S(6)} %sub.150.seq_ref, bf16[3,192,2048]{2,1,0:T(8,128)(2,1)S(1)} %convert_bitcast_fusion.qkv_ref, bf16[192,1024]{1,0:T(8,128)(2,1)S(1)} %fusion.21.grad_ref, f32[3,1,1024]{2,1,0:T(1,128)S(1)} %get-tuple-element.155.lse_ref, ...), custom_call_target="tpu_custom_call" | custom-call | flops 14092861440 | bytes 41943040 | tf_op jit(solution)/shard_map/attention_backward/pallas_call | solution.py:129
  247.8 6.6 %reshape.418 = f32[4,4,2,96,192]{3,2,1,4,0:T(2,128)} reshape(f32[4,768,192]{1,2,0:T(8,128)} %pad_maximum_fusion) | data formatting | bytes 4718592 | tf_op jit(solution)/shard_map/reshape | solution.py:465
  254.4 3.3 constant_dynamic-slice_fusion.9
  257.7 3.5 copy.80
  261.8 3.1 fusion.35
  277.2 15.2 %collective-permute-done.30 = f32[40,128]{1,0:T(8,128)S(1)} collective-permute-done((f32[40,128]{1,0:T(8,128)S(1)}, f32[40,128]{1,0:T(8,128)S(1)}, u32[]{:S(2)}, u32[]{:S(2)}) %collective-permute-start.30) | collective-permute-done | bytes 20512 | tf_op jit(solution)/shard_map/ppermute | solution.py:441
  304.8 4.8 %copy.72 = f32[4,4,1,96,192]{4,3,1,0,2:T(8,128)S(1)} copy(f32[4,4,1,96,192]{3,2,1,4,0:T(1,128)} %constant_dynamic-slice_fusion.8) | data formatting | bytes 2359296 | tf_op jit(solution)/shard_map/jit(dynamic_index_in_dim)/dynamic_slice | solution.py:467
  321.2 12.8 %collective-permute-done.34 = bf16[4,4,96,192]{3,2,1,0:T(8,128)(2,1)S(1)} collective-permute-done((bf16[4,4,96,192]{3,2,1,0:T(8,128)(2,1)}, bf16[4,4,96,192]{3,2,1,0:T(8,128)(2,1)S(1)}, u32[]{:S(2)}, u32[]{:S(2)}) %collective-permute-start.34) | collective-permute-done | bytes 589856 | tf_op jit(solution)/shard_map/ppermute | solution.py:441
  340.5 7.4 %collective-permute-done.35 = bf16[4,2,96,192]{3,2,1,0:T(8,128)(2,1)S(1)} collective-permute-done((bf16[4,2,96,192]{3,2,1,0:T(8,128)(2,1)S(1)}, bf16[4,2,96,192]{3,2,1,0:T(8,128)(2,1)S(1)}, u32[]{:S(2)}, u32[]{:S(2)}) %collective-permute-start.35) | collective-permute-done | bytes 294944 | tf_op jit(solution)/shard_map/ppermute | solution.py:441
  349.5 9.4 %collective-permute-done.36 = bf16[4,1,96,192]{3,2,1,0:T(8,128)(2,1)S(1)} collective-permute-done((bf16[4,1,96,192]{3,2,1,0:T(8,128)(2,1)S(1)}, bf16[4,1,96,192]{3,2,1,0:T(8,128)(2,1)S(1)}, u32[]{:S(2)}, u32[]{:S(2)}) %collective-permute-start.36) | collective-permute-done | bytes 147488 | tf_op jit(solution)/shard_map/ppermute | solution.py:441
  360.3 6.2 %collective-permute-done.39 = bf16[2,2,96,768]{3,2,0,1:T(8,128)(2,1)S(1)} collective-permute-done((bf16[2,2,96,768]{3,2,0,1:T(8,128)(2,1)S(1)}, bf16[2,2,96,768]{3,2,0,1:T(8,128)(2,1)S(1)}, u32[]{:S(2)}, u32[]{:S(2)}) %collective-permute-start.39) | collective-permute-done | bytes 589856 | tf_op jit(solution)/shard_map/ppermute | solution.py:441
  369.8 11.2 %collective-permute-done.40 = bf16[2,1,96,768]{3,2,0,1:T(8,128)(2,1)S(1)} collective-permute-done((bf16[2,1,96,768]{3,2,0,1:T(8,128)(2,1)S(1)}, bf16[2,1,96,768]{3,2,0,1:T(8,128)(2,1)S(1)}, u32[]{:S(2)}, u32[]{:S(2)}) %collective-permute-start.40) | collective-permute-done | bytes 294944 | tf_op jit(solution)/shard_map/ppermute | solution.py:441
  (359 shorter events, 154.1 us)
Async XLA Ops:
  26.7 21.1 %collective-permute-start.2 = (bf16[512,768]{1,0:T(8,128)(2,1)}, bf16[512,768]{1,0:T(8,128)(2,1)}, u32[]{:S(2)}, u32[]{:S(2)}) collective-permute-start(bf16[512,768]{1,0:T(8,128)(2,1)} %add_convert_fusion.4), channel_id=1, source_target_pairs={{0,2},{1,3},{2,0},{3,1},{4,6},{5,7},{6,4},{7,5},{8,10},{9,11},{10,... | collective-permute-start | bytes 2359304 | tf_op jit(solution)/shard_map/ppermute | solution.py:441
  44.4 20.3 %collective-permute-start.7 = (bf16[512,768]{1,0:T(8,128)(2,1)}, bf16[512,768]{1,0:T(8,128)(2,1)}, u32[]{:S(2)}, u32[]{:S(2)}) collective-permute-start(bf16[512,768]{1,0:T(8,128)(2,1)} %convolution_convert_fusion.2.refs_3_), channel_id=1, source_target_pairs={{0,2},{1,3},{2,0},{3,1},{4,6},{5,7},{6,4},{7,5},{8,10},{9,11},{10,... | collective-permute-start | bytes 2359304 | tf_op jit(solution)/shard_map/ppermute | solution.py:441
  44.5 21.9 %collective-permute-start.4 = (bf16[512,768]{1,0:T(8,128)(2,1)}, bf16[512,768]{1,0:T(8,128)(2,1)}, u32[]{:S(2)}, u32[]{:S(2)}) collective-permute-start(bf16[512,768]{1,0:T(8,128)(2,1)} %convolution_convert_fusion.2.refs_3_), channel_id=1, source_target_pairs={{0,1},{1,0},{2,3},{3,2},{4,5},{5,4},{6,7},{7,6},{8,9},{9,8},{10,11... | collective-permute-start | bytes 2359304 | tf_op jit(solution)/shard_map/ppermute | solution.py:441
  64.6 28.2 %collective-permute-start.8 = (bf16[512,768]{1,0:T(8,128)(2,1)}, bf16[512,768]{1,0:T(8,128)(2,1)}, u32[]{:S(2)}, u32[]{:S(2)}) collective-permute-start(bf16[512,768]{1,0:T(8,128)(2,1)} %collective-permute-done.7.refs_4_), channel_id=1, source_target_pairs={{0,1},{1,0},{2,3},{3,2},{4,5},{5,4},{6,7},{7,6},{8,9},{9,8},{10,11... | collective-permute-start | bytes 2359304 | tf_op jit(solution)/shard_map/ppermute | solution.py:441
  64.6 22.6 %collective-permute-start.5 = (bf16[512,768]{1,0:T(8,128)(2,1)}, bf16[512,768]{1,0:T(8,128)(2,1)}, u32[]{:S(2)}, u32[]{:S(2)}) collective-permute-start(bf16[512,768]{1,0:T(8,128)(2,1)} %convolution_convert_fusion.3.refs_1_), channel_id=1, source_target_pairs={{0,2},{1,3},{2,0},{3,1},{4,6},{5,7},{6,4},{7,5},{8,10},{9,11},{10,... | collective-permute-start | bytes 2359304 | tf_op jit(solution)/shard_map/ppermute | solution.py:441
  137.2 27.8 %collective-permute-start.9 = (bf16[512,768]{1,0:T(8,128)(2,1)S(1)}, bf16[512,768]{1,0:T(8,128)(2,1)S(1)}, u32[]{:S(2)}, u32[]{:S(2)}) collective-permute-start(bf16[512,768]{1,0:T(8,128)(2,1)S(1)} %copy-done.66), channel_id=1, source_target_pairs={{0,1},{1,0},{2,3},{3,2},{4,5},{5,4},{6,7},{7,6},{8,9},{9,8},{10,11... | collective-permute-start | bytes 2359304 | tf_op jit(solution)/shard_map/ppermute | solution.py:441
  137.6 35.3 %collective-permute-start.16 = (bf16[2,4,96,768]{3,2,1,0:T(8,128)(2,1)}, bf16[2,4,96,768]{3,2,1,0:T(8,128)(2,1)}, u32[]{:S(2)}, u32[]{:S(2)}) collective-permute-start(bf16[2,4,96,768]{3,2,1,0:T(8,128)(2,1)} %get-tuple-element.254), channel_id=1, source_target_pairs={{0,4},{4,0},{8,12},{12,8},{16,20},{20,16},{24,28},{28,24},{1,5},{5... | collective-permute-start | bytes 3538952 | tf_op jit(solution)/shard_map/ppermute | solution.py:441
  145.7 19.3 %collective-permute-start.11 = (bf16[512,768]{1,0:T(8,128)(2,1)S(1)}, bf16[512,768]{1,0:T(8,128)(2,1)S(1)}, u32[]{:S(2)}, u32[]{:S(2)}) collective-permute-start(bf16[512,768]{1,0:T(8,128)(2,1)S(1)} %add_convert_fusion.2), channel_id=1, source_target_pairs={{0,2},{1,3},{2,0},{3,1},{4,6},{5,7},{6,4},{7,5},{8,10},{9,11},{10,... | collective-permute-start | bytes 2359304 | tf_op jit(solution)/shard_map/ppermute | solution.py:441
  171.6 29.1 %collective-permute-start.22 = (bf16[2,4,96,768]{3,2,1,0:T(8,128)(2,1)}, bf16[2,4,96,768]{3,2,1,0:T(8,128)(2,1)S(1)}, u32[]{:S(2)}, u32[]{:S(2)}) collective-permute-start(bf16[2,4,96,768]{3,2,1,0:T(8,128)(2,1)} %get-tuple-element.252), channel_id=1, source_target_pairs={{0,4},{4,0},{8,12},{12,8},{16,20},{20,16},{24,28},{28,24},{1,5},{5... | collective-permute-start | bytes 3538952 | tf_op jit(solution)/shard_map/ppermute | solution.py:441
  172.2 28.5 %collective-permute-start.20 = (bf16[512,768]{1,0:T(8,128)(2,1)}, bf16[512,768]{1,0:T(8,128)(2,1)S(1)}, u32[]{:S(2)}, u32[]{:S(2)}) collective-permute-start(bf16[512,768]{1,0:T(8,128)(2,1)} %fusion.90), channel_id=1, source_target_pairs={{0,2},{1,3},{2,0},{3,1},{4,6},{5,7},{6,4},{7,5},{8,10},{9,11},{10,... | collective-permute-start | bytes 2359304 | tf_op jit(solution)/shard_map/ppermute | solution.py:441
  175.0 19.0 %collective-permute-start.23 = (bf16[2,2,96,768]{3,2,1,0:T(8,128)(2,1)S(1)}, bf16[2,2,96,768]{3,2,1,0:T(8,128)(2,1)S(1)}, u32[]{:S(2)}, u32[]{:S(2)}) collective-permute-start(bf16[2,2,96,768]{3,2,1,0:T(8,128)(2,1)S(1)} %fusion.30), channel_id=1, source_target_pairs={{0,8},{4,12},{8,0},{12,4},{16,24},{20,28},{24,16},{28,20},{1,9},{5... | collective-permute-start | bytes 1769480 | tf_op jit(solution)/shard_map/ppermute | solution.py:441
  176.9 64.1 %collective-permute-start.27 = (bf16[2,4,96,768]{3,2,1,0:T(8,128)(2,1)}, bf16[2,4,96,768]{3,2,1,0:T(8,128)(2,1)}, u32[]{:S(2)}, u32[]{:S(2)}) collective-permute-start(bf16[2,4,96,768]{3,2,1,0:T(8,128)(2,1)} %get-tuple-element.250), channel_id=1, source_target_pairs={{0,4},{4,0},{8,12},{12,8},{16,20},{20,16},{24,28},{28,24},{1,5},{5... | collective-permute-start | bytes 3538952 | tf_op jit(solution)/shard_map/ppermute | solution.py:441
  202.3 72.9 %collective-permute-start.41 = (bf16[2,1,96,768]{3,2,1,0:T(8,128)(2,1)}, bf16[2,1,96,768]{3,2,1,0:T(8,128)(2,1)}, u32[]{:S(2)}, u32[]{:S(2)}) collective-permute-start(bf16[2,1,96,768]{3,2,1,0:T(8,128)(2,1)} %dynamic-slice_convert_fusion.6), channel_id=1, source_target_pairs={{0,16},{4,20},{8,24},{12,28},{16,0},{20,4},{24,8},{28,12},{1,17},{... | collective-permute-start | bytes 884744 | tf_op jit(solution)/shard_map/ppermute | solution.py:441
  207.9 30.8 %collective-permute-start.28 = (bf16[2,2,96,768]{3,2,1,0:T(8,128)(2,1)}, bf16[2,2,96,768]{3,2,1,0:T(8,128)(2,1)}, u32[]{:S(2)}, u32[]{:S(2)}) collective-permute-start(bf16[2,2,96,768]{3,2,1,0:T(8,128)(2,1)} %fusion.31), channel_id=1, source_target_pairs={{0,8},{4,12},{8,0},{12,4},{16,24},{20,28},{24,16},{28,20},{1,9},{5... | collective-permute-start | bytes 1769480 | tf_op jit(solution)/shard_map/ppermute | solution.py:441
  212.3 27.9 %collective-permute-start.19 = (bf16[512,768]{1,0:T(8,128)(2,1)}, bf16[512,768]{1,0:T(8,128)(2,1)}, u32[]{:S(2)}, u32[]{:S(2)}) collective-permute-start(bf16[512,768]{1,0:T(8,128)(2,1)} %add_convert_fusion.1), channel_id=1, source_target_pairs={{0,2},{1,3},{2,0},{3,1},{4,6},{5,7},{6,4},{7,5},{8,10},{9,11},{10,... | collective-permute-start | bytes 2359304 | tf_op jit(solution)/shard_map/ppermute | solution.py:441
  235.4 99.0 %collective-permute-start.38 = (bf16[2,4,96,768]{3,2,1,0:T(8,128)(2,1)}, bf16[2,4,96,768]{3,2,1,0:T(8,128)(2,1)}, u32[]{:S(2)}, u32[]{:S(2)}) collective-permute-start(bf16[2,4,96,768]{3,2,1,0:T(8,128)(2,1)} %get-tuple-element.248), channel_id=1, source_target_pairs={{0,4},{4,0},{8,12},{12,8},{16,20},{20,16},{24,28},{28,24},{1,5},{5... | collective-permute-start | bytes 3538952 | tf_op jit(solution)/shard_map/ppermute | solution.py:441
  238.8 26.2 %collective-permute-start.17 = (bf16[512,768]{1,0:T(8,128)(2,1)}, bf16[512,768]{1,0:T(8,128)(2,1)}, u32[]{:S(2)}, u32[]{:S(2)}) collective-permute-start(bf16[512,768]{1,0:T(8,128)(2,1)} %get-tuple-element.142), channel_id=1, source_target_pairs={{0,1},{1,0},{2,3},{3,2},{4,5},{5,4},{6,7},{7,6},{8,9},{9,8},{10,11... | collective-permute-start | bytes 2359304 | tf_op jit(solution)/shard_map/ppermute | solution.py:441
  241.0 72.9 %collective-permute-start.37 = (bf16[2,1,96,768]{3,2,1,0:T(8,128)(2,1)}, bf16[2,1,96,768]{3,2,1,0:T(8,128)(2,1)}, u32[]{:S(2)}, u32[]{:S(2)}) collective-permute-start(bf16[2,1,96,768]{3,2,1,0:T(8,128)(2,1)} %dynamic-slice_convert_fusion.5), channel_id=1, source_target_pairs={{0,16},{4,20},{8,24},{12,28},{16,0},{20,4},{24,8},{28,12},{1,17},{... | collective-permute-start | bytes 884744 | tf_op jit(solution)/shard_map/ppermute | solution.py:441
  272.1 46.2 %collective-permute-start.26 = (bf16[512,768]{1,0:T(8,128)(2,1)}, bf16[512,768]{1,0:T(8,128)(2,1)}, u32[]{:S(2)}, u32[]{:S(2)}) collective-permute-start(bf16[512,768]{1,0:T(8,128)(2,1)} %fusion.14), channel_id=1, source_target_pairs={{0,2},{1,3},{2,0},{3,1},{4,6},{5,7},{6,4},{7,5},{8,10},{9,11},{10,... | collective-permute-start | bytes 2359304 | tf_op jit(solution)/shard_map/ppermute | solution.py:441
  273.5 18.9 %collective-permute-start.30 = (f32[40,128]{1,0:T(8,128)S(1)}, f32[40,128]{1,0:T(8,128)S(1)}, u32[]{:S(2)}, u32[]{:S(2)}) collective-permute-start(f32[40,128]{1,0:T(8,128)S(1)} %add.464), channel_id=1, source_target_pairs={{0,2},{1,3},{2,0},{3,1},{4,6},{5,7},{6,4},{7,5},{8,10},{9,11},{10,... | collective-permute-start | bytes 61448 | tf_op jit(solution)/shard_map/ppermute | solution.py:441
  275.2 41.5 %collective-permute-start.42 = (bf16[2,2,96,768]{3,2,0,1:T(8,128)(2,1)}, bf16[2,2,96,768]{3,2,0,1:T(8,128)(2,1)}, u32[]{:S(2)}, u32[]{:S(2)}) collective-permute-start(bf16[2,2,96,768]{3,2,0,1:T(8,128)(2,1)} %fusion.32), channel_id=1, source_target_pairs={{0,8},{4,12},{8,0},{12,4},{16,24},{20,28},{24,16},{28,20},{1,9},{5... | collective-permute-start | bytes 1769480 | tf_op jit(solution)/shard_map/ppermute | solution.py:441
  313.9 20.1 %collective-permute-start.34 = (bf16[4,4,96,192]{3,2,1,0:T(8,128)(2,1)}, bf16[4,4,96,192]{3,2,1,0:T(8,128)(2,1)S(1)}, u32[]{:S(2)}, u32[]{:S(2)}) collective-permute-start(bf16[4,4,96,192]{3,2,1,0:T(8,128)(2,1)} %bitcast.177), channel_id=1, source_target_pairs={{0,4},{4,0},{8,12},{12,8},{16,20},{20,16},{24,28},{28,24},{1,5},{5... | collective-permute-start | bytes 1769480 | tf_op jit(solution)/shard_map/ppermute | solution.py:441
  318.0 48.8 %collective-permute-start.43 = (bf16[2,1,96,768]{3,2,0,1:T(8,128)(2,1)S(1)}, bf16[2,1,96,768]{3,2,0,1:T(8,128)(2,1)S(1)}, u32[]{:S(2)}, u32[]{:S(2)}) collective-permute-start(bf16[2,1,96,768]{3,2,0,1:T(8,128)(2,1)S(1)} %dynamic-slice_convert_fusion.3), channel_id=1, source_target_pairs={{0,16},{4,20},{8,24},{12,28},{16,0},{20,4},{24,8},{28,12},{1,17},{... | collective-permute-start | bytes 884744 | tf_op jit(solution)/shard_map/ppermute | solution.py:441
  348.4 18.1 %collective-permute-start.39 = (bf16[2,2,96,768]{3,2,0,1:T(8,128)(2,1)S(1)}, bf16[2,2,96,768]{3,2,0,1:T(8,128)(2,1)S(1)}, u32[]{:S(2)}, u32[]{:S(2)}) collective-permute-start(bf16[2,2,96,768]{3,2,0,1:T(8,128)(2,1)S(1)} %fusion.33), channel_id=1, source_target_pairs={{0,8},{4,12},{8,0},{12,4},{16,24},{20,28},{24,16},{28,20},{1,9},{5... | collective-permute-start | bytes 1769480 | tf_op jit(solution)/shard_map/ppermute | solution.py:441
  (88 other events, 509.6 us)

commit v2 on v1

--- a/solution.py
+++ b/solution.py
@@ -70,11 +70,7 @@
             jax.ShapeDtypeStruct((heads, 1, seq_len), jnp.float32),
         ],
         compiler_params=pltpu.CompilerParams(vmem_limit_bytes=48 * 2**20),
-        cost_estimate=pl.CostEstimate(
-            flops=60 * heads * seq_len * seq_len * size,
-            bytes_accessed=30 * 2**20,
-            transcendentals=heads * seq_len * seq_len,
-        ),
+        cost_estimate=pl.CostEstimate(flops=1, bytes_accessed=1, transcendentals=0),
         name="attention_forward",
     )(seq, qkv, offsets)
 
@@ -153,11 +149,7 @@
             jax.ShapeDtypeStruct((heads, 1, 2 * seq_len), jnp.float32),
         ],
         compiler_params=pltpu.CompilerParams(vmem_limit_bytes=48 * 2**20),
-        cost_estimate=pl.CostEstimate(
-            flops=70 * heads * seq_len * seq_len * size,
-            bytes_accessed=40 * 2**20,
-            transcendentals=heads * seq_len * seq_len,
-        ),
+        cost_estimate=pl.CostEstimate(flops=1, bytes_accessed=1, transcendentals=0),
         name="attention_backward",
     )(seq, qkv, grads, lse, offsets)
 
@@ -247,10 +239,23 @@
         filled = filled + chunks
 
 
-def expert_kernel(*refs, shares, first_expert, expert_count, with_grads):
+def store_parts(outs, values, side, bit, piece):
+    if len(outs) == 1:
+        outs[0][0] = values[...].astype(jnp.bfloat16)
+        return
+    for index in range(values.shape[0] // (2 * piece)):
+        low, high = index % bit, index // bit
+        for which, out in enumerate(outs):
+            chosen = side if which == 0 else 1 - side
+            start = ((high * 2 + chosen) * bit + low) * piece
+            rows = values[pl.ds(pl.multiple_of(start, CH), piece)]
+            out[0, index] = rows.astype(jnp.bfloat16)
+
+
+def expert_kernel(*refs, shares, first_expert, expert_count, with_grads, bits, piece):
     plan_ref, refs = refs[0], refs[1:]
     if with_grads:
-        past_plan, refs = refs[0], refs[1:]
+        past_plan, side_ref, refs = refs[0], refs[1], refs[2:]
     x_refs, refs = refs[:shares], refs[shares:]
     c_refs, refs = refs[:shares], refs[shares:]
     router_ref, up_ref, down_ref, *refs = refs
@@ -260,11 +265,15 @@
     back_refs, refs = refs[:shares], refs[shares:]
     gate_refs, refs = refs[:shares], refs[shares:]
     if with_grads:
-        up_out, down_out, *refs = refs
-        xs, ms, dys, dus, cs, ybuf, bbuf, gbuf, *refs = refs
+        parts = 2 if bits else 1
+        up_outs, refs = refs[:parts], refs[parts:]
+        down_outs, refs = refs[:parts], refs[parts:]
+        xs, ms, dys, dus, *refs = refs
+        cs, ybuf, bbuf, gbuf, *refs = refs
+        gates, refs = refs[:shares], refs[shares:]
         old, up_acc, down_acc, sems = refs[:4], refs[4], refs[5], refs[6]
     else:
-        xs, ms, dys, dus, cs, ybuf, bbuf, gbuf = refs
+        xs, ms, dys, dus, cs, ybuf, bbuf, gbuf, *gates = refs
     step = pl.program_id(0)
     expert = step + first_expert
     units = plan_ref[4 * shares, expert]
@@ -272,7 +281,7 @@
 
     @pl.when(step == 0)
     def _():
-        for out in (*y_refs, *back_refs, *gate_refs):
+        for out in (*y_refs, *back_refs, *gates):
             out[...] = jnp.zeros_like(out)
 
     if with_grads:
@@ -334,8 +343,13 @@
 
     for_units(units, tile)
     scatter_rows(
-        plan_ref, expert, shares, (ybuf, bbuf, gbuf), (y_refs, back_refs, gate_refs)
-    )
+        plan_ref, expert, shares, (ybuf, bbuf, gbuf), (y_refs, back_refs, gates)
+    )
+
+    @pl.when(step == pl.num_programs(0) - 1)
+    def _():
+        for gate, out in zip(gates, gate_refs):
+            out[...] = gate[...].T[:1]
 
     if with_grads:
         up_acc[...] = jnp.zeros_like(up_acc)
@@ -353,8 +367,9 @@
         for_units(units, add((xs, ms, dys, dus)))
         lax.fori_loop(0, past_units, finish, 0)
         for_units(past_units, add(old))
-        up_out[0] = up_acc[...].astype(jnp.bfloat16)
-        down_out[0] = down_acc[...].astype(jnp.bfloat16)
+        up_bit, down_bit = bits or (0, 0)
+        store_parts(up_outs, up_acc, side_ref[0], up_bit, piece)
+        store_parts(down_outs, down_acc, side_ref[1], down_bit, piece)
 
 
 def run_experts(plan, x, c, router, up, down, past=None, first_expert=0, step_count=None):
@@ -373,23 +388,27 @@
     in_specs = [whole((rows, width))] * (2 * shares) + [whole(router.shape), block, block]
     row_types = [full] + [brain] * (shares - 1)
     out_shape = [jax.ShapeDtypeStruct((rows, width), kind) for kind in row_types * 2]
-    out_specs = [whole((rows, width))] * (2 * shares) + [whole((rows, 128))] * shares
-    out_shape += [jax.ShapeDtypeStruct((rows, 128), full)] * shares
+    out_specs = [whole((rows, width))] * (2 * shares) + [whole((1, rows))] * shares
+    out_shape += [jax.ShapeDtypeStruct((1, rows), full)] * shares
     scratch = [
         pltpu.VMEM((most, width), brain),
         pltpu.VMEM((most, width), full),
         pltpu.VMEM((most, width), full),
         pltpu.VMEM((most, 128), full),
-    ]
+    ] + [pltpu.VMEM((rows, 128), full)] * shares
     widths = (width, hidden, width, hidden)
     if with_grads:
-        past_plan, past_arrays = past
-        scalars.append(past_plan)
+        past_plan, past_arrays, sides, bits, piece = past
+        scalars += [past_plan, sides]
         inputs += past_arrays
         in_specs += [pl.BlockSpec(memory_space=pl.ANY)] * 4
-        grad_block = pl.BlockSpec((1, width, hidden), lambda e, *p: (e, 0, 0))
-        out_specs += [grad_block, grad_block]
-        out_shape += [jax.ShapeDtypeStruct((steps, width, hidden), brain)] * 2
+        if bits:
+            shape = (width // (2 * piece), piece, hidden)
+            out_specs += [pl.BlockSpec((1, *shape), lambda e, *p: (e, 0, 0, 0))] * 4
+            out_shape += [jax.ShapeDtypeStruct((steps, *shape), brain)] * 4
+        else:
+            out_specs += [pl.BlockSpec((1, width, hidden), lambda e, *p: (e, 0, 0))] * 2
+            out_shape += [jax.ShapeDtypeStruct((steps, width, hidden), brain)] * 2
         buffers = [pltpu.VMEM((most, size), brain) for size in widths]
         scratch = (
             buffers
@@ -408,6 +427,8 @@
             first_expert=first_expert,
             expert_count=experts,
             with_grads=with_grads,
+            bits=bits if with_grads else None,
+            piece=piece if with_grads else None,
         ),
         grid_spec=pltpu.PrefetchScalarGridSpec(
             num_scalar_prefetch=len(scalars),
@@ -418,13 +439,80 @@
         ),
         out_shape=out_shape,
         compiler_params=pltpu.CompilerParams(vmem_limit_bytes=58 * 2**20),
-        cost_estimate=pl.CostEstimate(
-            flops=20 * rows * shares * width * hidden * steps // experts,
-            bytes_accessed=30 * 2**20,
-            transcendentals=0,
-        ),
+        cost_estimate=pl.CostEstimate(flops=1, bytes_accessed=1, transcendentals=0),
         name="experts_and_grads" if with_grads else "experts",
     )(*scalars, *inputs)
+
+
+def input_kernel(core_ref, grad_ref, weight_ref, keep_ref, send_ref):
+    share = keep_ref.shape[0]
+    for target, out in ((core_ref[0], keep_ref), (1 - core_ref[0], send_ref)):
+        here = pl.ds(pl.multiple_of(target * share, share), share)
+        total = sum(
+            mm(grad_ref[which, :, here].T, weight_ref[which], ((1,), (1,))) for which in range(3)
+        )
+        out[...] = total.astype(out.dtype)
+
+
+def input_grads(core, qkv_rows, qkv_weight):
+    share = qkv_rows.shape[2] // 2
+    width = qkv_weight.shape[1]
+    vmem = pl.BlockSpec(memory_space=pltpu.VMEM)
+    return pl.pallas_call(
+        input_kernel,
+        in_specs=[pl.BlockSpec(memory_space=pltpu.SMEM), vmem, vmem],
+        out_specs=[vmem, vmem],
+        out_shape=[
+            jax.ShapeDtypeStruct((share, width), jnp.float32),
+            jax.ShapeDtypeStruct((share, width), jnp.bfloat16),
+        ],
+        compiler_params=pltpu.CompilerParams(vmem_limit_bytes=40 * 2**20),
+        name="input_grads",
+    )(core, qkv_rows, qkv_weight)
+
+
+def projection_kernel(*refs):
+    _, _, *refs = refs
+    (rows_a, rows_b, grad_a, grad_b, out_a, out_b, mixed_a, mixed_b, weight, total, gain) = refs
+    gain_total = jnp.zeros(gain.shape, jnp.float32)
+    for which in range(3):
+        part = mm(grad_a[which], rows_a[...], ((1,), (0,)))
+        part = part + mm(grad_b[which], rows_b[...], ((1,), (0,)))
+        total[which] = part.T.astype(jnp.bfloat16)
+        turned = weight[which].astype(jnp.float32).T
+        gain_total = gain_total + jnp.sum(turned * part, axis=0, keepdims=True)
+    part = mm(mixed_a[...], out_a[...], ((1,), (0,))) + mm(mixed_b[...], out_b[...], ((1,), (0,)))
+    total[3] = part.T.astype(jnp.bfloat16)
+    gain[...] = gain_total
+
+
+def projection_grads(seqs, normed, qkv_rows, out_rows, mixed, qkv_weight):
+    _, size, seq_len = qkv_rows[0].shape
+    width = normed.shape[1]
+    whole = lambda array: pl.BlockSpec(array.shape, lambda i, a, b: (0,) * array.ndim)
+    operands = [normed, normed, *qkv_rows, *out_rows, *mixed, qkv_weight]
+    in_specs = [
+        pl.BlockSpec((seq_len, width), lambda i, a, b: (a[0], 0)),
+        pl.BlockSpec((seq_len, width), lambda i, a, b: (b[0], 0)),
+    ] + [whole(array) for array in operands[2:]]
+    return pl.pallas_call(
+        projection_kernel,
+        grid_spec=pltpu.PrefetchScalarGridSpec(
+            num_scalar_prefetch=2,
+            grid=(1,),
+            in_specs=in_specs,
+            out_specs=[
+                pl.BlockSpec((4, width, size), lambda i, a, b: (0, 0, 0)),
+                pl.BlockSpec((1, width), lambda i, a, b: (0, 0)),
+            ],
+        ),
+        out_shape=[
+            jax.ShapeDtypeStruct((4, width, size), jnp.bfloat16),
+            jax.ShapeDtypeStruct((1, width), jnp.float32),
+        ],
+        compiler_params=pltpu.CompilerParams(vmem_limit_bytes=56 * 2**20),
+        name="projection_grads",
+    )(*seqs, *operands)
 
 
 EPS = 1e-06
@@ -445,35 +533,65 @@
     return lax.optimization_barrier((value, milestones))[0]
 
 
+def join(values, *moving):
+    values, landed = lax.optimization_barrier((values, tuple(move.moving for move in moving)))
+    for move, received in zip(moving, landed):
+        move.moving = received
+    return values
+
+
+class Transfer:
+    def __init__(self, values, axis, bit):
+        self.moving = swap(values, axis, bit)
+
+
 class ScatterSum:
-    def __init__(self, values):
-        self.values = values
-        self.bit = 1
-        self.count = lax.axis_size("dp")
-        self.piece = values.shape[1] // self.count
+    def __init__(self, parts, bits):
+        self.bits = list(bits)
+        self.left = sorted(bits, reverse=True)
         self.moving = None
-
-    def start(self, *milestones):
+        self.parts = None
+        experts, width = parts[0].shape[0], parts[0].shape[-1]
+        sizes = [2] * len(self.bits)
+        if len(parts) == 1:
+            values = parts[0]
+            self.values = values.reshape(experts, *sizes, values.shape[1] >> len(sizes), width)
+        else:
+            self.parts = parts
+            self.shape = (experts, *sizes[1:], parts[0].shape[-2], width)
+
+    def pick(self, other):
+        mine = (lax.axis_index("dp") // self.bit) % 2
+        index = 1 - mine if other else mine
+        return lax.dynamic_index_in_dim(self.values, index, self.spot, keepdims=False)
+
+    def land(self):
+        keep = self.parts[0] if self.parts else self.pick(False)
+        self.values = keep.astype(F32) + self.moving.astype(F32)
+        if self.parts:
+            self.values = self.values.reshape(self.shape)
+        self.parts = None
+        self.moving = None
+        self.left.remove(self.bit)
+
+    def launch(self, *milestones):
         if self.moving is not None:
-            keep, received = after((self.keep, self.moving), *milestones)
-            self.values = keep.astype(F32) + received.astype(F32)
-            self.moving = None
-        if self.bit >= self.count:
+            self.land()
+        if not self.bits:
             return
-        experts, width = self.values.shape[0], self.values.shape[-1]
-        shape = (experts, self.count // (2 * self.bit), 2, self.piece, width)
-        values = after(self.values, *milestones).reshape(shape)
-        mine = (lax.axis_index("dp") // self.bit) % 2
-        self.keep = lax.dynamic_index_in_dim(values, mine, 2, keepdims=False)
-        send = lax.dynamic_index_in_dim(values, 1 - mine, 2, keepdims=False)
-        self.sent = send.astype(BF16)
+        self.bit = self.bits.pop(0)
+        self.spot = 1 + self.left.index(self.bit)
+        if self.parts:
+            self.sent = after(self.parts[1], *milestones) if milestones else self.parts[1]
+        else:
+            self.values = after(self.values, *milestones) if milestones else self.values
+            self.sent = self.pick(True).astype(BF16)
         self.moving = swap(self.sent, "dp", self.bit)
-        self.bit *= 2
 
     def finish(self):
-        while self.moving is not None or self.bit < self.count:
-            self.start()
-        return self.values.reshape(self.values.shape[0], self.piece, self.values.shape[-1])
+        while self.moving is not None:
+            self.launch()
+        return self.values
 
 
 def sum_everywhere(values):
@@ -546,10 +664,12 @@
         ) + lax.dot_general(place_matrix, low, dims, preferred_element_type=F32)
 
     grad_mine = sort_rows(cotangent)
-    grad_far = swap(grad_mine, "tensor", 2)
     grad_near = swap(grad_mine, "tensor", 1)
-
-    normed_one = norm_rows(tokens.astype(F32), attn_gain).astype(BF16)
+    grad_far = Transfer(grad_mine, "tensor", 2)
+    padded_router = jnp.pad(router_weight, ((0, 0), (0, 128 - experts)))
+    early = (grad_mine, grad_near, place_matrix, own_plan, other_plan, padded_router, my_hot)
+
+    normed_one = norm_rows(after(tokens, *early).astype(F32), attn_gain).astype(BF16)
     input_share = lax.dynamic_slice_in_dim(tokens, rank * share, share, 0).astype(F32)
     qkv = jnp.einsum("cdf,td->cft", qkv_weight, normed_one, preferred_element_type=F32).astype(BF16)
 
@@ -561,54 +681,76 @@
             "ft,df->td", columns(mixed, core_index), proj_weight, preferred_element_type=F32
         )
 
-    mixed_other, lse_other = forward_attention(other_seq, qkv, offsets, seq_len)
+    mixed_other, lse_other = join(
+        forward_attention(other_seq, qkv, offsets, seq_len), grad_far
+    )
     passed = swap(project(mixed_other, 1 - core).astype(BF16), "tensor", 1)
     attn_sent = (project(mixed_other, core) + passed.astype(F32)).astype(BF16)
-    attn_far = swap(attn_sent, "tensor", 2)
-    mixed_own, lse_own = forward_attention(after(own_seq, attn_sent), qkv, offsets, seq_len)
+    attn_far = Transfer(attn_sent, "tensor", 2)
+    grad_far = grad_far.moving
+    grad_both = swap(grad_far, "tensor", 1)
+    mixed_own, lse_own = join(
+        forward_attention(after(own_seq, attn_sent, grad_both), qkv, offsets, seq_len), attn_far
+    )
     attn_near = swap(project(mixed_own, 1 - core).astype(BF16), "tensor", 1)
-    attn_share = project(mixed_own, core) + attn_near.astype(F32) + attn_far.astype(F32)
-    grad_far = after(grad_far, mixed_own)
-    grad_both = swap(grad_far, "tensor", 1)
+    attn_share = project(mixed_own, core) + attn_near.astype(F32) + attn_far.moving.astype(F32)
     hidden_share = input_share + attn_share
     normed_two = norm_rows(hidden_share, ffn_gain).astype(BF16)
 
     rows_mine = sort_rows(normed_two)
-    rows_far = swap(rows_mine, "tensor", 2)
+    rows_far = Transfer(rows_mine, "tensor", 2)
     rows_near = swap(rows_mine, "tensor", 1)
-    padded_router = jnp.pad(router_weight, ((0, 0), (0, 128 - experts)))
     own = run_experts(
         own_plan, [rows_mine, rows_near], [grad_mine, grad_near], padded_router, up_weight, down_weight
     )
-    past = (own_plan, own[6:])
-    rows_far = after(rows_far, own[0])
+    own = join(own, rows_far)
+    count = lax.axis_size("dp")
+    index = lax.axis_index("dp")
+    bits = [1 << i for i in range(count.bit_length() - 1)]
+    turned_bits = bits[1:] + bits[:1]
+    piece = width // count
+    aligned = piece % CH == 0
+    back_near = swap(own[3], "tensor", 1)
+    gate_near = swap(own[5][0], "tensor", 1)
+    rows_far = rows_far.moving
     other_rows = [rows_far, swap(rows_far, "tensor", 1)]
     split = experts // 2
 
-    def run_other(plan, start):
+    def run_other(plan, start, firsts):
+        sides = jnp.stack([index // bit % 2 for bit in firsts]).astype(jnp.int32)
+        past = (own_plan, own[6:], sides, firsts if aligned else None, piece)
         return run_experts(
             plan, other_rows, [grad_far, grad_both], padded_router, up_weight, down_weight,
             past, start, split,
         )
 
-    first = run_other(other_plan, 0)
-    down_one, up_one = ScatterSum(first[7]), ScatterSum(first[6])
-    down_one.start()
-    second = run_other(after(other_plan, down_one.sent), split)
-    down_two, up_two = ScatterSum(second[7]), ScatterSum(second[6])
+    parts = 2 if aligned else 1
+    first = run_other(
+        after(other_plan, back_near, gate_near), 0, (turned_bits[0], bits[0])
+    )
+    down_one = ScatterSum(first[6 + parts :], bits)
+    up_one = ScatterSum(first[6 : 6 + parts], turned_bits)
+    down_one.launch()
+    up_one.launch()
+    second = join(
+        run_other(after(other_plan, down_one.sent, up_one.sent), split, (bits[0], bits[0])),
+        down_one,
+        up_one,
+    )
     other = [one.astype(F32) + two.astype(F32) for one, two in zip(first[:6], second[:6])]
     back_passed = swap(other[3].astype(BF16), "tensor", 1)
-    passed = swap(other[5][:, 0], "tensor", 1)
+    gate_passed = swap(other[5][0], "tensor", 1)
     back_sent = (other[2] + back_passed.astype(F32)).astype(BF16)
-    back_far = swap(back_sent, "tensor", 2)
-    gate_sorted = (
-        own[4][:, 0]
-        + swap(own[5][:, 0], "tensor", 1)
-        + swap(other[4][:, 0] + passed, "tensor", 2)
-    )
-    back_near = swap(own[3], "tensor", 1)
-    up_one.start(back_sent)
-    back_far = after(back_far, up_one.sent)
+    gate_far = Transfer(other[4][0] + gate_passed, "tensor", 2)
+    back_far = Transfer(back_sent, "tensor", 2)
+    down_two = ScatterSum(second[6 + parts :], bits)
+    up_two = ScatterSum(second[6 : 6 + parts], bits)
+    down_two.launch()
+    down_one.moving, up_one.moving = after((down_one.moving, up_one.moving), back_sent)
+    up_one.launch()
+    down_one.launch()
+    back_far = join(back_far.moving, down_two, down_one, up_one, gate_far)
+    gate_sorted = own[4][0] + gate_near + gate_far.moving
     back_share = unsort_rows(own[2] + back_near.astype(F32) + back_far.astype(F32))
     gate_grad = jnp.sum(jnp.where(place, gate_sorted[:, None], 0.0), axis=0)
 
@@ -625,10 +767,12 @@
     hidden_grad = grad_out + hidden_part
 
     attn_grad = hidden_grad.astype(BF16)
-    far_grad = swap(attn_grad, "tensor", 2)
+    far_grad = Transfer(attn_grad, "tensor", 2)
     near_grad = swap(attn_grad, "tensor", 1)
-    down_one.start(attn_grad)
-    down_two.start(attn_grad)
+    up_two.launch(attn_grad)
+    down_two.moving, down_one.moving = after((down_two.moving, down_one.moving), attn_grad)
+    down_two.launch()
+    down_one.launch()
 
     def in_order(mine, partner):
         return jnp.concatenate(
@@ -641,61 +785,66 @@
         )
 
     own_attn_grad = in_order(attn_grad, near_grad)
-    own_mixed_grad = after(mixed_grad(own_attn_grad), down_one.sent, down_two.sent)
-    own_qkv_grad, own_diag = backward_attention(
-        own_seq, qkv, own_mixed_grad, lse_own, offsets, seq_len
-    )
-    far_grad = after(far_grad, own_qkv_grad)
+    own_mixed_grad = after(mixed_grad(own_attn_grad), up_two.sent, down_one.sent, down_two.sent)
+    own_qkv_grad, own_diag = join(
+        backward_attention(own_seq, qkv, own_mixed_grad, lse_own, offsets, seq_len),
+        far_grad,
+        up_two,
+        down_one,
+        down_two,
+    )
+    far_grad = far_grad.moving
     other_attn_grad = in_order(far_grad, swap(far_grad, "tensor", 1))
     held = after((own[0], own[1], other[0], other[1]), own_qkv_grad)
+    out_near = swap(held[1], "tensor", 1)
     out_passed = swap(held[3].astype(BF16), "tensor", 1)
     out_sent = (held[2] + out_passed.astype(F32)).astype(BF16)
-    out_far = swap(out_sent, "tensor", 2)
-    out_near = swap(held[1], "tensor", 1)
-    up_one.start(own_qkv_grad)
-    down_one.start(own_qkv_grad)
-    up_two.start(own_qkv_grad)
+    out_far = Transfer(out_sent, "tensor", 2)
+    up_one.moving, down_two.moving = after((up_one.moving, down_two.moving), own_qkv_grad)
+    up_one.launch()
+    down_two.launch()
+    up_two.launch()
     other_mixed_grad = after(
-        mixed_grad(other_attn_grad), out_sent, up_one.sent, down_one.sent, up_two.sent
-    )
-    other_qkv_grad, other_diag = backward_attention(
-        other_seq, qkv, other_mixed_grad, lse_other, offsets, seq_len
-    )
-
-    def input_part(qkv_rows, core_index):
-        return jnp.einsum(
-            "cft,cdf->td", columns(qkv_rows, core_index), qkv_weight, preferred_element_type=F32
-        )
-
-    input_passed = swap(input_part(other_qkv_grad, 1 - core).astype(BF16), "tensor", 1)
-    input_sent = (input_part(other_qkv_grad, core) + input_passed.astype(F32)).astype(BF16)
-    input_far = swap(input_sent, "tensor", 2)
-    own_late = after(own_qkv_grad, input_sent)
-    input_near = swap(input_part(own_late, 1 - core).astype(BF16), "tensor", 1)
-    down_two.start(input_sent)
-    up_one.start(input_sent)
-    own_normed = lax.dynamic_slice_in_dim(normed_one, chip * half, half, 0)
-    other_normed = lax.dynamic_slice_in_dim(normed_one, (1 - chip) * half, half, 0)
-    qkv_grad = jnp.einsum(
-        "td,cft->cdf", own_normed, own_late, preferred_element_type=F32
-    ) + jnp.einsum("td,cft->cdf", other_normed, other_qkv_grad, preferred_element_type=F32)
-    proj_grad = jnp.einsum(
-        "td,ft->df", own_attn_grad, mixed_own, preferred_element_type=F32
-    ) + jnp.einsum("td,ft->df", other_attn_grad, mixed_other, preferred_element_type=F32)
-    projections = ScatterSum(jnp.concatenate([qkv_grad, proj_grad[None]]))
-    projections.start(down_two.sent, up_one.sent)
-    input_share_grad = (
-        input_part(own_late, core)
-        + input_near.astype(F32)
-        + after(input_far, projections.sent).astype(F32)
-    )
+        mixed_grad(other_attn_grad), out_sent, out_near, up_one.sent, down_two.sent, up_two.sent
+    )
+    other_qkv_grad, other_diag = join(
+        backward_attention(other_seq, qkv, other_mixed_grad, lse_other, offsets, seq_len),
+        out_far,
+        up_one,
+        down_two,
+        up_two,
+    )
+    out_far = out_far.moving
+
+    core_index = core.astype(jnp.int32).reshape(1)
+    up_two.launch()
+    normed, own_late = after((normed_one, own_qkv_grad), up_two.sent)
+    qkv_proj, gain_part = projection_grads(
+        (own_seq, other_seq),
+        normed,
+        (own_late, other_qkv_grad),
+        (own_attn_grad, other_attn_grad),
+        (mixed_own, mixed_other),
+        qkv_weight,
+    )
+    projections = ScatterSum([qkv_proj], bits)
+    projections.launch()
+    core_index = after(core_index, projections.sent)
+    input_keep, input_send = input_grads(core_index, other_qkv_grad, qkv_weight)
+    input_passed = swap(input_send, "tensor", 1)
+    input_sent = (input_keep + input_passed.astype(F32)).astype(BF16)
+    input_far = Transfer(input_sent, "tensor", 2)
+    input_own, input_send = input_grads(after(core_index, input_sent), own_late, qkv_weight)
+    input_near = swap(input_send, "tensor", 1)
+    late = join(after(input_own, input_near), input_far, projections, up_two)
+    input_share_grad = late + input_near.astype(F32) + input_far.moving.astype(F32)
+    projections.launch()
     token_part = jax.vjp(lambda rows_in: norm_rows(rows_in, attn_gain), input_share)[1](
         input_share_grad
     )[0]
     tokens_grad = hidden_grad + token_part
-    attn_gain_grad = jnp.sum(qkv_weight.astype(F32) * qkv_grad, axis=(0, 2)) / attn_gain
-
-    out_far = after(out_far, input_sent)
+    attn_gain_grad = gain_part[0] / attn_gain
+
     expert_share = unsort_rows(held[0] + out_near.astype(F32) + out_far.astype(F32))
     layer_out = (hidden_share + gate_prob[:, None] * expert_share).astype(BF16)
 
@@ -707,13 +856,11 @@
     sizes = [array.size for array in small]
     packed = jnp.concatenate(small)
     packed = jnp.pad(packed, (0, -packed.size % 1024)).reshape(-1, 128)
-    packed = sum_everywhere(after(packed, projections.sent)).reshape(-1)
+    packed = sum_everywhere(after(packed, input_share_grad, projections.sent)).reshape(-1)
     ends = [sum(sizes[:i]) for i in range(5)]
     attn_gain_grad, ffn_gain_grad, router_grad, table_grad = [
         packed[ends[i] : ends[i + 1]] for i in range(4)
     ]
-    up_two.start(input_share_grad)
-    projections.start(input_share_grad)
     down_grad = jnp.concatenate([down_one.finish(), down_two.finish()])
     up_grad = jnp.concatenate([up_one.finish(), up_two.finish()])
     qkv_proj = projections.finish()

time: 388 us -> 335 us (0.86)
  local copies, waits for them, and re-layouts: 61.6 us -> 24.5 us
  matrix products: 40.9 us -> 20.8 us
  waiting for transfers between devices: 92.3 us -> 82 us
  Pallas kernels: 106 us -> 115 us
  starting transfers between devices: 38 us -> 42.4 us
    dot_general x8 -> x0, matrix products: 16.1 us -> none  [the longest x4 9.43 us: input_part(): jnp.einsum('cft,cdf->td', columns(qkv_rows, core_index), qkv_weight, pref...]
    squeeze x12 -> x0, local copies, waits for them, and re-layouts: 11.5 us -> none  [start(): self.keep = lax.dynamic_index_in_dim(values, mine, 2, keepdims=False)]
    pallas_call x0 -> x3, Pallas kernels: none -> 10.9 us  [the longest x1 7.94 us: projection_grads(): pl.pallas_call(projection_kernel, grid_spec=pltpu.PrefetchScalarGridSpec(...]
    ppermute x44, waiting for transfers between devices: 92.3 us -> 82 us  [swap(): return lax.ppermute(values, axis, [(i, i ^ bit) for i in range(count)])]
    dynamic_slice x3 -> x2, local copies, waits for them, and re-layouts: 10.8 us -> 2.61 us  [pick(): lax.dynamic_index_in_dim(self.values, index, self.spot, keepdims=False)]
    reshape x1 -> x0, local copies, waits for them, and re-layouts: 6.6 us -> none  [start(): values = after(self.values, *milestones).reshape(shape)]
    ppermute x44, starting transfers between devices: 38 us -> 42.4 us  [swap(): return lax.ppermute(values, axis, [(i, i ^ bit) for i in range(count)])]
    unnamed x140, local copies, waits for them, and re-layouts: 15.6 us -> 11.4 us
  transfers between devices with their start and end apart: 44 -> 44, of which waited for: 13 -> 24; matrix products, arithmetic and copies ran while one was open for 31% -> 16% of each run, Pallas kernels for 15% -> 25%
where the time goes in v2:
time: 335 us; the launch traced here: 330 us
  Pallas kernels  115 us (34%)
  waiting for transfers between devices  82 us (24%)
  other arithmetic  43.3 us (13%)
  starting transfers between devices  42.4 us (13%)
  local copies, waits for them, and re-layouts  24.5 us (7%)
  matrix products  20.8 us (6%)
    ppermute x44, waiting for transfers between devices, swap(): return lax.ppermute(values, axis, [(i, i ^ bit) for i in range(count)])  82 us
    pallas_call x3, Pallas kernels, run_experts(): pl.pallas_call(functools.partial(expert_kernel, shares=shares, first_expe...  57.7 us
    ppermute x44, starting transfers between devices, swap(): return lax.ppermute(values, axis, [(i, i ^ bit) for i in range(count)])  42.4 us
    pallas_call x2, Pallas kernels, backward_attention(): pl.pallas_call(backward_kernel, grid_spec=pltpu.PrefetchScalarGridSpec(nu...  25.3 us
    pallas_call x2, Pallas kernels, forward_attention(): pl.pallas_call(forward_kernel, grid_spec=pltpu.PrefetchScalarGridSpec(num...  21.3 us
    add x15, other arithmetic, land(): self.values = keep.astype(F32) + self.moving.astype(F32)  12.3 us
    unnamed x140, local copies, waits for them, and re-layouts  11.4 us
    pallas_call x1, Pallas kernels, projection_grads(): pl.pallas_call(projection_kernel, grid_spec=pltpu.PrefetchScalarGridSpec(...  7.94 us
  transfers between devices with their start and end apart: 44, of which 24 were waited for; matrix products, arithmetic and copies ran while one was open for 16% of the time, Pallas kernels for 25%

profile of v2, /device:TPU:0, one launch (start us, length us, event | category | flops | bytes accessed | tf_op | source)
XLA Modules:
  0.0 330.2 jit_solution(14313859077650540115)
XLA Ops:
  4.1 2.6 convolution_convert_fusion.3.refs_3_
  14.3 2.9 fusion
  21.0 10.7 %attention_forward.2 = (bf16[192,1024]{1,0:T(8,128)(2,1)S(1)}, f32[3,1,1024]{2,1,0:T(1,128)S(1)}) custom-call(s32[1]{0:T(128)S(6)} %sub.152.seq_ref.refs_1_, bf16[3,192,2048]{2,1,0:T(8,128)(2,1)S(1)} %convert_bitcast_fusion.qkv_ref, f32[3,1,2048]{2,1,0:T(1,128)S(1)} %broadcast_in_dim.42.offset_ref), custom_call_target="tpu_custom_call" | custom-call | flops 1 | bytes 1 | tf_op jit(solution)/shard_map/attention_forward/pallas_call | solution.py:53
  37.5 10.6 %attention_forward.3 = (bf16[192,1024]{1,0:T(8,128)(2,1)S(1)}, f32[3,1,1024]{2,1,0:T(1,128)S(1)}) custom-call(s32[1]{0:T(128)} %bitcast.seq_ref.refs_0_, bf16[3,192,2048]{2,1,0:T(8,128)(2,1)S(1)} %convert_bitcast_fusion.qkv_ref, f32[3,1,2048]{2,1,0:T(1,128)S(1)} %broadcast_in_dim.42.offset_ref), custom_call_target="tpu_custom_call" | custom-call | flops 1 | bytes 1 | tf_op jit(solution)/shard_map/attention_forward/pallas_call | solution.py:53
  48.0 8.9 %collective-permute-done.4 = bf16[512,768]{1,0:T(8,128)(2,1)S(1)} collective-permute-done((bf16[512,768]{1,0:T(8,128)(2,1)S(1)}, bf16[512,768]{1,0:T(8,128)(2,1)S(1)}, u32[]{:S(2)}, u32[]{:S(2)}) %collective-permute-start.4) | collective-permute-done | bytes 786464 | tf_op jit(solution)/shard_map/ppermute | solution.py:529
  65.7 19.8 %experts.1 = (f32[512,768]{1,0:T(8,128)}, bf16[512,768]{1,0:T(8,128)(2,1)}, f32[512,768]{1,0:T(8,128)}, bf16[512,768]{1,0:T(8,128)(2,1)}, f32[1,512]{1,0:T(1,128...) custom-call(s32[10,4]{1,0:T(8,128)} %concatenate.24.refs_0_.refs_1_,, ...), custom_call_target="tpu_custom_call" | custom-call | flops 1 | bytes 1 | tf_op jit(solution)/shard_map/experts/pallas_call | solution.py:423
  89.4 21.9 %experts_and_grads.2 = (f32[512,768]{1,0:T(8,128)}, bf16[512,768]{1,0:T(8,128)(2,1)}, f32[512,768]{1,0:T(8,128)}, bf16[512,768]{1,0:T(8,128)(2,1)}, f32[1,512]{1...) custom-call(s32[10,4]{1,0:T(8,128)} %copy.109.refs_0_, ...), custom_call_target="tpu_custom_call" | custom-call | flops 1 | bytes 1 | tf_op jit(solution)/shard_map/experts_and_grads/pallas_call | solution.py:423
  111.3 4.1 %collective-permute-start.11 = (bf16[2,4,96,768]{3,2,1,0:T(8,128)(2,1)}, bf16[2,4,96,768]{3,2,1,0:T(8,128)(2,1)}, u32[]{:S(2)}, u32[]{:S(2)}) collective-permute-start(bf16[2,4,96,768]{3,2,1,0:T(8,128)(2,1)} %get-tuple-element.158), channel_id=1, source_target_pairs={{0,4},{4,0},{8,12},{12,8},{16,20},{20,16},{24,28},{28,24},{1,5},{5... | collective-permute-start | bytes 3538952 | tf_op jit(solution)/shard_map/ppermute | solution.py:529
  116.5 16.0 %experts_and_grads.3 = (f32[512,768]{1,0:T(8,128)}, bf16[512,768]{1,0:T(8,128)(2,1)}, f32[512,768]{1,0:T(8,128)}, bf16[512,768]{1,0:T(8,128)(2,1)}, f32[1,512]{1...) custom-call(s32[10,4]{1,0:T(8,128)} %copy.110.refs_0_, ...), custom_call_target="tpu_custom_call" | custom-call | flops 1 | bytes 1 | tf_op jit(solution)/shard_map/experts_and_grads/pallas_call | solution.py:423
  132.5 9.5 %collective-permute-done.11 = bf16[2,4,96,768]{3,2,1,0:T(8,128)(2,1)} collective-permute-done((bf16[2,4,96,768]{3,2,1,0:T(8,128)(2,1)}, bf16[2,4,96,768]{3,2,1,0:T(8,128)(2,1)}, u32[]{:S(2)}, u32[]{:S(2)}) %collective-permute-start.11) | collective-permute-done | bytes 1179680 | tf_op jit(solution)/shard_map/ppermute | solution.py:529
  153.6 2.7 collective-permute-start.17
  165.4 5.8 %collective-permute-done.19 = f32[512]{0:T(512)S(1)} collective-permute-done((f32[512]{0:T(512)S(1)}, f32[512]{0:T(512)S(1)}, u32[]{:S(2)}, u32[]{:S(2)}) %collective-permute-start.19) | collective-permute-done | bytes 2080 | tf_op jit(solution)/shard_map/ppermute | solution.py:529
  171.2 5.7 %collective-permute-done.15 = bf16[2,4,96,768]{3,2,1,0:T(8,128)(2,1)S(1)} collective-permute-done((bf16[2,4,96,768]{3,2,1,0:T(8,128)(2,1)}, bf16[2,4,96,768]{3,2,1,0:T(8,128)(2,1)S(1)}, u32[]{:S(2)}, u32[]{:S(2)}) %collective-permute-start.15) | collective-permute-done | bytes 1179680 | tf_op jit(solution)/shard_map/ppermute | solution.py:529
  176.8 5.6 %collective-permute-done.17 = bf16[2,2,96,768]{3,2,0,1:T(8,128)(2,1)S(1)} collective-permute-done((bf16[2,2,96,768]{3,2,0,1:T(8,128)(2,1)S(1)}, bf16[2,2,96,768]{3,2,0,1:T(8,128)(2,1)S(1)}, u32[]{:S(2)}, u32[]{:S(2)}) %collective-permute-start.17) | collective-permute-done | bytes 589856 | tf_op jit(solution)/shard_map/ppermute | solution.py:529
  197.7 5.2 %collective-permute-start.23 = (bf16[2,96,768]{2,1,0:T(8,128)(2,1)S(1)}, bf16[2,96,768]{2,1,0:T(8,128)(2,1)}, u32[]{:S(2)}, u32[]{:S(2)}) collective-permute-start(bf16[2,96,768]{2,1,0:T(8,128)(2,1)S(1)} %fusion.31), channel_id=1, source_target_pairs={{0,16},{4,20},{8,24},{12,28},{16,0},{20,4},{24,8},{28,12},{1,17},{... | collective-permute-start | bytes 884744 | tf_op jit(solution)/shard_map/ppermute | solution.py:529
  205.2 12.7 %attention_backward.2 = (bf16[3,192,1024]{2,1,0:T(8,128)(2,1)S(1)}, f32[3,1,2048]{2,1,0:T(1,128)S(1)}) custom-call(s32[1]{0:T(128)} %bitcast.seq_ref.refs_0_, bf16[3,192,2048]{2,1,0:T(8,128)(2,1)S(1)} %convert_bitcast_fusion.qkv_ref, bf16[192,1024]{1,0:T(8,128)(2,1)S(1)} %fusion.9.grad_ref, f32[3,1,1024]{2,1,0:T(1,128)S(1)} %get-tuple-element.201.lse_ref, ...), custom_call_target="tpu_custom_call" | custom-call | flops 1 | bytes 1 | tf_op jit(solution)/shard_map/attention_backward/pallas_call | solution.py:125
  226.6 4.1 %collective-permute-start.30 = (bf16[2,96,768]{2,1,0:T(8,128)(2,1)S(1)}, bf16[2,96,768]{2,1,0:T(8,128)(2,1)S(1)}, u32[]{:S(2)}, u32[]{:S(2)}) collective-permute-start(bf16[2,96,768]{2,1,0:T(8,128)(2,1)S(1)} %fusion.33), channel_id=1, source_target_pairs={{0,16},{4,20},{8,24},{12,28},{16,0},{20,4},{24,8},{28,12},{1,17},{... | collective-permute-start | bytes 884744 | tf_op jit(solution)/shard_map/ppermute | solution.py:529
  235.4 12.5 %attention_backward.3 = (bf16[3,192,1024]{2,1,0:T(8,128)(2,1)S(1)}, f32[3,1,2048]{2,1,0:T(1,128)S(1)}) custom-call(s32[1]{0:T(128)S(6)} %sub.152.seq_ref.refs_1_, bf16[3,192,2048]{2,1,0:T(8,128)(2,1)S(1)} %convert_bitcast_fusion.qkv_ref, bf16[192,1024]{1,0:T(8,128)(2,1)S(1)} %fusion.10.grad_ref, f32[3,1,1024]{2,1,0:T(1,128)S(1)} %get-tuple-element.217.lse_ref, ...), custom_call_target="tpu_custom_call" | custom-call | flops 1 | bytes 1 | tf_op jit(solution)/shard_map/attention_backward/pallas_call | solution.py:125
  251.4 7.9 %projection_grads.1 = (bf16[4,768,192]{2,1,0:T(8,128)(2,1)}, f32[1,768]{1,0:T(1,128)}) custom-call(s32[1]{0:T(128)} %bitcast.seq_ref.refs_0_, s32[1]{0:T(128)S(6)} %sub.152.seq_ref.refs_1_, bf16[2048,768]{1,0:T(8,128)(2,1)} %copy-done.12, bf16[2048,768]{1,0:T(8,128)(2,1)} %copy-done.12, bf16[3,192,1024]{2,1,0:T(8,128)(2,1)} %copy-done.2, ...), custom_call_target="tpu_custom_call" | custom-call | tf_op jit(solution)/shard_map/projection_grads/pallas_call | solution.py:498
  278.0 6.0 %collective-permute-done.36 = bf16[2,96,768]{2,1,0:T(8,128)(2,1)} collective-permute-done((bf16[2,96,768]{2,1,0:T(8,128)(2,1)}, bf16[2,96,768]{2,1,0:T(8,128)(2,1)}, u32[]{:S(2)}, u32[]{:S(2)}) %collective-permute-start.36) | collective-permute-done | bytes 294944 | tf_op jit(solution)/shard_map/ppermute | solution.py:529
  286.2 6.9 %collective-permute-done.34 = bf16[512,768]{1,0:T(8,128)(2,1)} collective-permute-done((bf16[512,768]{1,0:T(8,128)(2,1)}, bf16[512,768]{1,0:T(8,128)(2,1)}, u32[]{:S(2)}, u32[]{:S(2)}) %collective-permute-start.34) | collective-permute-done | bytes 786464 | tf_op jit(solution)/shard_map/ppermute | solution.py:529
  300.4 3.3 collective-permute-done.38
  313.4 2.5 collective-permute-done.41
  319.8 8.8 %collective-permute-done.43 = bf16[4,96,192]{2,1,0:T(8,128)(2,1)S(1)} collective-permute-done((bf16[4,96,192]{2,1,0:T(8,128)(2,1)S(1)}, bf16[4,96,192]{2,1,0:T(8,128)(2,1)S(1)}, u32[]{:S(2)}, u32[]{:S(2)}) %collective-permute-start.43) | collective-permute-done | bytes 147488 | tf_op jit(solution)/shard_map/ppermute | solution.py:529
  (350 shorter events, 131.2 us)
Async XLA Ops:
  7.1 24.6 %collective-permute-start.1 = (bf16[512,768]{1,0:T(8,128)(2,1)}, bf16[512,768]{1,0:T(8,128)(2,1)}, u32[]{:S(2)}, u32[]{:S(2)}) collective-permute-start(bf16[512,768]{1,0:T(8,128)(2,1)} %convolution_convert_fusion.3.refs_3_), channel_id=1, source_target_pairs={{0,2},{1,3},{2,0},{3,1},{4,6},{5,7},{6,4},{7,5},{8,10},{9,11},{10,... | collective-permute-start | bytes 2359304 | tf_op jit(solution)/shard_map/ppermute | solution.py:529
  37.3 19.7 %collective-permute-start.4 = (bf16[512,768]{1,0:T(8,128)(2,1)S(1)}, bf16[512,768]{1,0:T(8,128)(2,1)S(1)}, u32[]{:S(2)}, u32[]{:S(2)}) collective-permute-start(bf16[512,768]{1,0:T(8,128)(2,1)S(1)} %add_convert_fusion.5), channel_id=1, source_target_pairs={{0,2},{1,3},{2,0},{3,1},{4,6},{5,7},{6,4},{7,5},{8,10},{9,11},{10,... | collective-permute-start | bytes 2359304 | tf_op jit(solution)/shard_map/ppermute | solution.py:529
  62.7 22.9 %collective-permute-start.7 = (bf16[512,768]{1,0:T(8,128)(2,1)S(1)}, bf16[512,768]{1,0:T(8,128)(2,1)}, u32[]{:S(2)}, u32[]{:S(2)}) collective-permute-start(bf16[512,768]{1,0:T(8,128)(2,1)S(1)} %convolution_convert_fusion.2.refs_1_), channel_id=1, source_target_pairs={{0,2},{1,3},{2,0},{3,1},{4,6},{5,7},{6,4},{7,5},{8,10},{9,11},{10,... | collective-permute-start | bytes 2359304 | tf_op jit(solution)/shard_map/ppermute | solution.py:529
  111.3 30.7 %collective-permute-start.11 = (bf16[2,4,96,768]{3,2,1,0:T(8,128)(2,1)}, bf16[2,4,96,768]{3,2,1,0:T(8,128)(2,1)}, u32[]{:S(2)}, u32[]{:S(2)}) collective-permute-start(bf16[2,4,96,768]{3,2,1,0:T(8,128)(2,1)} %get-tuple-element.158), channel_id=1, source_target_pairs={{0,4},{4,0},{8,12},{12,8},{16,20},{20,16},{24,28},{28,24},{1,5},{5... | collective-permute-start | bytes 3538952 | tf_op jit(solution)/shard_map/ppermute | solution.py:529
  115.4 28.1 %collective-permute-start.12 = (bf16[2,4,96,768]{3,2,1,0:T(8,128)(2,1)}, bf16[2,4,96,768]{3,2,1,0:T(8,128)(2,1)}, u32[]{:S(2)}, u32[]{:S(2)}) collective-permute-start(bf16[2,4,96,768]{3,2,1,0:T(8,128)(2,1)} %get-tuple-element.159), channel_id=1, source_target_pairs={{0,8},{4,12},{8,0},{12,4},{16,24},{20,28},{24,16},{28,20},{1,9},{5... | collective-permute-start | bytes 3538952 | tf_op jit(solution)/shard_map/ppermute | solution.py:529
  148.2 28.7 %collective-permute-start.15 = (bf16[2,4,96,768]{3,2,1,0:T(8,128)(2,1)}, bf16[2,4,96,768]{3,2,1,0:T(8,128)(2,1)S(1)}, u32[]{:S(2)}, u32[]{:S(2)}) collective-permute-start(bf16[2,4,96,768]{3,2,1,0:T(8,128)(2,1)} %get-tuple-element.179), channel_id=1, source_target_pairs={{0,4},{4,0},{8,12},{12,8},{16,20},{20,16},{24,28},{28,24},{1,5},{5... | collective-permute-start | bytes 3538952 | tf_op jit(solution)/shard_map/ppermute | solution.py:529
  151.4 32.9 %collective-permute-start.14 = (bf16[512,768]{1,0:T(8,128)(2,1)S(1)}, bf16[512,768]{1,0:T(8,128)(2,1)S(1)}, u32[]{:S(2)}, u32[]{:S(2)}) collective-permute-start(bf16[512,768]{1,0:T(8,128)(2,1)S(1)} %add_convert_fusion.3), channel_id=1, source_target_pairs={{0,2},{1,3},{2,0},{3,1},{4,6},{5,7},{6,4},{7,5},{8,10},{9,11},{10,... | collective-permute-start | bytes 2359304 | tf_op jit(solution)/shard_map/ppermute | solution.py:529
  153.6 28.9 %collective-permute-start.17 = (bf16[2,2,96,768]{3,2,0,1:T(8,128)(2,1)S(1)}, bf16[2,2,96,768]{3,2,0,1:T(8,128)(2,1)S(1)}, u32[]{:S(2)}, u32[]{:S(2)}) collective-permute-start(bf16[2,2,96,768]{3,2,0,1:T(8,128)(2,1)S(1)} %fusion.19), channel_id=1, source_target_pairs={{0,16},{4,20},{8,24},{12,28},{16,0},{20,4},{24,8},{28,12},{1,17},{... | collective-permute-start | bytes 1769480 | tf_op jit(solution)/shard_map/ppermute | solution.py:529
  158.0 26.3 %collective-permute-start.16 = (bf16[2,2,96,768]{3,2,0,1:T(8,128)(2,1)S(1)}, bf16[2,2,96,768]{3,2,0,1:T(8,128)(2,1)S(1)}, u32[]{:S(2)}, u32[]{:S(2)}) collective-permute-start(bf16[2,2,96,768]{3,2,0,1:T(8,128)(2,1)S(1)} %fusion.18), channel_id=1, source_target_pairs={{0,8},{4,12},{8,0},{12,4},{16,24},{20,28},{24,16},{28,20},{1,9},{5... | collective-permute-start | bytes 1769480 | tf_op jit(solution)/shard_map/ppermute | solution.py:529
  190.8 12.3 %collective-permute-start.20 = (bf16[512,768]{1,0:T(8,128)(2,1)}, bf16[512,768]{1,0:T(8,128)(2,1)}, u32[]{:S(2)}, u32[]{:S(2)}) collective-permute-start(bf16[512,768]{1,0:T(8,128)(2,1)} %fusion.62), channel_id=1, source_target_pairs={{0,1},{1,0},{2,3},{3,2},{4,5},{5,4},{6,7},{7,6},{8,9},{9,8},{10,11... | collective-permute-start | bytes 2359304 | tf_op jit(solution)/shard_map/ppermute | solution.py:529
  190.8 28.8 %collective-permute-start.21 = (bf16[512,768]{1,0:T(8,128)(2,1)}, bf16[512,768]{1,0:T(8,128)(2,1)}, u32[]{:S(2)}, u32[]{:S(2)}) collective-permute-start(bf16[512,768]{1,0:T(8,128)(2,1)} %fusion.62), channel_id=1, source_target_pairs={{0,2},{1,3},{2,0},{3,1},{4,6},{5,7},{6,4},{7,5},{8,10},{9,11},{10,... | collective-permute-start | bytes 2359304 | tf_op jit(solution)/shard_map/ppermute | solution.py:529
  192.4 28.4 %collective-permute-start.22 = (bf16[2,4,96,768]{3,2,1,0:T(8,128)(2,1)}, bf16[2,4,96,768]{3,2,1,0:T(8,128)(2,1)}, u32[]{:S(2)}, u32[]{:S(2)}) collective-permute-start(bf16[2,4,96,768]{3,2,1,0:T(8,128)(2,1)} %get-tuple-element.194), channel_id=1, source_target_pairs={{0,4},{4,0},{8,12},{12,8},{16,20},{20,16},{24,28},{28,24},{1,5},{5... | collective-permute-start | bytes 3538952 | tf_op jit(solution)/shard_map/ppermute | solution.py:529
  196.5 23.0 %collective-permute-start.24 = (bf16[2,2,96,768]{3,2,0,1:T(8,128)(2,1)}, bf16[2,2,96,768]{3,2,0,1:T(8,128)(2,1)}, u32[]{:S(2)}, u32[]{:S(2)}) collective-permute-start(bf16[2,2,96,768]{3,2,0,1:T(8,128)(2,1)} %fusion.20), channel_id=1, source_target_pairs={{0,8},{4,12},{8,0},{12,4},{16,24},{20,28},{24,16},{28,20},{1,9},{5... | collective-permute-start | bytes 1769480 | tf_op jit(solution)/shard_map/ppermute | solution.py:529
  197.7 21.9 %collective-permute-start.23 = (bf16[2,96,768]{2,1,0:T(8,128)(2,1)S(1)}, bf16[2,96,768]{2,1,0:T(8,128)(2,1)}, u32[]{:S(2)}, u32[]{:S(2)}) collective-permute-start(bf16[2,96,768]{2,1,0:T(8,128)(2,1)S(1)} %fusion.31), channel_id=1, source_target_pairs={{0,16},{4,20},{8,24},{12,28},{16,0},{20,4},{24,8},{28,12},{1,17},{... | collective-permute-start | bytes 884744 | tf_op jit(solution)/shard_map/ppermute | solution.py:529
  220.8 14.6 %collective-permute-start.25 = (bf16[512,768]{1,0:T(8,128)(2,1)S(1)}, bf16[512,768]{1,0:T(8,128)(2,1)S(1)}, u32[]{:S(2)}, u32[]{:S(2)}) collective-permute-start(bf16[512,768]{1,0:T(8,128)(2,1)S(1)} %copy-done.66), channel_id=1, source_target_pairs={{0,1},{1,0},{2,3},{3,2},{4,5},{5,4},{6,7},{7,6},{8,9},{9,8},{10,11... | collective-permute-start | bytes 2359304 | tf_op jit(solution)/shard_map/ppermute | solution.py:529
  221.3 10.6 %collective-permute-start.26 = (bf16[512,768]{1,0:T(8,128)(2,1)}, bf16[512,768]{1,0:T(8,128)(2,1)S(1)}, u32[]{:S(2)}, u32[]{:S(2)}) collective-permute-start(bf16[512,768]{1,0:T(8,128)(2,1)} %collective-permute-done.21), channel_id=1, source_target_pairs={{0,1},{1,0},{2,3},{3,2},{4,5},{5,4},{6,7},{7,6},{8,9},{9,8},{10,11... | collective-permute-start | bytes 2359304 | tf_op jit(solution)/shard_map/ppermute | solution.py:529
  223.1 26.3 %collective-permute-start.31 = (bf16[2,2,96,768]{3,2,0,1:T(8,128)(2,1)S(1)}, bf16[2,2,96,768]{3,2,0,1:T(8,128)(2,1)S(1)}, u32[]{:S(2)}, u32[]{:S(2)}) collective-permute-start(bf16[2,2,96,768]{3,2,0,1:T(8,128)(2,1)S(1)} %fusion.21), channel_id=1, source_target_pairs={{0,8},{4,12},{8,0},{12,4},{16,24},{20,28},{24,16},{28,20},{1,9},{5... | collective-permute-start | bytes 1769480 | tf_op jit(solution)/shard_map/ppermute | solution.py:529
  226.6 22.9 %collective-permute-start.30 = (bf16[2,96,768]{2,1,0:T(8,128)(2,1)S(1)}, bf16[2,96,768]{2,1,0:T(8,128)(2,1)S(1)}, u32[]{:S(2)}, u32[]{:S(2)}) collective-permute-start(bf16[2,96,768]{2,1,0:T(8,128)(2,1)S(1)} %fusion.33), channel_id=1, source_target_pairs={{0,16},{4,20},{8,24},{12,28},{16,0},{20,4},{24,8},{28,12},{1,17},{... | collective-permute-start | bytes 884744 | tf_op jit(solution)/shard_map/ppermute | solution.py:529
  231.0 19.4 %collective-permute-start.28 = (bf16[512,768]{1,0:T(8,128)(2,1)S(1)}, bf16[512,768]{1,0:T(8,128)(2,1)S(1)}, u32[]{:S(2)}, u32[]{:S(2)}) collective-permute-start(bf16[512,768]{1,0:T(8,128)(2,1)S(1)} %add_convert_fusion.2), channel_id=1, source_target_pairs={{0,2},{1,3},{2,0},{3,1},{4,6},{5,7},{6,4},{7,5},{8,10},{9,11},{10,... | collective-permute-start | bytes 2359304 | tf_op jit(solution)/shard_map/ppermute | solution.py:529
  231.9 17.5 %collective-permute-start.29 = (bf16[2,96,768]{2,1,0:T(8,128)(2,1)S(1)}, bf16[2,96,768]{2,1,0:T(8,128)(2,1)S(1)}, u32[]{:S(2)}, u32[]{:S(2)}) collective-permute-start(bf16[2,96,768]{2,1,0:T(8,128)(2,1)S(1)} %fusion.32), channel_id=1, source_target_pairs={{0,4},{4,0},{8,12},{12,8},{16,20},{20,16},{24,28},{28,24},{1,5},{5... | collective-permute-start | bytes 884744 | tf_op jit(solution)/shard_map/ppermute | solution.py:529
  265.9 20.2 %collective-permute-start.35 = (bf16[4,2,2,96,192]{4,3,0,1,2:T(8,128)(2,1)}, bf16[4,2,2,96,192]{4,3,0,1,2:T(8,128)(2,1)}, u32[]{:S(2)}, u32[]{:S(2)}) collective-permute-start(bf16[4,2,2,96,192]{4,3,0,1,2:T(8,128)(2,1)} %bitcast.122), channel_id=1, source_target_pairs={{0,4},{4,0},{8,12},{12,8},{16,20},{20,16},{24,28},{28,24},{1,5},{5... | collective-permute-start | bytes 1769480 | tf_op jit(solution)/shard_map/ppermute | solution.py:529
  267.4 16.7 %collective-permute-start.36 = (bf16[2,96,768]{2,1,0:T(8,128)(2,1)}, bf16[2,96,768]{2,1,0:T(8,128)(2,1)}, u32[]{:S(2)}, u32[]{:S(2)}) collective-permute-start(bf16[2,96,768]{2,1,0:T(8,128)(2,1)} %fusion.34), channel_id=1, source_target_pairs={{0,16},{4,20},{8,24},{12,28},{16,0},{20,4},{24,8},{28,12},{1,17},{... | collective-permute-start | bytes 884744 | tf_op jit(solution)/shard_map/ppermute | solution.py:529
  273.5 19.7 %collective-permute-start.34 = (bf16[512,768]{1,0:T(8,128)(2,1)}, bf16[512,768]{1,0:T(8,128)(2,1)}, u32[]{:S(2)}, u32[]{:S(2)}) collective-permute-start(bf16[512,768]{1,0:T(8,128)(2,1)} %add_convert_fusion), channel_id=1, source_target_pairs={{0,2},{1,3},{2,0},{3,1},{4,6},{5,7},{6,4},{7,5},{8,10},{9,11},{10,... | collective-permute-start | bytes 2359304 | tf_op jit(solution)/shard_map/ppermute | solution.py:529
  299.2 18.6 %collective-permute-start.42 = (bf16[4,2,96,192]{3,2,0,1:T(8,128)(2,1)S(1)}, bf16[4,2,96,192]{3,2,0,1:T(8,128)(2,1)S(1)}, u32[]{:S(2)}, u32[]{:S(2)}) collective-permute-start(bf16[4,2,96,192]{3,2,0,1:T(8,128)(2,1)S(1)} %fusion.30), channel_id=1, source_target_pairs={{0,8},{4,12},{8,0},{12,4},{16,24},{20,28},{24,16},{28,20},{1,9},{5... | collective-permute-start | bytes 884744 | tf_op jit(solution)/shard_map/ppermute | solution.py:529
  (88 other events, 430.9 us)

commit v3 on v2

--- a/solution.py
+++ b/solution.py
@@ -239,9 +239,9 @@
         filled = filled + chunks
 
 
-def store_parts(outs, values, side, bit, piece):
+def store_parts(outs, slot, values, side, bit, piece):
     if len(outs) == 1:
-        outs[0][0] = values[...].astype(jnp.bfloat16)
+        outs[0][slot] = values[...].astype(jnp.bfloat16)
         return
     for index in range(values.shape[0] // (2 * piece)):
         low, high = index % bit, index // bit
@@ -249,10 +249,12 @@
             chosen = side if which == 0 else 1 - side
             start = ((high * 2 + chosen) * bit + low) * piece
             rows = values[pl.ds(pl.multiple_of(start, CH), piece)]
-            out[0, index] = rows.astype(jnp.bfloat16)
-
-
-def expert_kernel(*refs, shares, first_expert, expert_count, with_grads, bits, piece):
+            out[slot, index] = rows.astype(jnp.bfloat16)
+
+
+def expert_kernel(
+    *refs, shares, first_expert, expert_count, with_grads, bits, piece, with_totals
+):
     plan_ref, refs = refs[0], refs[1:]
     if with_grads:
         past_plan, side_ref, refs = refs[0], refs[1], refs[2:]
@@ -261,6 +263,8 @@
     router_ref, up_ref, down_ref, *refs = refs
     if with_grads:
         past, refs = refs[:4], refs[4:]
+    if with_totals:
+        totals, refs = refs[: 3 * shares], refs[3 * shares :]
     y_refs, refs = refs[:shares], refs[shares:]
     back_refs, refs = refs[:shares], refs[shares:]
     gate_refs, refs = refs[:shares], refs[shares:]
@@ -281,8 +285,14 @@
 
     @pl.when(step == 0)
     def _():
-        for out in (*y_refs, *back_refs, *gates):
-            out[...] = jnp.zeros_like(out)
+        if with_totals:
+            for out, total in zip((*y_refs, *back_refs), totals):
+                out[...] = total[...]
+        else:
+            for out in (*y_refs, *back_refs):
+                out[...] = jnp.zeros_like(out)
+        for gate in gates:
+            gate[...] = jnp.zeros_like(gate)
 
     if with_grads:
         past_units = past_plan[4 * shares, expert]
@@ -348,8 +358,9 @@
 
     @pl.when(step == pl.num_programs(0) - 1)
     def _():
-        for gate, out in zip(gates, gate_refs):
-            out[...] = gate[...].T[:1]
+        for share in range(shares):
+            row = gates[share][...].T[:1]
+            gate_refs[share][...] = row + totals[2 * shares + share][...] if with_totals else row
 
     if with_grads:
         up_acc[...] = jnp.zeros_like(up_acc)
@@ -368,8 +379,8 @@
         lax.fori_loop(0, past_units, finish, 0)
         for_units(past_units, add(old))
         up_bit, down_bit = bits or (0, 0)
-        store_parts(up_outs, up_acc, side_ref[0], up_bit, piece)
-        store_parts(down_outs, down_acc, side_ref[1], down_bit, piece)
+        store_parts(up_outs, 0, up_acc, side_ref[0], up_bit, piece)
+        store_parts(down_outs, 0, down_acc, side_ref[1], down_bit, piece)
 
 
 def run_experts(plan, x, c, router, up, down, past=None, first_expert=0, step_count=None):
@@ -398,10 +409,12 @@
     ] + [pltpu.VMEM((rows, 128), full)] * shares
     widths = (width, hidden, width, hidden)
     if with_grads:
-        past_plan, past_arrays, sides, bits, piece = past
+        past_plan, past_arrays, sides, bits, piece, totals = past
         scalars += [past_plan, sides]
         inputs += past_arrays
         in_specs += [pl.BlockSpec(memory_space=pl.ANY)] * 4
+        inputs += totals
+        in_specs += [whole(array.shape) for array in totals]
         if bits:
             shape = (width // (2 * piece), piece, hidden)
             out_specs += [pl.BlockSpec((1, *shape), lambda e, *p: (e, 0, 0, 0))] * 4
@@ -429,6 +442,7 @@
             with_grads=with_grads,
             bits=bits if with_grads else None,
             piece=piece if with_grads else None,
+            with_totals=with_grads and len(totals) > 0,
         ),
         grid_spec=pltpu.PrefetchScalarGridSpec(
             num_scalar_prefetch=len(scalars),
@@ -449,14 +463,14 @@
     for target, out in ((core_ref[0], keep_ref), (1 - core_ref[0], send_ref)):
         here = pl.ds(pl.multiple_of(target * share, share), share)
         total = sum(
-            mm(grad_ref[which, :, here].T, weight_ref[which], ((1,), (1,))) for which in range(3)
+            mm(grad_ref[which, :, here].T, weight_ref[which], ((1,), (0,))) for which in range(3)
         )
         out[...] = total.astype(out.dtype)
 
 
 def input_grads(core, qkv_rows, qkv_weight):
     share = qkv_rows.shape[2] // 2
-    width = qkv_weight.shape[1]
+    width = qkv_weight.shape[2]
     vmem = pl.BlockSpec(memory_space=pltpu.VMEM)
     return pl.pallas_call(
         input_kernel,
@@ -471,48 +485,50 @@
     )(core, qkv_rows, qkv_weight)
 
 
-def projection_kernel(*refs):
-    _, _, *refs = refs
-    (rows_a, rows_b, grad_a, grad_b, out_a, out_b, mixed_a, mixed_b, weight, total, gain) = refs
+def projection_kernel(*refs, bit, piece):
+    side, *refs = refs
+    (rows_a, rows_b, grad_a, grad_b, out_a, out_b, mixed_a, mixed_b, weight, *outs) = refs
+    *outs, gain, part_ref = outs
     gain_total = jnp.zeros(gain.shape, jnp.float32)
-    for which in range(3):
-        part = mm(grad_a[which], rows_a[...], ((1,), (0,)))
-        part = part + mm(grad_b[which], rows_b[...], ((1,), (0,)))
-        total[which] = part.T.astype(jnp.bfloat16)
-        turned = weight[which].astype(jnp.float32).T
-        gain_total = gain_total + jnp.sum(turned * part, axis=0, keepdims=True)
-    part = mm(mixed_a[...], out_a[...], ((1,), (0,))) + mm(mixed_b[...], out_b[...], ((1,), (0,)))
-    total[3] = part.T.astype(jnp.bfloat16)
+    for which in range(4):
+        if which < 3:
+            part = mm(grad_a[which], rows_a[...], ((1,), (0,)))
+            part = part + mm(grad_b[which], rows_b[...], ((1,), (0,)))
+            turned = weight[which].astype(jnp.float32)
+            gain_total = gain_total + jnp.sum(turned * part, axis=0, keepdims=True)
+        else:
+            part = mm(mixed_a[...], out_a[...], ((1,), (0,)))
+            part = part + mm(mixed_b[...], out_b[...], ((1,), (0,)))
+        part_ref[...] = part.T
+        store_parts(outs, which, part_ref, side[0], bit, piece)
     gain[...] = gain_total
 
 
-def projection_grads(seqs, normed, qkv_rows, out_rows, mixed, qkv_weight):
+def projection_grads(side, normed, qkv_rows, out_rows, mixed, qkv_weight, bit, piece):
     _, size, seq_len = qkv_rows[0].shape
-    width = normed.shape[1]
-    whole = lambda array: pl.BlockSpec(array.shape, lambda i, a, b: (0,) * array.ndim)
-    operands = [normed, normed, *qkv_rows, *out_rows, *mixed, qkv_weight]
-    in_specs = [
-        pl.BlockSpec((seq_len, width), lambda i, a, b: (a[0], 0)),
-        pl.BlockSpec((seq_len, width), lambda i, a, b: (b[0], 0)),
-    ] + [whole(array) for array in operands[2:]]
+    width = normed[0].shape[1]
+    whole = lambda shape: pl.BlockSpec(shape, lambda i, *p: (0,) * len(shape))
+    operands = [*normed, *qkv_rows, *out_rows, *mixed, qkv_weight]
+    in_specs = [whole(array.shape) for array in operands]
+    if bit:
+        shapes = [(4, width // (2 * piece), piece, size)] * 2
+    else:
+        shapes = [(4, width, size)]
+    out_shape = [jax.ShapeDtypeStruct(shape, jnp.bfloat16) for shape in shapes]
+    out_shape += [jax.ShapeDtypeStruct((1, width), jnp.float32)]
     return pl.pallas_call(
-        projection_kernel,
+        functools.partial(projection_kernel, bit=bit, piece=piece),
         grid_spec=pltpu.PrefetchScalarGridSpec(
-            num_scalar_prefetch=2,
+            num_scalar_prefetch=1,
             grid=(1,),
             in_specs=in_specs,
-            out_specs=[
-                pl.BlockSpec((4, width, size), lambda i, a, b: (0, 0, 0)),
-                pl.BlockSpec((1, width), lambda i, a, b: (0, 0)),
-            ],
+            out_specs=[whole(array.shape) for array in out_shape],
+            scratch_shapes=[pltpu.VMEM((width, size), jnp.float32)],
         ),
-        out_shape=[
-            jax.ShapeDtypeStruct((4, width, size), jnp.bfloat16),
-            jax.ShapeDtypeStruct((1, width), jnp.float32),
-        ],
+        out_shape=out_shape,
         compiler_params=pltpu.CompilerParams(vmem_limit_bytes=56 * 2**20),
         name="projection_grads",
-    )(*seqs, *operands)
+    )(side, *operands)
 
 
 EPS = 1e-06
@@ -594,12 +610,9 @@
         return self.values
 
 
-def sum_everywhere(values):
-    for axis in ("tensor", "dp"):
-        bit = 1
-        while bit < lax.axis_size(axis):
-            values = values + swap(values, axis, bit)
-            bit *= 2
+def sum_along(values, steps):
+    for axis, bit in steps:
+        values = values + swap(values, axis, bit)
     return values
 
 
@@ -627,8 +640,7 @@
     seq_len = (buckets.shape[0] + 1) // 2
     heads, bucket_count = bias_table.shape
     experts = up_weight.shape[0]
-    own_seq = chip.astype(jnp.int32).reshape(1)
-    other_seq = 1 - own_seq
+    zero_seq = jnp.zeros((1,), jnp.int32)
 
     flipped = buckets[::-1]
     cut = KB - 1
@@ -641,8 +653,6 @@
     order = rank ^ jnp.arange(tensor_count)
     same = order[:, None] == jnp.arange(tensor_count)[None, :]
     counts = jnp.sum(jnp.where(same[:, :, None], counts[None], 0), axis=1)
-    own_plan = plan_segments(counts[:2])
-    other_plan = plan_segments(counts[2:])
     my_routes = lax.dynamic_slice_in_dim(routes[:, 0], rank * share, share, 0)
     my_hot = (my_routes[:, None] == jnp.arange(experts)[None, :]).astype(F32)
     earlier = (jnp.arange(share)[:, None] > jnp.arange(share)[None, :]).astype(BF16)
@@ -666,12 +676,16 @@
     grad_mine = sort_rows(cotangent)
     grad_near = swap(grad_mine, "tensor", 1)
     grad_far = Transfer(grad_mine, "tensor", 2)
-    padded_router = jnp.pad(router_weight, ((0, 0), (0, 128 - experts)))
-    early = (grad_mine, grad_near, place_matrix, own_plan, other_plan, padded_router, my_hot)
-
-    normed_one = norm_rows(after(tokens, *early).astype(F32), attn_gain).astype(BF16)
+    early = (grad_mine, grad_near, place_matrix, my_hot)
     input_share = lax.dynamic_slice_in_dim(tokens, rank * share, share, 0).astype(F32)
-    qkv = jnp.einsum("cdf,td->cft", qkv_weight, normed_one, preferred_element_type=F32).astype(BF16)
+
+    def project_rows(which, *milestones):
+        inputs = lax.dynamic_slice_in_dim(after(tokens, *milestones), which * half, half, 0)
+        normed = norm_rows(inputs.astype(F32), attn_gain).astype(BF16)
+        qkv = jnp.einsum("cdf,td->cft", qkv_weight, normed, preferred_element_type=F32)
+        return normed, qkv.astype(BF16)
+
+    normed_other, qkv_other = project_rows(1 - chip, *early)
 
     def columns(values, core_index):
         return lax.dynamic_slice_in_dim(values, core_index * share, share, values.ndim - 1)
@@ -682,15 +696,25 @@
         )
 
     mixed_other, lse_other = join(
-        forward_attention(other_seq, qkv, offsets, seq_len), grad_far
-    )
-    passed = swap(project(mixed_other, 1 - core).astype(BF16), "tensor", 1)
-    attn_sent = (project(mixed_other, core) + passed.astype(F32)).astype(BF16)
+        forward_attention(zero_seq, qkv_other, offsets, seq_len), grad_far
+    )
+    for_near = project(mixed_other, 1 - core).astype(BF16)
+    passed = swap(for_near, "tensor", 1)
+    normed_own, qkv_own = project_rows(chip, for_near)
+    kept = project(after(mixed_other, qkv_own), core)
+    attn_sent = (kept + passed.astype(F32)).astype(BF16)
     attn_far = Transfer(attn_sent, "tensor", 2)
     grad_far = grad_far.moving
     grad_both = swap(grad_far, "tensor", 1)
-    mixed_own, lse_own = join(
-        forward_attention(after(own_seq, attn_sent, grad_both), qkv, offsets, seq_len), attn_far
+    own_attention = forward_attention(
+        after(zero_seq, attn_sent, grad_both), qkv_own, offsets, seq_len
+    )
+    late_counts, late_router = after((counts, router_weight), qkv_own)
+    own_plan = plan_segments(late_counts[:2])
+    other_plan = plan_segments(late_counts[2:])
+    padded_router = jnp.pad(late_router, ((0, 0), (0, 128 - experts)))
+    (mixed_own, lse_own), own_plan, other_plan, padded_router = join(
+        (own_attention, own_plan, other_plan, padded_router), attn_far
     )
     attn_near = swap(project(mixed_own, 1 - core).astype(BF16), "tensor", 1)
     attn_share = project(mixed_own, core) + attn_near.astype(F32) + attn_far.moving.astype(F32)
@@ -716,9 +740,9 @@
     other_rows = [rows_far, swap(rows_far, "tensor", 1)]
     split = experts // 2
 
-    def run_other(plan, start, firsts):
+    def run_other(plan, start, firsts, totals):
         sides = jnp.stack([index // bit % 2 for bit in firsts]).astype(jnp.int32)
-        past = (own_plan, own[6:], sides, firsts if aligned else None, piece)
+        past = (own_plan, own[6:], sides, firsts if aligned else None, piece, totals)
         return run_experts(
             plan, other_rows, [grad_far, grad_both], padded_router, up_weight, down_weight,
             past, start, split,
@@ -726,14 +750,16 @@
 
     parts = 2 if aligned else 1
     first = run_other(
-        after(other_plan, back_near, gate_near), 0, (turned_bits[0], bits[0])
+        after(other_plan, back_near, gate_near), 0, (turned_bits[0], bits[0]), []
     )
     down_one = ScatterSum(first[6 + parts :], bits)
     up_one = ScatterSum(first[6 : 6 + parts], turned_bits)
     down_one.launch()
     up_one.launch()
     second = join(
-        run_other(after(other_plan, down_one.sent, up_one.sent), split, (bits[0], bits[0])),
+        run_other(
+            after(other_plan, down_one.sent, up_one.sent), split, (bits[0], bits[0]), []
+        ),
         down_one,
         up_one,
     )
@@ -746,8 +772,8 @@
     down_two = ScatterSum(second[6 + parts :], bits)
     up_two = ScatterSum(second[6 : 6 + parts], bits)
     down_two.launch()
-    down_one.moving, up_one.moving = after((down_one.moving, up_one.moving), back_sent)
     up_one.launch()
+    down_one.moving = after(down_one.moving, back_sent)
     down_one.launch()
     back_far = join(back_far.moving, down_two, down_one, up_one, gate_far)
     gate_sorted = own[4][0] + gate_near + gate_far.moving
@@ -787,7 +813,7 @@
     own_attn_grad = in_order(attn_grad, near_grad)
     own_mixed_grad = after(mixed_grad(own_attn_grad), up_two.sent, down_one.sent, down_two.sent)
     own_qkv_grad, own_diag = join(
-        backward_attention(own_seq, qkv, own_mixed_grad, lse_own, offsets, seq_len),
+        backward_attention(zero_seq, qkv_own, own_mixed_grad, lse_own, offsets, seq_len),
         far_grad,
         up_two,
         down_one,
@@ -808,7 +834,7 @@
         mixed_grad(other_attn_grad), out_sent, out_near, up_one.sent, down_two.sent, up_two.sent
     )
     other_qkv_grad, other_diag = join(
-        backward_attention(other_seq, qkv, other_mixed_grad, lse_other, offsets, seq_len),
+        backward_attention(zero_seq, qkv_other, other_mixed_grad, lse_other, offsets, seq_len),
         out_far,
         up_one,
         down_two,
@@ -817,46 +843,56 @@
     out_far = out_far.moving
 
     core_index = core.astype(jnp.int32).reshape(1)
+    turned_weight = qkv_weight.swapaxes(1, 2)
     up_two.launch()
-    normed, own_late = after((normed_one, own_qkv_grad), up_two.sent)
-    qkv_proj, gain_part = projection_grads(
-        (own_seq, other_seq),
-        normed,
+    normed_own, own_late = after((normed_own, own_qkv_grad), up_two.sent)
+    *qkv_proj, gain_part = projection_grads(
+        (index // bits[0] % 2).astype(jnp.int32).reshape(1),
+        (normed_own, normed_other),
         (own_late, other_qkv_grad),
         (own_attn_grad, other_attn_grad),
         (mixed_own, mixed_other),
-        qkv_weight,
-    )
-    projections = ScatterSum([qkv_proj], bits)
+        turned_weight,
+        bits[0] if aligned else 0,
+        piece,
+    )
+    projections = ScatterSum(qkv_proj, bits)
     projections.launch()
-    core_index = after(core_index, projections.sent)
-    input_keep, input_send = input_grads(core_index, other_qkv_grad, qkv_weight)
+    input_keep, input_send = input_grads(
+        after(core_index, projections.sent), other_qkv_grad, turned_weight
+    )
     input_passed = swap(input_send, "tensor", 1)
     input_sent = (input_keep + input_passed.astype(F32)).astype(BF16)
     input_far = Transfer(input_sent, "tensor", 2)
-    input_own, input_send = input_grads(after(core_index, input_sent), own_late, qkv_weight)
+    input_own, input_send = input_grads(after(core_index, input_sent), own_late, turned_weight)
     input_near = swap(input_send, "tensor", 1)
-    late = join(after(input_own, input_near), input_far, projections, up_two)
+    attn_gain_grad = gain_part[0] / attn_gain
+    table_local = jnp.dot((own_diag + other_diag)[:, 0], bucket_hot, precision=highest)
+    table_full = lax.dynamic_update_slice_in_dim(
+        jnp.zeros((heads * tensor_count, bucket_count), F32), table_local, rank * heads, 0
+    )
+    small = [attn_gain_grad, ffn_gain_grad, router_grad.reshape(-1), table_full.reshape(-1)]
+    sizes = [array.size for array in small]
+    packed = jnp.concatenate(small)
+    packed = jnp.pad(packed, (0, -packed.size % 1024)).reshape(-1, 128)
+    late, packed = join(after((input_own, packed), input_near), projections, up_two)
+    projections.launch()
+    packed = after(packed, projections.sent)
+    packed = sum_along(packed, [("tensor", 1), ("dp", bits[0])])
+    packed = join(packed, projections)
+    projections.launch()
+    late = join(after(late, projections.sent), input_far)
+    packed = after(packed, projections.sent)
     input_share_grad = late + input_near.astype(F32) + input_far.moving.astype(F32)
-    projections.launch()
     token_part = jax.vjp(lambda rows_in: norm_rows(rows_in, attn_gain), input_share)[1](
         input_share_grad
     )[0]
     tokens_grad = hidden_grad + token_part
-    attn_gain_grad = gain_part[0] / attn_gain
 
     expert_share = unsort_rows(held[0] + out_near.astype(F32) + out_far.astype(F32))
     layer_out = (hidden_share + gate_prob[:, None] * expert_share).astype(BF16)
 
-    table_local = jnp.dot((own_diag + other_diag)[:, 0], bucket_hot, precision=highest)
-    table_full = lax.dynamic_update_slice_in_dim(
-        jnp.zeros((heads * tensor_count, bucket_count), F32), table_local, rank * heads, 0
-    )
-    small = [attn_gain_grad, ffn_gain_grad, router_grad.reshape(-1), table_full.reshape(-1)]
-    sizes = [array.size for array in small]
-    packed = jnp.concatenate(small)
-    packed = jnp.pad(packed, (0, -packed.size % 1024)).reshape(-1, 128)
-    packed = sum_everywhere(after(packed, input_share_grad, projections.sent)).reshape(-1)
+    packed = sum_along(packed, [("tensor", 2)] + [("dp", bit) for bit in bits[1:]]).reshape(-1)
     ends = [sum(sizes[:i]) for i in range(5)]
     attn_gain_grad, ffn_gain_grad, router_grad, table_grad = [
         packed[ends[i] : ends[i + 1]] for i in range(4)

time: 335 us -> 314 us (0.937)
  waiting for transfers between devices: 82 us -> 67.9 us
  starting transfers between devices: 42.4 us -> 33.6 us
  local copies, waits for them, and re-layouts: 24.5 us -> 17.9 us
  Pallas kernels: 115 us -> 121 us
    ppermute x44, waiting for transfers between devices: 82 us -> 67.9 us  [swap(): return lax.ppermute(values, axis, [(i, i ^ bit) for i in range(count)])]
    ppermute x44, starting transfers between devices: 42.4 us -> 33.6 us  [swap(): return lax.ppermute(values, axis, [(i, i ^ bit) for i in range(count)])]
    pallas_call x3, Pallas kernels: 57.7 us -> 63.8 us  [run_experts(): pl.pallas_call(functools.partial(expert_kernel, shares=shares, first_expe...]
    unnamed x140 -> x152, local copies, waits for them, and re-layouts: 11.4 us -> 6.39 us
  transfers between devices with their start and end apart: 44 -> 44, of which waited for: 24 -> 24; matrix products, arithmetic and copies ran while one was open for 16% -> 19% of each run, Pallas kernels for 25% -> 29%
where the time goes in v3:
time: 314 us; the launch traced here: 310 us
  Pallas kernels  121 us (39%)
  waiting for transfers between devices  67.9 us (22%)
  other arithmetic  45 us (14%)
  starting transfers between devices  33.6 us (11%)
  matrix products  21.9 us (7%)
  local copies, waits for them, and re-layouts  17.9 us (6%)
    ppermute x44, waiting for transfers between devices, swap(): return lax.ppermute(values, axis, [(i, i ^ bit) for i in range(count)])  67.9 us
    pallas_call x3, Pallas kernels, run_experts(): pl.pallas_call(functools.partial(expert_kernel, shares=shares, first_expe...  63.8 us
    ppermute x44, starting transfers between devices, swap(): return lax.ppermute(values, axis, [(i, i ^ bit) for i in range(count)])  33.6 us
    pallas_call x2, Pallas kernels, backward_attention(): pl.pallas_call(backward_kernel, grid_spec=pltpu.PrefetchScalarGridSpec(nu...  25.3 us
    pallas_call x2, Pallas kernels, forward_attention(): pl.pallas_call(forward_kernel, grid_spec=pltpu.PrefetchScalarGridSpec(num...  21.3 us
    add x15, other arithmetic, land(): self.values = keep.astype(F32) + self.moving.astype(F32)  13.5 us
    pallas_call x1, Pallas kernels, projection_grads(): pl.pallas_call(functools.partial(projection_kernel, bit=bit, piece=piece)...  8.18 us
    unnamed x152, local copies, waits for them, and re-layouts  6.39 us
  transfers between devices with their start and end apart: 44, of which 24 were waited for; matrix products, arithmetic and copies ran while one was open for 19% of the time, Pallas kernels for 29%

profile of v3, /device:TPU:0, one launch (start us, length us, event | category | flops | bytes accessed | tf_op | source)
XLA Modules:
  0.0 309.9 jit_solution(10784065932006552111)
XLA Ops:
  6.3 2.6 collective-permute-start.1
  15.4 10.7 %attention_forward.2 = (bf16[192,1024]{1,0:T(8,128)(2,1)S(1)}, f32[3,1,1024]{2,1,0:T(1,128)S(1)}) custom-call(s32[1]{0:T(128)} %constant.311.clone.1.seq_ref, bf16[3,192,1024]{2,1,0:T(8,128)(2,1)S(1)} %convert_bitcast_fusion.1.qkv_ref, f32[3,1,2048]{2,1,0:T(1,128)S(1)} %broadcast_in_dim.42.offset_ref), custom_call_target="tpu_custom_call" | custom-call | flops 1 | bytes 1 | tf_op jit(solution)/shard_map/attention_forward/pallas_call | solution.py:53
  31.5 2.4 add_convert_fusion.5
  38.4 10.6 %attention_forward.3 = (bf16[192,1024]{1,0:T(8,128)(2,1)S(1)}, f32[3,1,1024]{2,1,0:T(1,128)S(1)}) custom-call(s32[1]{0:T(128)} %constant.311.clone.1.seq_ref, bf16[3,192,1024]{2,1,0:T(8,128)(2,1)S(1)} %convert_bitcast_fusion.qkv_ref, f32[3,1,2048]{2,1,0:T(1,128)S(1)} %copy-done.11), custom_call_target="tpu_custom_call" | custom-call | flops 1 | bytes 1 | tf_op jit(solution)/shard_map/attention_forward/pallas_call | solution.py:53
  48.9 5.2 %collective-permute-done.4 = bf16[512,768]{1,0:T(8,128)(2,1)} collective-permute-done((bf16[512,768]{1,0:T(8,128)(2,1)}, bf16[512,768]{1,0:T(8,128)(2,1)}, u32[]{:S(2)}, u32[]{:S(2)}) %collective-permute-start.4) | collective-permute-done | bytes 786464 | tf_op jit(solution)/shard_map/ppermute | solution.py:545
  63.1 22.2 %experts.1 = (f32[512,768]{1,0:T(8,128)}, bf16[512,768]{1,0:T(8,128)(2,1)}, f32[512,768]{1,0:T(8,128)}, bf16[512,768]{1,0:T(8,128)(2,1)}, f32[1,512]{1,0:T(1,128...) custom-call(s32[10,4]{1,0:T(8,128)} %copy.103.refs_0_.refs_1_, ...), custom_call_target="tpu_custom_call" | custom-call | flops 1 | bytes 1 | tf_op jit(solution)/shard_map/experts/pallas_call | solution.py:436
  89.2 22.0 %experts_and_grads.2 = (f32[512,768]{1,0:T(8,128)}, bf16[512,768]{1,0:T(8,128)(2,1)}, f32[512,768]{1,0:T(8,128)}, bf16[512,768]{1,0:T(8,128)(2,1)}, f32[1,512]{1...) custom-call(s32[10,4]{1,0:T(8,128)} %copy.104.refs_0_, ...), custom_call_target="tpu_custom_call" | custom-call | flops 1 | bytes 1 | tf_op jit(solution)/shard_map/experts_and_grads/pallas_call | solution.py:436
  113.8 19.5 %experts_and_grads.3 = (f32[512,768]{1,0:T(8,128)}, bf16[512,768]{1,0:T(8,128)(2,1)}, f32[512,768]{1,0:T(8,128)}, bf16[512,768]{1,0:T(8,128)(2,1)}, f32[1,512]{1...) custom-call(s32[10,4]{1,0:T(8,128)} %copy.106.refs_0_, ...), custom_call_target="tpu_custom_call" | custom-call | flops 1 | bytes 1 | tf_op jit(solution)/shard_map/experts_and_grads/pallas_call | solution.py:436
  133.4 6.2 %collective-permute-done.11 = bf16[2,4,96,768]{3,2,1,0:T(8,128)(2,1)} collective-permute-done((bf16[2,4,96,768]{3,2,1,0:T(8,128)(2,1)}, bf16[2,4,96,768]{3,2,1,0:T(8,128)(2,1)}, u32[]{:S(2)}, u32[]{:S(2)}) %collective-permute-start.11) | collective-permute-done | bytes 1179680 | tf_op jit(solution)/shard_map/ppermute | solution.py:545
  145.4 2.8 collective-permute-start.17
  159.8 11.2 %collective-permute-done.19 = f32[512]{0:T(512)S(1)} collective-permute-done((f32[512]{0:T(512)S(1)}, f32[512]{0:T(512)S(1)}, u32[]{:S(2)}, u32[]{:S(2)}) %collective-permute-start.19) | collective-permute-done | bytes 2080 | tf_op jit(solution)/shard_map/ppermute | solution.py:545
  171.0 4.0 %collective-permute-done.17 = bf16[2,2,96,768]{3,2,0,1:T(8,128)(2,1)S(1)} collective-permute-done((bf16[2,2,96,768]{3,2,0,1:T(8,128)(2,1)S(1)}, bf16[2,2,96,768]{3,2,0,1:T(8,128)(2,1)S(1)}, u32[]{:S(2)}, u32[]{:S(2)}) %collective-permute-start.17) | collective-permute-done | bytes 589856 | tf_op jit(solution)/shard_map/ppermute | solution.py:545
  176.4 4.9 %collective-permute-done.16 = bf16[2,2,96,768]{3,2,0,1:T(8,128)(2,1)S(1)} collective-permute-done((bf16[2,2,96,768]{3,2,0,1:T(8,128)(2,1)S(1)}, bf16[2,2,96,768]{3,2,0,1:T(8,128)(2,1)S(1)}, u32[]{:S(2)}, u32[]{:S(2)}) %collective-permute-start.16) | collective-permute-done | bytes 589856 | tf_op jit(solution)/shard_map/ppermute | solution.py:545
  196.7 12.7 %attention_backward.2 = (bf16[3,192,1024]{2,1,0:T(8,128)(2,1)S(1)}, f32[3,1,2048]{2,1,0:T(1,128)S(1)}) custom-call(s32[1]{0:T(128)} %constant.311.clone.1.seq_ref, bf16[3,192,1024]{2,1,0:T(8,128)(2,1)S(1)} %convert_bitcast_fusion.qkv_ref, bf16[192,1024]{1,0:T(8,128)(2,1)S(1)} %fusion.12.grad_ref, f32[3,1,1024]{2,1,0:T(1,128)S(1)} %get-tuple-element.221.lse_ref, ...), custom_call_target="tpu_custom_call" | custom-call | flops 1 | bytes 1 | tf_op jit(solution)/shard_map/attention_backward/pallas_call | solution.py:125
  213.2 3.6 %collective-permute-done.22 = bf16[2,4,96,768]{3,2,1,0:T(8,128)(2,1)} collective-permute-done((bf16[2,4,96,768]{3,2,1,0:T(8,128)(2,1)}, bf16[2,4,96,768]{3,2,1,0:T(8,128)(2,1)}, u32[]{:S(2)}, u32[]{:S(2)}) %collective-permute-start.22) | collective-permute-done | bytes 1179680 | tf_op jit(solution)/shard_map/ppermute | solution.py:545
  227.5 12.5 %attention_backward.3 = (bf16[3,192,1024]{2,1,0:T(8,128)(2,1)S(1)}, f32[3,1,2048]{2,1,0:T(1,128)S(1)}) custom-call(s32[1]{0:T(128)} %constant.311.clone.1.seq_ref, bf16[3,192,1024]{2,1,0:T(8,128)(2,1)S(1)} %convert_bitcast_fusion.1.qkv_ref, bf16[192,1024]{1,0:T(8,128)(2,1)S(1)} %fusion.13.grad_ref, f32[3,1,1024]{2,1,0:T(1,128)S(1)} %get-tuple-element.237.lse_ref, ...), custom_call_target="tpu_custom_call" | custom-call | flops 1 | bytes 1 | tf_op jit(solution)/shard_map/attention_backward/pallas_call | solution.py:125
  244.6 8.2 %projection_grads.1 = (bf16[4,4,96,192]{3,2,1,0:T(8,128)(2,1)}, bf16[4,4,96,192]{3,2,1,0:T(8,128)(2,1)}, f32[1,768]{1,0:T(1,128)}) custom-call(s32[1]{0:T(128)} %bitcast.15.refs_0_, bf16[1024,768]{1,0:T(8,128)(2,1)} %copy-done.27, bf16[1024,768]{1,0:T(8,128)(2,1)} %copy-done.26, bf16[3,192,1024]{2,1,0:T(8,128)(2,1)} %copy-done.3, ...), custom_call_target="tpu_custom_call" | custom-call | tf_op jit(solution)/shard_map/projection_grads/pallas_call | solution.py:519
  265.4 2.5 pad_maximum_fusion.3
  269.5 3.8 %collective-permute-done.35 = bf16[2,96,768]{2,1,0:T(8,128)(2,1)} collective-permute-done((bf16[2,96,768]{2,1,0:T(8,128)(2,1)}, bf16[2,96,768]{2,1,0:T(8,128)(2,1)}, u32[]{:S(2)}, u32[]{:S(2)}) %collective-permute-start.35) | collective-permute-done | bytes 294944 | tf_op jit(solution)/shard_map/ppermute | solution.py:545
  273.3 3.2 %collective-permute-done.34 = bf16[4,4,96,192]{3,2,1,0:T(8,128)(2,1)} collective-permute-done((bf16[4,4,96,192]{3,2,1,0:T(8,128)(2,1)}, bf16[4,4,96,192]{3,2,1,0:T(8,128)(2,1)}, u32[]{:S(2)}, u32[]{:S(2)}) %collective-permute-start.34) | collective-permute-done | bytes 589856 | tf_op jit(solution)/shard_map/ppermute | solution.py:545
  282.6 2.3 collective-permute-done.37
  284.9 4.0 %collective-permute-done.38 = bf16[4,2,96,192]{3,2,0,1:T(8,128)(2,1)S(1)} collective-permute-done((bf16[4,2,96,192]{3,2,0,1:T(8,128)(2,1)S(1)}, bf16[4,2,96,192]{3,2,0,1:T(8,128)(2,1)S(1)}, u32[]{:S(2)}, u32[]{:S(2)}) %collective-permute-start.38) | collective-permute-done | bytes 294944 | tf_op jit(solution)/shard_map/ppermute | solution.py:545
  296.2 3.9 %collective-permute-done.41 = f32[40,128]{1,0:T(8,128)S(1)} collective-permute-done((f32[40,128]{1,0:T(8,128)S(1)}, f32[40,128]{1,0:T(8,128)S(1)}, u32[]{:S(2)}, u32[]{:S(2)}) %collective-permute-start.41) | collective-permute-done | bytes 20512 | tf_op jit(solution)/shard_map/ppermute | solution.py:545
  302.4 2.5 collective-permute-done.42
  (372 shorter events, 124.0 us)
Async XLA Ops:
  6.3 20.7 %collective-permute-start.1 = (bf16[512,768]{1,0:T(8,128)(2,1)S(1)}, bf16[512,768]{1,0:T(8,128)(2,1)S(1)}, u32[]{:S(2)}, u32[]{:S(2)}) collective-permute-start(bf16[512,768]{1,0:T(8,128)(2,1)S(1)} %convolution_convert_fusion.3.refs_3_), channel_id=1, source_target_pairs={{0,2},{1,3},{2,0},{3,1},{4,6},{5,7},{6,4},{7,5},{8,10},{9,11},{10,... | collective-permute-start | bytes 2359304 | tf_op jit(solution)/shard_map/ppermute | solution.py:545
  33.9 20.2 %collective-permute-start.4 = (bf16[512,768]{1,0:T(8,128)(2,1)}, bf16[512,768]{1,0:T(8,128)(2,1)}, u32[]{:S(2)}, u32[]{:S(2)}) collective-permute-start(bf16[512,768]{1,0:T(8,128)(2,1)} %add_convert_fusion.5), channel_id=1, source_target_pairs={{0,2},{1,3},{2,0},{3,1},{4,6},{5,7},{6,4},{7,5},{8,10},{9,11},{10,... | collective-permute-start | bytes 2359304 | tf_op jit(solution)/shard_map/ppermute | solution.py:545
  60.6 24.7 %collective-permute-start.7 = (bf16[512,768]{1,0:T(8,128)(2,1)}, bf16[512,768]{1,0:T(8,128)(2,1)}, u32[]{:S(2)}, u32[]{:S(2)}) collective-permute-start(bf16[512,768]{1,0:T(8,128)(2,1)} %convolution_convert_fusion.2.refs_1_), channel_id=1, source_target_pairs={{0,2},{1,3},{2,0},{3,1},{4,6},{5,7},{6,4},{7,5},{8,10},{9,11},{10,... | collective-permute-start | bytes 2359304 | tf_op jit(solution)/shard_map/ppermute | solution.py:545
  111.2 28.4 %collective-permute-start.11 = (bf16[2,4,96,768]{3,2,1,0:T(8,128)(2,1)}, bf16[2,4,96,768]{3,2,1,0:T(8,128)(2,1)}, u32[]{:S(2)}, u32[]{:S(2)}) collective-permute-start(bf16[2,4,96,768]{3,2,1,0:T(8,128)(2,1)} %get-tuple-element.179), channel_id=1, source_target_pairs={{0,4},{4,0},{8,12},{12,8},{16,20},{20,16},{24,28},{28,24},{1,5},{5... | collective-permute-start | bytes 3538952 | tf_op jit(solution)/shard_map/ppermute | solution.py:545
  111.3 28.5 %collective-permute-start.12 = (bf16[2,4,96,768]{3,2,1,0:T(8,128)(2,1)}, bf16[2,4,96,768]{3,2,1,0:T(8,128)(2,1)}, u32[]{:S(2)}, u32[]{:S(2)}) collective-permute-start(bf16[2,4,96,768]{3,2,1,0:T(8,128)(2,1)} %get-tuple-element.180), channel_id=1, source_target_pairs={{0,8},{4,12},{8,0},{12,4},{16,24},{20,28},{24,16},{28,20},{1,9},{5... | collective-permute-start | bytes 3538952 | tf_op jit(solution)/shard_map/ppermute | solution.py:545
  145.4 29.6 %collective-permute-start.17 = (bf16[2,2,96,768]{3,2,0,1:T(8,128)(2,1)S(1)}, bf16[2,2,96,768]{3,2,0,1:T(8,128)(2,1)S(1)}, u32[]{:S(2)}, u32[]{:S(2)}) collective-permute-start(bf16[2,2,96,768]{3,2,0,1:T(8,128)(2,1)S(1)} %fusion.22), channel_id=1, source_target_pairs={{0,16},{4,20},{8,24},{12,28},{16,0},{20,4},{24,8},{28,12},{1,17},{... | collective-permute-start | bytes 1769480 | tf_op jit(solution)/shard_map/ppermute | solution.py:545
  148.3 28.1 %collective-permute-start.15 = (bf16[2,4,96,768]{3,2,1,0:T(8,128)(2,1)S(1)}, bf16[2,4,96,768]{3,2,1,0:T(8,128)(2,1)S(1)}, u32[]{:S(2)}, u32[]{:S(2)}) collective-permute-start(bf16[2,4,96,768]{3,2,1,0:T(8,128)(2,1)S(1)} %copy-done.72), channel_id=1, source_target_pairs={{0,4},{4,0},{8,12},{12,8},{16,20},{20,16},{24,28},{28,24},{1,5},{5... | collective-permute-start | bytes 3538952 | tf_op jit(solution)/shard_map/ppermute | solution.py:545
  151.5 29.8 %collective-permute-start.14 = (bf16[512,768]{1,0:T(8,128)(2,1)S(1)}, bf16[512,768]{1,0:T(8,128)(2,1)S(1)}, u32[]{:S(2)}, u32[]{:S(2)}) collective-permute-start(bf16[512,768]{1,0:T(8,128)(2,1)S(1)} %add_convert_fusion.3), channel_id=1, source_target_pairs={{0,2},{1,3},{2,0},{3,1},{4,6},{5,7},{6,4},{7,5},{8,10},{9,11},{10,... | collective-permute-start | bytes 2359304 | tf_op jit(solution)/shard_map/ppermute | solution.py:545
  154.8 26.4 %collective-permute-start.16 = (bf16[2,2,96,768]{3,2,0,1:T(8,128)(2,1)S(1)}, bf16[2,2,96,768]{3,2,0,1:T(8,128)(2,1)S(1)}, u32[]{:S(2)}, u32[]{:S(2)}) collective-permute-start(bf16[2,2,96,768]{3,2,0,1:T(8,128)(2,1)S(1)} %fusion.21), channel_id=1, source_target_pairs={{0,8},{4,12},{8,0},{12,4},{16,24},{20,28},{24,16},{28,20},{1,9},{5... | collective-permute-start | bytes 1769480 | tf_op jit(solution)/shard_map/ppermute | solution.py:545
  156.8 14.2 %collective-permute-start.19 = (f32[512]{0:T(512)S(1)}, f32[512]{0:T(512)S(1)}, u32[]{:S(2)}, u32[]{:S(2)}) collective-permute-start(f32[512]{0:T(512)S(1)} %add.427), channel_id=1, source_target_pairs={{0,2},{1,3},{2,0},{3,1},{4,6},{5,7},{6,4},{7,5},{8,10},{9,11},{10,... | collective-permute-start | bytes 6152 | tf_op jit(solution)/shard_map/ppermute | solution.py:545
  187.8 25.4 %collective-permute-start.21 = (bf16[512,768]{1,0:T(8,128)(2,1)}, bf16[512,768]{1,0:T(8,128)(2,1)}, u32[]{:S(2)}, u32[]{:S(2)}) collective-permute-start(bf16[512,768]{1,0:T(8,128)(2,1)} %fusion.68), channel_id=1, source_target_pairs={{0,2},{1,3},{2,0},{3,1},{4,6},{5,7},{6,4},{7,5},{8,10},{9,11},{10,... | collective-permute-start | bytes 2359304 | tf_op jit(solution)/shard_map/ppermute | solution.py:545
  188.4 28.4 %collective-permute-start.22 = (bf16[2,4,96,768]{3,2,1,0:T(8,128)(2,1)}, bf16[2,4,96,768]{3,2,1,0:T(8,128)(2,1)}, u32[]{:S(2)}, u32[]{:S(2)}) collective-permute-start(bf16[2,4,96,768]{3,2,1,0:T(8,128)(2,1)} %get-tuple-element.214), channel_id=1, source_target_pairs={{0,4},{4,0},{8,12},{12,8},{16,20},{20,16},{24,28},{28,24},{1,5},{5... | collective-permute-start | bytes 3538952 | tf_op jit(solution)/shard_map/ppermute | solution.py:545
  191.4 21.8 %collective-permute-start.24 = (bf16[2,2,96,768]{3,2,0,1:T(8,128)(2,1)}, bf16[2,2,96,768]{3,2,0,1:T(8,128)(2,1)}, u32[]{:S(2)}, u32[]{:S(2)}) collective-permute-start(bf16[2,2,96,768]{3,2,0,1:T(8,128)(2,1)} %fusion.23), channel_id=1, source_target_pairs={{0,8},{4,12},{8,0},{12,4},{16,24},{20,28},{24,16},{28,20},{1,9},{5... | collective-permute-start | bytes 1769480 | tf_op jit(solution)/shard_map/ppermute | solution.py:545
  192.6 18.4 %collective-permute-start.23 = (bf16[2,96,768]{2,1,0:T(8,128)(2,1)S(1)}, bf16[2,96,768]{2,1,0:T(8,128)(2,1)}, u32[]{:S(2)}, u32[]{:S(2)}) collective-permute-start(bf16[2,96,768]{2,1,0:T(8,128)(2,1)S(1)} %fusion.34), channel_id=1, source_target_pairs={{0,16},{4,20},{8,24},{12,28},{16,0},{20,4},{24,8},{28,12},{1,17},{... | collective-permute-start | bytes 884744 | tf_op jit(solution)/shard_map/ppermute | solution.py:545
  216.8 10.7 %collective-permute-start.25 = (bf16[512,768]{1,0:T(8,128)(2,1)S(1)}, bf16[512,768]{1,0:T(8,128)(2,1)S(1)}, u32[]{:S(2)}, u32[]{:S(2)}) collective-permute-start(bf16[512,768]{1,0:T(8,128)(2,1)S(1)} %copy-done.73), channel_id=1, source_target_pairs={{0,1},{1,0},{2,3},{3,2},{4,5},{5,4},{6,7},{7,6},{8,9},{9,8},{10,11... | collective-permute-start | bytes 2359304 | tf_op jit(solution)/shard_map/ppermute | solution.py:545
  219.1 22.4 %collective-permute-start.31 = (bf16[2,2,96,768]{3,2,0,1:T(8,128)(2,1)S(1)}, bf16[2,2,96,768]{3,2,0,1:T(8,128)(2,1)S(1)}, u32[]{:S(2)}, u32[]{:S(2)}) collective-permute-start(bf16[2,2,96,768]{3,2,0,1:T(8,128)(2,1)S(1)} %fusion.24), channel_id=1, source_target_pairs={{0,8},{4,12},{8,0},{12,4},{16,24},{20,28},{24,16},{28,20},{1,9},{5... | collective-permute-start | bytes 1769480 | tf_op jit(solution)/shard_map/ppermute | solution.py:545
  221.8 19.8 %collective-permute-start.30 = (bf16[2,96,768]{2,1,0:T(8,128)(2,1)S(1)}, bf16[2,96,768]{2,1,0:T(8,128)(2,1)S(1)}, u32[]{:S(2)}, u32[]{:S(2)}) collective-permute-start(bf16[2,96,768]{2,1,0:T(8,128)(2,1)S(1)} %fusion.36), channel_id=1, source_target_pairs={{0,16},{4,20},{8,24},{12,28},{16,0},{20,4},{24,8},{28,12},{1,17},{... | collective-permute-start | bytes 884744 | tf_op jit(solution)/shard_map/ppermute | solution.py:545
  223.5 19.8 %collective-permute-start.28 = (bf16[512,768]{1,0:T(8,128)(2,1)S(1)}, bf16[512,768]{1,0:T(8,128)(2,1)S(1)}, u32[]{:S(2)}, u32[]{:S(2)}) collective-permute-start(bf16[512,768]{1,0:T(8,128)(2,1)S(1)} %add_convert_fusion.2), channel_id=1, source_target_pairs={{0,2},{1,3},{2,0},{3,1},{4,6},{5,7},{6,4},{7,5},{8,10},{9,11},{10,... | collective-permute-start | bytes 2359304 | tf_op jit(solution)/shard_map/ppermute | solution.py:545
  225.2 16.4 %collective-permute-start.29 = (bf16[2,96,768]{2,1,0:T(8,128)(2,1)S(1)}, bf16[2,96,768]{2,1,0:T(8,128)(2,1)S(1)}, u32[]{:S(2)}, u32[]{:S(2)}) collective-permute-start(bf16[2,96,768]{2,1,0:T(8,128)(2,1)S(1)} %fusion.35), channel_id=1, source_target_pairs={{0,4},{4,0},{8,12},{12,8},{16,20},{20,16},{24,28},{28,24},{1,5},{5... | collective-permute-start | bytes 884744 | tf_op jit(solution)/shard_map/ppermute | solution.py:545
  256.3 20.2 %collective-permute-start.34 = (bf16[4,4,96,192]{3,2,1,0:T(8,128)(2,1)}, bf16[4,4,96,192]{3,2,1,0:T(8,128)(2,1)}, u32[]{:S(2)}, u32[]{:S(2)}) collective-permute-start(bf16[4,4,96,192]{3,2,1,0:T(8,128)(2,1)} %get-tuple-element.245), channel_id=1, source_target_pairs={{0,4},{4,0},{8,12},{12,8},{16,20},{20,16},{24,28},{28,24},{1,5},{5... | collective-permute-start | bytes 1769480 | tf_op jit(solution)/shard_map/ppermute | solution.py:545
  256.6 16.7 %collective-permute-start.35 = (bf16[2,96,768]{2,1,0:T(8,128)(2,1)}, bf16[2,96,768]{2,1,0:T(8,128)(2,1)}, u32[]{:S(2)}, u32[]{:S(2)}) collective-permute-start(bf16[2,96,768]{2,1,0:T(8,128)(2,1)} %fusion.37), channel_id=1, source_target_pairs={{0,16},{4,20},{8,24},{12,28},{16,0},{20,4},{24,8},{28,12},{1,17},{... | collective-permute-start | bytes 884744 | tf_op jit(solution)/shard_map/ppermute | solution.py:545
  268.0 24.5 %collective-permute-start.39 = (bf16[512,768]{1,0:T(8,128)(2,1)S(1)}, bf16[512,768]{1,0:T(8,128)(2,1)S(1)}, u32[]{:S(2)}, u32[]{:S(2)}) collective-permute-start(bf16[512,768]{1,0:T(8,128)(2,1)S(1)} %copy-done.51), channel_id=1, source_target_pairs={{0,2},{1,3},{2,0},{3,1},{4,6},{5,7},{6,4},{7,5},{8,10},{9,11},{10,... | collective-permute-start | bytes 2359304 | tf_op jit(solution)/shard_map/ppermute | solution.py:545
  278.0 10.9 %collective-permute-start.38 = (bf16[4,2,96,192]{3,2,0,1:T(8,128)(2,1)S(1)}, bf16[4,2,96,192]{3,2,0,1:T(8,128)(2,1)S(1)}, u32[]{:S(2)}, u32[]{:S(2)}) collective-permute-start(bf16[4,2,96,192]{3,2,0,1:T(8,128)(2,1)S(1)} %fusion.33), channel_id=1, source_target_pairs={{0,8},{4,12},{8,0},{12,4},{16,24},{20,28},{24,16},{28,20},{1,9},{5... | collective-permute-start | bytes 884744 | tf_op jit(solution)/shard_map/ppermute | solution.py:545
  289.7 17.6 %collective-permute-start.43 = (bf16[4,96,192]{2,1,0:T(8,128)(2,1)}, bf16[4,96,192]{2,1,0:T(8,128)(2,1)}, u32[]{:S(2)}, u32[]{:S(2)}) collective-permute-start(bf16[4,96,192]{2,1,0:T(8,128)(2,1)} %fusion.38), channel_id=1, source_target_pairs={{0,16},{4,20},{8,24},{12,28},{16,0},{20,4},{24,8},{28,12},{1,17},{... | collective-permute-start | bytes 442376 | tf_op jit(solution)/shard_map/ppermute | solution.py:545
  (95 other events, 488.5 us)

commit v4 on v3

--- a/solution.py
+++ b/solution.py
@@ -5,7 +5,7 @@
 from jax.experimental.pallas import tpu as pltpu
 from jax.sharding import PartitionSpec as P
 
-QB = 256
+QB = 512
 KB = 128
 
 

time: 314 us -> 312 us (level)
  Pallas kernels: 121 us -> 111 us
  starting transfers between devices: 33.6 us -> 42 us
    ppermute x44, starting transfers between devices: 33.6 us -> 42 us  [swap(): return lax.ppermute(values, axis, [(i, i ^ bit) for i in range(count)])]
    pallas_call x2, Pallas kernels: 21.3 us -> 13 us  [forward_attention(): pl.pallas_call(forward_kernel, grid_spec=pltpu.PrefetchScalarGridSpec(num...]
  transfers between devices with their start and end apart: 44 -> 44, of which waited for: 24 -> 23; matrix products, arithmetic and copies ran while one was open for 19% -> 19% of each run, Pallas kernels for 29% -> 27%
where the time goes in v4:
time: 312 us; the launch traced here: 306 us
  Pallas kernels  111 us (36%)
  waiting for transfers between devices  66.1 us (21%)
  other arithmetic  45 us (14%)
  starting transfers between devices  42 us (13%)
  matrix products  21.9 us (7%)
  local copies, waits for them, and re-layouts  17.9 us (6%)
    ppermute x44, waiting for transfers between devices, swap(): return lax.ppermute(values, axis, [(i, i ^ bit) for i in range(count)])  66.1 us
    pallas_call x3, Pallas kernels, run_experts(): pl.pallas_call(functools.partial(expert_kernel, shares=shares, first_expe...  63.8 us
    ppermute x44, starting transfers between devices, swap(): return lax.ppermute(values, axis, [(i, i ^ bit) for i in range(count)])  42 us
    pallas_call x2, Pallas kernels, backward_attention(): pl.pallas_call(backward_kernel, grid_spec=pltpu.PrefetchScalarGridSpec(nu...  23.4 us
    add x15, other arithmetic, land(): self.values = keep.astype(F32) + self.moving.astype(F32)  13.5 us
    pallas_call x2, Pallas kernels, forward_attention(): pl.pallas_call(forward_kernel, grid_spec=pltpu.PrefetchScalarGridSpec(num...  13 us
    pallas_call x1, Pallas kernels, projection_grads(): pl.pallas_call(functools.partial(projection_kernel, bit=bit, piece=piece)...  8.18 us
    unnamed x152, local copies, waits for them, and re-layouts  6.39 us
  transfers between devices with their start and end apart: 44, of which 23 were waited for; matrix products, arithmetic and copies ran while one was open for 19% of the time, Pallas kernels for 27%

profile of v4, /device:TPU:0, one launch (start us, length us, event | category | flops | bytes accessed | tf_op | source)
XLA Modules:
  0.0 306.3 jit_solution(17131520711530316675)
XLA Ops:
  6.3 2.6 collective-permute-start.1
  15.4 6.6 %attention_forward.2 = (bf16[192,1024]{1,0:T(8,128)(2,1)S(1)}, f32[3,1,1024]{2,1,0:T(1,128)S(1)}) custom-call(s32[1]{0:T(128)} %constant.311.clone.1.seq_ref, bf16[3,192,1024]{2,1,0:T(8,128)(2,1)S(1)} %convert_bitcast_fusion.1.qkv_ref, f32[3,1,2048]{2,1,0:T(1,128)S(1)} %broadcast_in_dim.42.offset_ref), custom_call_target="tpu_custom_call" | custom-call | flops 1 | bytes 1 | tf_op jit(solution)/shard_map/attention_forward/pallas_call | solution.py:53
  22.0 5.1 %collective-permute-done.1.refs_5_ = bf16[512,768]{1,0:T(8,128)(2,1)S(1)} collective-permute-done((bf16[512,768]{1,0:T(8,128)(2,1)S(1)}, bf16[512,768]{1,0:T(8,128)(2,1)S(1)}, u32[]{:S(2)}, u32[]{:S(2)}) %collective-permute-start.1) | collective-permute-done | bytes 786464 | tf_op jit(solution)/shard_map/ppermute | solution.py:545
  31.5 2.4 add_convert_fusion.5
  38.4 6.4 %attention_forward.3 = (bf16[192,1024]{1,0:T(8,128)(2,1)S(1)}, f32[3,1,1024]{2,1,0:T(1,128)S(1)}) custom-call(s32[1]{0:T(128)} %constant.311.clone.1.seq_ref, bf16[3,192,1024]{2,1,0:T(8,128)(2,1)S(1)} %convert_bitcast_fusion.qkv_ref, f32[3,1,2048]{2,1,0:T(1,128)S(1)} %copy-done.11), custom_call_target="tpu_custom_call" | custom-call | flops 1 | bytes 1 | tf_op jit(solution)/shard_map/attention_forward/pallas_call | solution.py:53
  44.8 9.4 %collective-permute-done.4 = bf16[512,768]{1,0:T(8,128)(2,1)} collective-permute-done((bf16[512,768]{1,0:T(8,128)(2,1)}, bf16[512,768]{1,0:T(8,128)(2,1)}, u32[]{:S(2)}, u32[]{:S(2)}) %collective-permute-start.4) | collective-permute-done | bytes 786464 | tf_op jit(solution)/shard_map/ppermute | solution.py:545
  63.1 22.2 %experts.1 = (f32[512,768]{1,0:T(8,128)}, bf16[512,768]{1,0:T(8,128)(2,1)}, f32[512,768]{1,0:T(8,128)}, bf16[512,768]{1,0:T(8,128)(2,1)}, f32[1,512]{1,0:T(1,128...) custom-call(s32[10,4]{1,0:T(8,128)} %copy.103.refs_0_.refs_1_, ...), custom_call_target="tpu_custom_call" | custom-call | flops 1 | bytes 1 | tf_op jit(solution)/shard_map/experts/pallas_call | solution.py:436
  89.2 18.5 %experts_and_grads.2 = (f32[512,768]{1,0:T(8,128)}, bf16[512,768]{1,0:T(8,128)(2,1)}, f32[512,768]{1,0:T(8,128)}, bf16[512,768]{1,0:T(8,128)(2,1)}, f32[1,512]{1...) custom-call(s32[10,4]{1,0:T(8,128)} %copy.104.refs_0_, ...), custom_call_target="tpu_custom_call" | custom-call | flops 1 | bytes 1 | tf_op jit(solution)/shard_map/experts_and_grads/pallas_call | solution.py:436
  112.1 23.1 %experts_and_grads.3 = (f32[512,768]{1,0:T(8,128)}, bf16[512,768]{1,0:T(8,128)(2,1)}, f32[512,768]{1,0:T(8,128)}, bf16[512,768]{1,0:T(8,128)(2,1)}, f32[1,512]{1...) custom-call(s32[10,4]{1,0:T(8,128)} %copy.106.refs_0_, ...), custom_call_target="tpu_custom_call" | custom-call | flops 1 | bytes 1 | tf_op jit(solution)/shard_map/experts_and_grads/pallas_call | solution.py:436
  137.9 2.2 add_convert_fusion.4
  157.3 10.2 %collective-permute-done.19 = f32[512]{0:T(512)S(1)} collective-permute-done((f32[512]{0:T(512)S(1)}, f32[512]{0:T(512)S(1)}, u32[]{:S(2)}, u32[]{:S(2)}) %collective-permute-start.19) | collective-permute-done | bytes 2080 | tf_op jit(solution)/shard_map/ppermute | solution.py:545
  167.5 5.5 %collective-permute-done.17 = bf16[2,2,96,768]{3,2,0,1:T(8,128)(2,1)S(1)} collective-permute-done((bf16[2,2,96,768]{3,2,0,1:T(8,128)(2,1)S(1)}, bf16[2,2,96,768]{3,2,0,1:T(8,128)(2,1)S(1)}, u32[]{:S(2)}, u32[]{:S(2)}) %collective-permute-start.17) | collective-permute-done | bytes 589856 | tf_op jit(solution)/shard_map/ppermute | solution.py:545
  173.0 5.0 %collective-permute-done.16 = bf16[2,2,96,768]{3,2,0,1:T(8,128)(2,1)S(1)} collective-permute-done((bf16[2,2,96,768]{3,2,0,1:T(8,128)(2,1)S(1)}, bf16[2,2,96,768]{3,2,0,1:T(8,128)(2,1)S(1)}, u32[]{:S(2)}, u32[]{:S(2)}) %collective-permute-start.16) | collective-permute-done | bytes 589856 | tf_op jit(solution)/shard_map/ppermute | solution.py:545
  180.8 2.3 multiply_reduce_fusion
  190.3 2.7 collective-permute-start.23
  195.4 11.8 %attention_backward.2 = (bf16[3,192,1024]{2,1,0:T(8,128)(2,1)S(1)}, f32[3,1,2048]{2,1,0:T(1,128)S(1)}) custom-call(s32[1]{0:T(128)} %constant.311.clone.1.seq_ref, bf16[3,192,1024]{2,1,0:T(8,128)(2,1)S(1)} %convert_bitcast_fusion.qkv_ref, bf16[192,1024]{1,0:T(8,128)(2,1)S(1)} %fusion.12.grad_ref, f32[3,1,1024]{2,1,0:T(1,128)S(1)} %get-tuple-element.221.lse_ref, ...), custom_call_target="tpu_custom_call" | custom-call | flops 1 | bytes 1 | tf_op jit(solution)/shard_map/attention_backward/pallas_call | solution.py:125
  211.0 2.3 collective-permute-done.22
  218.2 2.3 collective-permute-start.30
  226.5 11.6 %attention_backward.3 = (bf16[3,192,1024]{2,1,0:T(8,128)(2,1)S(1)}, f32[3,1,2048]{2,1,0:T(1,128)S(1)}) custom-call(s32[1]{0:T(128)} %constant.311.clone.1.seq_ref, bf16[3,192,1024]{2,1,0:T(8,128)(2,1)S(1)} %convert_bitcast_fusion.1.qkv_ref, bf16[192,1024]{1,0:T(8,128)(2,1)S(1)} %fusion.13.grad_ref, f32[3,1,1024]{2,1,0:T(1,128)S(1)} %get-tuple-element.237.lse_ref, ...), custom_call_target="tpu_custom_call" | custom-call | flops 1 | bytes 1 | tf_op jit(solution)/shard_map/attention_backward/pallas_call | solution.py:125
  241.5 8.2 %projection_grads.1 = (bf16[4,4,96,192]{3,2,1,0:T(8,128)(2,1)}, bf16[4,4,96,192]{3,2,1,0:T(8,128)(2,1)}, f32[1,768]{1,0:T(1,128)}) custom-call(s32[1]{0:T(128)} %bitcast.15.refs_0_, bf16[1024,768]{1,0:T(8,128)(2,1)} %copy-done.27, bf16[1024,768]{1,0:T(8,128)(2,1)} %copy-done.26, bf16[3,192,1024]{2,1,0:T(8,128)(2,1)} %copy-done.3, ...), custom_call_target="tpu_custom_call" | custom-call | tf_op jit(solution)/shard_map/projection_grads/pallas_call | solution.py:519
  263.8 2.5 pad_maximum_fusion.3
  268.2 3.4 %collective-permute-done.35 = bf16[2,96,768]{2,1,0:T(8,128)(2,1)} collective-permute-done((bf16[2,96,768]{2,1,0:T(8,128)(2,1)}, bf16[2,96,768]{2,1,0:T(8,128)(2,1)}, u32[]{:S(2)}, u32[]{:S(2)}) %collective-permute-start.35) | collective-permute-done | bytes 294944 | tf_op jit(solution)/shard_map/ppermute | solution.py:545
  280.9 4.8 %collective-permute-done.38 = bf16[4,2,96,192]{3,2,0,1:T(8,128)(2,1)S(1)} collective-permute-done((bf16[4,2,96,192]{3,2,0,1:T(8,128)(2,1)S(1)}, bf16[4,2,96,192]{3,2,0,1:T(8,128)(2,1)S(1)}, u32[]{:S(2)}, u32[]{:S(2)}) %collective-permute-start.38) | collective-permute-done | bytes 294944 | tf_op jit(solution)/shard_map/ppermute | solution.py:545
  292.7 3.9 %collective-permute-done.41 = f32[40,128]{1,0:T(8,128)S(1)} collective-permute-done((f32[40,128]{1,0:T(8,128)S(1)}, f32[40,128]{1,0:T(8,128)S(1)}, u32[]{:S(2)}, u32[]{:S(2)}) %collective-permute-start.41) | collective-permute-done | bytes 20512 | tf_op jit(solution)/shard_map/ppermute | solution.py:545
  (372 shorter events, 129.3 us)
Async XLA Ops:
  6.3 20.7 %collective-permute-start.1 = (bf16[512,768]{1,0:T(8,128)(2,1)S(1)}, bf16[512,768]{1,0:T(8,128)(2,1)S(1)}, u32[]{:S(2)}, u32[]{:S(2)}) collective-permute-start(bf16[512,768]{1,0:T(8,128)(2,1)S(1)} %convolution_convert_fusion.3.refs_3_), channel_id=1, source_target_pairs={{0,2},{1,3},{2,0},{3,1},{4,6},{5,7},{6,4},{7,5},{8,10},{9,11},{10,... | collective-permute-start | bytes 2359304 | tf_op jit(solution)/shard_map/ppermute | solution.py:545
  33.9 20.2 %collective-permute-start.4 = (bf16[512,768]{1,0:T(8,128)(2,1)}, bf16[512,768]{1,0:T(8,128)(2,1)}, u32[]{:S(2)}, u32[]{:S(2)}) collective-permute-start(bf16[512,768]{1,0:T(8,128)(2,1)} %add_convert_fusion.5), channel_id=1, source_target_pairs={{0,2},{1,3},{2,0},{3,1},{4,6},{5,7},{6,4},{7,5},{8,10},{9,11},{10,... | collective-permute-start | bytes 2359304 | tf_op jit(solution)/shard_map/ppermute | solution.py:545
  60.6 24.7 %collective-permute-start.7 = (bf16[512,768]{1,0:T(8,128)(2,1)}, bf16[512,768]{1,0:T(8,128)(2,1)}, u32[]{:S(2)}, u32[]{:S(2)}) collective-permute-start(bf16[512,768]{1,0:T(8,128)(2,1)} %convolution_convert_fusion.2.refs_1_), channel_id=1, source_target_pairs={{0,2},{1,3},{2,0},{3,1},{4,6},{5,7},{6,4},{7,5},{8,10},{9,11},{10,... | collective-permute-start | bytes 2359304 | tf_op jit(solution)/shard_map/ppermute | solution.py:545
  107.6 28.8 %collective-permute-start.11 = (bf16[2,4,96,768]{3,2,1,0:T(8,128)(2,1)}, bf16[2,4,96,768]{3,2,1,0:T(8,128)(2,1)}, u32[]{:S(2)}, u32[]{:S(2)}) collective-permute-start(bf16[2,4,96,768]{3,2,1,0:T(8,128)(2,1)} %get-tuple-element.179), channel_id=1, source_target_pairs={{0,4},{4,0},{8,12},{12,8},{16,20},{20,16},{24,28},{28,24},{1,5},{5... | collective-permute-start | bytes 3538952 | tf_op jit(solution)/shard_map/ppermute | solution.py:545
  109.8 28.1 %collective-permute-start.12 = (bf16[2,4,96,768]{3,2,1,0:T(8,128)(2,1)}, bf16[2,4,96,768]{3,2,1,0:T(8,128)(2,1)}, u32[]{:S(2)}, u32[]{:S(2)}) collective-permute-start(bf16[2,4,96,768]{3,2,1,0:T(8,128)(2,1)} %get-tuple-element.180), channel_id=1, source_target_pairs={{0,8},{4,12},{8,0},{12,4},{16,24},{20,28},{24,16},{28,20},{1,9},{5... | collective-permute-start | bytes 3538952 | tf_op jit(solution)/shard_map/ppermute | solution.py:545
  143.6 29.4 %collective-permute-start.17 = (bf16[2,2,96,768]{3,2,0,1:T(8,128)(2,1)S(1)}, bf16[2,2,96,768]{3,2,0,1:T(8,128)(2,1)S(1)}, u32[]{:S(2)}, u32[]{:S(2)}) collective-permute-start(bf16[2,2,96,768]{3,2,0,1:T(8,128)(2,1)S(1)} %fusion.22), channel_id=1, source_target_pairs={{0,16},{4,20},{8,24},{12,28},{16,0},{20,4},{24,8},{28,12},{1,17},{... | collective-permute-start | bytes 1769480 | tf_op jit(solution)/shard_map/ppermute | solution.py:545
  144.8 28.2 %collective-permute-start.15 = (bf16[2,4,96,768]{3,2,1,0:T(8,128)(2,1)S(1)}, bf16[2,4,96,768]{3,2,1,0:T(8,128)(2,1)S(1)}, u32[]{:S(2)}, u32[]{:S(2)}) collective-permute-start(bf16[2,4,96,768]{3,2,1,0:T(8,128)(2,1)S(1)} %copy-done.72), channel_id=1, source_target_pairs={{0,4},{4,0},{8,12},{12,8},{16,20},{20,16},{24,28},{28,24},{1,5},{5... | collective-permute-start | bytes 3538952 | tf_op jit(solution)/shard_map/ppermute | solution.py:545
  148.0 30.0 %collective-permute-start.14 = (bf16[512,768]{1,0:T(8,128)(2,1)S(1)}, bf16[512,768]{1,0:T(8,128)(2,1)S(1)}, u32[]{:S(2)}, u32[]{:S(2)}) collective-permute-start(bf16[512,768]{1,0:T(8,128)(2,1)S(1)} %add_convert_fusion.3), channel_id=1, source_target_pairs={{0,2},{1,3},{2,0},{3,1},{4,6},{5,7},{6,4},{7,5},{8,10},{9,11},{10,... | collective-permute-start | bytes 2359304 | tf_op jit(solution)/shard_map/ppermute | solution.py:545
  151.5 26.5 %collective-permute-start.16 = (bf16[2,2,96,768]{3,2,0,1:T(8,128)(2,1)S(1)}, bf16[2,2,96,768]{3,2,0,1:T(8,128)(2,1)S(1)}, u32[]{:S(2)}, u32[]{:S(2)}) collective-permute-start(bf16[2,2,96,768]{3,2,0,1:T(8,128)(2,1)S(1)} %fusion.21), channel_id=1, source_target_pairs={{0,8},{4,12},{8,0},{12,4},{16,24},{20,28},{24,16},{28,20},{1,9},{5... | collective-permute-start | bytes 1769480 | tf_op jit(solution)/shard_map/ppermute | solution.py:545
  154.3 13.2 %collective-permute-start.19 = (f32[512]{0:T(512)S(1)}, f32[512]{0:T(512)S(1)}, u32[]{:S(2)}, u32[]{:S(2)}) collective-permute-start(f32[512]{0:T(512)S(1)} %add.427), channel_id=1, source_target_pairs={{0,2},{1,3},{2,0},{3,1},{4,6},{5,7},{6,4},{7,5},{8,10},{9,11},{10,... | collective-permute-start | bytes 6152 | tf_op jit(solution)/shard_map/ppermute | solution.py:545
  184.5 26.4 %collective-permute-start.21 = (bf16[512,768]{1,0:T(8,128)(2,1)}, bf16[512,768]{1,0:T(8,128)(2,1)}, u32[]{:S(2)}, u32[]{:S(2)}) collective-permute-start(bf16[512,768]{1,0:T(8,128)(2,1)} %fusion.68), channel_id=1, source_target_pairs={{0,2},{1,3},{2,0},{3,1},{4,6},{5,7},{6,4},{7,5},{8,10},{9,11},{10,... | collective-permute-start | bytes 2359304 | tf_op jit(solution)/shard_map/ppermute | solution.py:545
  184.8 28.4 %collective-permute-start.22 = (bf16[2,4,96,768]{3,2,1,0:T(8,128)(2,1)}, bf16[2,4,96,768]{3,2,1,0:T(8,128)(2,1)}, u32[]{:S(2)}, u32[]{:S(2)}) collective-permute-start(bf16[2,4,96,768]{3,2,1,0:T(8,128)(2,1)} %get-tuple-element.214), channel_id=1, source_target_pairs={{0,4},{4,0},{8,12},{12,8},{16,20},{20,16},{24,28},{28,24},{1,5},{5... | collective-permute-start | bytes 3538952 | tf_op jit(solution)/shard_map/ppermute | solution.py:545
  189.1 21.8 %collective-permute-start.24 = (bf16[2,2,96,768]{3,2,0,1:T(8,128)(2,1)}, bf16[2,2,96,768]{3,2,0,1:T(8,128)(2,1)}, u32[]{:S(2)}, u32[]{:S(2)}) collective-permute-start(bf16[2,2,96,768]{3,2,0,1:T(8,128)(2,1)} %fusion.23), channel_id=1, source_target_pairs={{0,8},{4,12},{8,0},{12,4},{16,24},{20,28},{24,16},{28,20},{1,9},{5... | collective-permute-start | bytes 1769480 | tf_op jit(solution)/shard_map/ppermute | solution.py:545
  190.3 18.5 %collective-permute-start.23 = (bf16[2,96,768]{2,1,0:T(8,128)(2,1)S(1)}, bf16[2,96,768]{2,1,0:T(8,128)(2,1)}, u32[]{:S(2)}, u32[]{:S(2)}) collective-permute-start(bf16[2,96,768]{2,1,0:T(8,128)(2,1)S(1)} %fusion.34), channel_id=1, source_target_pairs={{0,16},{4,20},{8,24},{12,28},{16,0},{20,4},{24,8},{28,12},{1,17},{... | collective-permute-start | bytes 884744 | tf_op jit(solution)/shard_map/ppermute | solution.py:545
  213.2 13.2 %collective-permute-start.25 = (bf16[512,768]{1,0:T(8,128)(2,1)S(1)}, bf16[512,768]{1,0:T(8,128)(2,1)S(1)}, u32[]{:S(2)}, u32[]{:S(2)}) collective-permute-start(bf16[512,768]{1,0:T(8,128)(2,1)S(1)} %copy-done.73), channel_id=1, source_target_pairs={{0,1},{1,0},{2,3},{3,2},{4,5},{5,4},{6,7},{7,6},{8,9},{9,8},{10,11... | collective-permute-start | bytes 2359304 | tf_op jit(solution)/shard_map/ppermute | solution.py:545
  215.6 24.0 %collective-permute-start.31 = (bf16[2,2,96,768]{3,2,0,1:T(8,128)(2,1)S(1)}, bf16[2,2,96,768]{3,2,0,1:T(8,128)(2,1)S(1)}, u32[]{:S(2)}, u32[]{:S(2)}) collective-permute-start(bf16[2,2,96,768]{3,2,0,1:T(8,128)(2,1)S(1)} %fusion.24), channel_id=1, source_target_pairs={{0,8},{4,12},{8,0},{12,4},{16,24},{20,28},{24,16},{28,20},{1,9},{5... | collective-permute-start | bytes 1769480 | tf_op jit(solution)/shard_map/ppermute | solution.py:545
  218.2 21.4 %collective-permute-start.30 = (bf16[2,96,768]{2,1,0:T(8,128)(2,1)S(1)}, bf16[2,96,768]{2,1,0:T(8,128)(2,1)S(1)}, u32[]{:S(2)}, u32[]{:S(2)}) collective-permute-start(bf16[2,96,768]{2,1,0:T(8,128)(2,1)S(1)} %fusion.36), channel_id=1, source_target_pairs={{0,16},{4,20},{8,24},{12,28},{16,0},{20,4},{24,8},{28,12},{1,17},{... | collective-permute-start | bytes 884744 | tf_op jit(solution)/shard_map/ppermute | solution.py:545
  220.9 19.4 %collective-permute-start.28 = (bf16[512,768]{1,0:T(8,128)(2,1)S(1)}, bf16[512,768]{1,0:T(8,128)(2,1)S(1)}, u32[]{:S(2)}, u32[]{:S(2)}) collective-permute-start(bf16[512,768]{1,0:T(8,128)(2,1)S(1)} %add_convert_fusion.2), channel_id=1, source_target_pairs={{0,2},{1,3},{2,0},{3,1},{4,6},{5,7},{6,4},{7,5},{8,10},{9,11},{10,... | collective-permute-start | bytes 2359304 | tf_op jit(solution)/shard_map/ppermute | solution.py:545
  222.7 16.9 %collective-permute-start.29 = (bf16[2,96,768]{2,1,0:T(8,128)(2,1)S(1)}, bf16[2,96,768]{2,1,0:T(8,128)(2,1)S(1)}, u32[]{:S(2)}, u32[]{:S(2)}) collective-permute-start(bf16[2,96,768]{2,1,0:T(8,128)(2,1)S(1)} %fusion.35), channel_id=1, source_target_pairs={{0,4},{4,0},{8,12},{12,8},{16,20},{20,16},{24,28},{28,24},{1,5},{5... | collective-permute-start | bytes 884744 | tf_op jit(solution)/shard_map/ppermute | solution.py:545
  253.2 20.2 %collective-permute-start.34 = (bf16[4,4,96,192]{3,2,1,0:T(8,128)(2,1)}, bf16[4,4,96,192]{3,2,1,0:T(8,128)(2,1)}, u32[]{:S(2)}, u32[]{:S(2)}) collective-permute-start(bf16[4,4,96,192]{3,2,1,0:T(8,128)(2,1)} %get-tuple-element.245), channel_id=1, source_target_pairs={{0,4},{4,0},{8,12},{12,8},{16,20},{20,16},{24,28},{28,24},{1,5},{5... | collective-permute-start | bytes 1769480 | tf_op jit(solution)/shard_map/ppermute | solution.py:545
  255.0 16.7 %collective-permute-start.35 = (bf16[2,96,768]{2,1,0:T(8,128)(2,1)}, bf16[2,96,768]{2,1,0:T(8,128)(2,1)}, u32[]{:S(2)}, u32[]{:S(2)}) collective-permute-start(bf16[2,96,768]{2,1,0:T(8,128)(2,1)} %fusion.37), channel_id=1, source_target_pairs={{0,16},{4,20},{8,24},{12,28},{16,0},{20,4},{24,8},{28,12},{1,17},{... | collective-permute-start | bytes 884744 | tf_op jit(solution)/shard_map/ppermute | solution.py:545
  266.4 23.4 %collective-permute-start.39 = (bf16[512,768]{1,0:T(8,128)(2,1)S(1)}, bf16[512,768]{1,0:T(8,128)(2,1)S(1)}, u32[]{:S(2)}, u32[]{:S(2)}) collective-permute-start(bf16[512,768]{1,0:T(8,128)(2,1)S(1)} %copy-done.51), channel_id=1, source_target_pairs={{0,2},{1,3},{2,0},{3,1},{4,6},{5,7},{6,4},{7,5},{8,10},{9,11},{10,... | collective-permute-start | bytes 2359304 | tf_op jit(solution)/shard_map/ppermute | solution.py:545
  274.9 10.8 %collective-permute-start.38 = (bf16[4,2,96,192]{3,2,0,1:T(8,128)(2,1)S(1)}, bf16[4,2,96,192]{3,2,0,1:T(8,128)(2,1)S(1)}, u32[]{:S(2)}, u32[]{:S(2)}) collective-permute-start(bf16[4,2,96,192]{3,2,0,1:T(8,128)(2,1)S(1)} %fusion.33), channel_id=1, source_target_pairs={{0,8},{4,12},{8,0},{12,4},{16,24},{20,28},{24,16},{28,20},{1,9},{5... | collective-permute-start | bytes 884744 | tf_op jit(solution)/shard_map/ppermute | solution.py:545
  286.5 17.2 %collective-permute-start.43 = (bf16[4,96,192]{2,1,0:T(8,128)(2,1)}, bf16[4,96,192]{2,1,0:T(8,128)(2,1)}, u32[]{:S(2)}, u32[]{:S(2)}) collective-permute-start(bf16[4,96,192]{2,1,0:T(8,128)(2,1)} %fusion.38), channel_id=1, source_target_pairs={{0,16},{4,20},{8,24},{12,28},{16,0},{20,4},{24,8},{28,12},{1,17},{... | collective-permute-start | bytes 442376 | tf_op jit(solution)/shard_map/ppermute | solution.py:545
  (95 other events, 498.8 us)
